TPU v7x, 256 devices: a whole 4x4x8 slice. The times are simulated.
256 devices in a mesh: batch: 32 (over y_hi, z, core), chan: 8 (over x, y_lo).
Axes of the slice: x: 4, y: 4 (y_hi: 2, y_lo: 2; y = y_hi * 2 + y_lo), z: 8, core: 2. Of those that a mesh axis runs over, the one named last changes fastest.
Arguments:
- token_ids: int32 [4, 128], P(None, 'batch'), may hold values from 0 to 65535
- embed_table: bfloat16 [65536, 8192], P('batch', 'chan'), may hold values from -3 to 3
- norm_gain: float32 [8192], replicated, may hold values from 0.1 to 1.9
- in_weight: bfloat16 [8192, 2, 16384], P('batch', None, 'chan'), may hold values from -0.0625 to 0.0625
- filter_weight: float32 [4, 16384], P(None, 'chan'), may hold values from -3 to 3
- filter_bias: float32 [16384], P('chan'), may hold values from -3 to 3
- select_weight: bfloat16 [16384, 544], P('chan'), may hold values from -0.046875 to 0.046875
- step_gain: float32 [512], replicated, may hold values from 0.1 to 1.9
- step_weight: bfloat16 [512, 16384], P('batch', 'chan'), may hold values from -0.25 to 0.25
- step_bias: float32 [16384], P('chan'), may hold values from -4 to -1
- decay_log: float32 [16, 16384], P(None, 'chan'), may hold values from 0 to 2.77
- skip_gain: float32 [16384], P('chan'), may hold values from 0.5 to 1.5
- out_weight: bfloat16 [16384, 8192], P('chan', 'batch'), may hold values from -0.0234375 to 0.0234375
- filter_state: float32 [128, 3, 16384], P('batch', None, 'chan'), may hold values from -3 to 3
- scan_state: float32 [128, 16, 16384], P('batch', None, 'chan'), may hold values from -3 to 3
Outputs:
- hidden: bfloat16 [4, 128, 8192], P(None, 'batch')
- filter_out: float32 [128, 3, 16384], P('batch', None, 'chan')
- scan_out: float32 [128, 16, 16384], P('batch', None, 'chan')
All inputs are finite; a program needn't handle non-finite values.
Results may differ from a plain program's by a relative error of at most 0.0072.
Values may be sent and summed in bfloat16 or wider, within the bound.
No kernel may reach another device: no remote copies, remote signals or barrier semaphores. Data moves between devices by JAX's collectives and lax.ppermute only.
A program may use at most 128 MiB of HBM per device.

v0:
```python
import jax
import jax.numpy as jnp
from jax import lax
from jax.sharding import PartitionSpec as P


def rms_scale(values, gain):
    mean_square = jnp.mean(values * values, axis=-1, keepdims=True)
    return values * lax.rsqrt(mean_square + 1e-06) * gain


def input_sums(normed_rows, in_flat):
    spread = lax.all_to_all(normed_rows, "batch", split_axis=1, concat_axis=0, tiled=True)
    return lax.psum_scatter(
        jnp.dot(spread, in_flat, preferred_element_type=jnp.float32),
        "batch",
        scatter_dimension=0,
        tiled=True,
    ).astype(jnp.bfloat16)


def output_rows(gated_rows, out_weight):
    partial_out = jnp.dot(
        lax.all_gather(gated_rows, "batch", axis=0, tiled=True),
        out_weight,
        preferred_element_type=jnp.float32,
    )
    mixed_cols = lax.psum(partial_out, "chan").astype(jnp.bfloat16)
    return lax.all_to_all(mixed_cols, "batch", split_axis=0, concat_axis=1, tiled=True)


def local(
    token_ids,
    embed_table,
    norm_gain,
    in_weight,
    filter_weight,
    filter_bias,
    select_weight,
    step_gain,
    step_weight,
    step_bias,
    decay_log,
    skip_gain,
    out_weight,
    filter_state,
    scan_state,
):
    step_count = token_ids.shape[0]
    vocab_rows = embed_table.shape[0]
    channels = filter_weight.shape[1]
    rank_size = step_gain.shape[0]
    state_size = decay_log.shape[0]
    feature_rows = in_weight.shape[0]
    every_ids = lax.all_gather(token_ids, "batch", axis=1, tiled=True)
    first_row = lax.axis_index("batch") * vocab_rows
    vocab_index = first_row + lax.broadcasted_iota(jnp.int32, (1, 1, vocab_rows), 2)
    lookup = (every_ids[:, :, None] == vocab_index).astype(jnp.bfloat16)
    picked = jnp.einsum("srv,vd->srd", lookup, embed_table, preferred_element_type=jnp.float32)
    summed = lax.psum_scatter(picked.astype(jnp.bfloat16), "batch", scatter_dimension=1, tiled=True)
    embedded_all = lax.all_gather(summed, "chan", axis=2, tiled=True)
    embed_wide_all = embedded_all.astype(jnp.float32)
    in_flat = in_weight.reshape(feature_rows, 2 * channels)
    decay_rate = -jnp.exp(decay_log)
    filter_now = filter_state
    scan_now = scan_state
    results = []
    for step in range(step_count):
        embed_wide = embed_wide_all[step]
        normed = rms_scale(embed_wide, norm_gain).astype(jnp.bfloat16)
        both = input_sums(normed, in_flat)
        stream = both[:, :channels]
        gate = both[:, channels:]
        window = jnp.concatenate([filter_now, stream.astype(jnp.float32)[:, None, :]], axis=1)
        convolved = jax.nn.silu(jnp.sum(window * filter_weight[None], axis=1) + filter_bias)
        filter_now = window[:, 1:, :]
        convolved_low = convolved.astype(jnp.bfloat16)
        selected = lax.psum(
            jnp.dot(convolved_low, select_weight, preferred_element_type=jnp.float32), "chan"
        )
        rank = selected[:, :rank_size]
        bvec = selected[:, rank_size : rank_size + state_size]
        cvec = selected[:, rank_size + state_size :]
        rank_normed = rms_scale(rank, step_gain).astype(jnp.bfloat16)
        delta_raw = jnp.dot(
            rank_normed,
            lax.all_gather(step_weight, "batch", axis=0, tiled=True),
            preferred_element_type=jnp.float32,
        )
        delta = jax.nn.softplus(delta_raw + step_bias)
        factor = jnp.exp(delta[:, None, :] * decay_rate[None])
        scan_now = factor * scan_now + (delta * convolved)[:, None, :] * bvec[:, :, None]
        readout = jnp.sum(scan_now * cvec[:, :, None], axis=1) + skip_gain * convolved
        gated = (readout * jax.nn.silu(gate.astype(jnp.float32))).astype(jnp.bfloat16)
        mixed = output_rows(gated, out_weight)
        results.append((embed_wide + mixed.astype(jnp.float32)).astype(jnp.bfloat16))
    hidden = jnp.stack(results)
    return (hidden, filter_now, scan_now)


def solution(mesh):
    return jax.shard_map(
        local,
        mesh=mesh,
        in_specs=(
            P(None, "batch"),
            P("batch", "chan"),
            P(),
            P("batch", None, "chan"),
            P(None, "chan"),
            P("chan"),
            P("chan", None),
            P(),
            P("batch", "chan"),
            P("chan"),
            P(None, "chan"),
            P("chan"),
            P("chan", "batch"),
            P("batch", None, "chan"),
            P("batch", None, "chan"),
        ),
        out_specs=(P(None, "batch", None), P("batch", None, "chan"), P("batch", None, "chan")),
        check_vma=False,
    )
```

profile of v0, /device:TPU:8, one launch (start us, length us, event | category | flops | bytes accessed | tf_op | source)
XLA Modules:
  0.0 909.5 jit_solution(17372833027860551026)
XLA Ops:
  8.1 44.1 %all-gather = s32[32,4,4]{2,1,0:T(4,128)S(1)} all-gather(s32[1,4,4]{2,1,0:T(4,128)S(1)} %bitcast.105), channel_id=1, replica_groups=mesh['batch'=32,'chan'=8] {'batch'}, dimensions={0}, use_global_device_ids=true | all-gather | bytes 2112 | tf_op jit(solution)/shard_map/all_gather | solution.py:55
  52.3 5.6 fusion.5
  59.2 261.0 %all-reduce.12.cloned.1.call-done = bf16[4,128,1024]{2,1,0:T(8,128)(2,1)} async-done(((bf16[4,128,1024]{2,1,0:T(8,128)(2,1)}), bf16[4,128,1024]{2,1,0:T(8,128)(2,1)}) %all-reduce.12.cloned.1.call-update) | async-done | bytes 1048592
  321.1 28.6 %all_gather.25 = bf16[4,4,8192]{2,1,0:T(4,128)(2,1)S(1)} all-gather(bf16[4,4,1024]{2,1,0:T(4,128)(2,1)S(1)} %constant_dynamic-slice_fusion), channel_id=1, replica_groups=mesh['batch'=32,'chan'=8] {'chan'}, dimensions={2}, use_global_device_ids=true | all-gather | bytes 294912 | tf_op jit(solution)/shard_map/all_gather | solution.py:61
  356.3 9.8 %all-to-all-done = bf16[4,32,256]{2,0,1:T(4,128)(2,1)S(1)} async-done(((bf16[4,32,256]{2,0,1:T(4,128)(2,1)}), bf16[4,32,256]{2,0,1:T(4,128)(2,1)S(1)}, u32[]{:S(2)}, u32[]{:S(2)}) %all-to-all-start) | async-done | bytes 65568 | tf_op jit(solution)/shard_map/all_to_all | solution.py:13
  366.1 3.9 all-to-all-start.2
  373.9 6.7 all-to-all-done.2
  389.8 5.0 all-to-all-done.4
  394.8 4.9 all-to-all-start.6
  403.1 7.1 all-to-all-done.6
  413.6 160.5 %all-reduce.13 = (bf16[128,4096]{1,0:T(8,128)(2,1)}, bf16[128,4096]{1,0:T(8,128)(2,1)}, bf16[128,4096]{1,0:T(8,128)(2,1)}, bf16[128,4096]{1,0:T(8,128)(2,1)}) all-reduce(f32[128,4096]{1,0:T(8,128)} %fusion.77, f32[128,4096]{1,0:T(8,128)} %fusion.71, f32[128,4096]{1,0:T(8,128)} %fusion.73, ...), channel_id=6, replica_groups=mesh['batch'=32,'chan'=8] {'batch'}, use_global_device_ids=true, to_apply=%region_23.24.clone | all-reduce | flops 2097152 | bytes 12582912
  579.2 30.7 %all-reduce.7 = (f32[4,544]{1,0:T(4,128)S(1)}, f32[4,544]{1,0:T(4,128)S(1)}, f32[4,544]{1,0:T(4,128)S(1)}, f32[4,544]{1,0:T(4,128)S(1)}) all-reduce(f32[4,544]{1,0:T(4,128)S(1)} %fusion.42, f32[4,544]{1,0:T(4,128)S(1)} %fusion.44, f32[4,544]{1,0:T(4,128)S(1)} %fusion.46, ...), channel_id=1, replica_groups=mesh['batch'=32,'chan'=8] {'chan'}, use_global_device_ids=true, to_apply=%region_25.26 | all-reduce | flops 8704 | bytes 69632 | tf_op jit(solution)/shard_map/psum | solution.py:78
  619.8 40.6 %all-gather.1 = bf16[32,4,2048]{2,1,0:T(4,128)(2,1)} all-gather(bf16[1,4,2048]{2,1,0:T(4,128)(2,1)S(1)} %get-tuple-element.42), channel_id=1, replica_groups=mesh['batch'=32,'chan'=8] {'batch'}, dimensions={0}, use_global_device_ids=true | all-gather | bytes 540672 | tf_op jit(solution)/shard_map/all_gather | solution.py:24
  663.8 42.4 %all-gather.2 = bf16[32,4,2048]{2,1,0:T(4,128)(2,1)} all-gather(bf16[1,4,2048]{2,1,0:T(4,128)(2,1)S(1)} %copy-done.26), channel_id=1, replica_groups=mesh['batch'=32,'chan'=8] {'batch'}, dimensions={0}, use_global_device_ids=true | all-gather | bytes 540672 | tf_op jit(solution)/shard_map/all_gather | solution.py:24
  710.2 40.8 %all-gather.3 = bf16[32,4,2048]{2,1,0:T(4,128)(2,1)} all-gather(bf16[1,4,2048]{2,1,0:T(4,128)(2,1)S(1)} %copy-done.25), channel_id=1, replica_groups=mesh['batch'=32,'chan'=8] {'batch'}, dimensions={0}, use_global_device_ids=true | all-gather | bytes 540672 | tf_op jit(solution)/shard_map/all_gather | solution.py:24
  754.9 42.1 %all-gather.4 = bf16[32,4,2048]{2,1,0:T(4,128)(2,1)} all-gather(bf16[1,4,2048]{2,1,0:T(4,128)(2,1)S(1)} %copy-done.24), channel_id=1, replica_groups=mesh['batch'=32,'chan'=8] {'batch'}, dimensions={0}, use_global_device_ids=true | all-gather | bytes 540672 | tf_op jit(solution)/shard_map/all_gather | solution.py:24
  801.0 42.1 %all-reduce.14 = (bf16[128,256]{1,0:T(8,128)(2,1)S(1)}, bf16[128,256]{1,0:T(8,128)(2,1)S(1)}, bf16[128,256]{1,0:T(8,128)(2,1)S(1)}, bf16[128,256]{1,0:T(8,128)(2,1)S(1)}) all-reduce(f32[128,256]{1,0:T(8,128)} %fusion.78, f32[128,256]{1,0:T(8,128)} %fusion.76, f32[128,256]{1,0:T(8,128)} %fusion.74, ...), channel_id=1, replica_groups=mesh['batch'=32,'chan'=8] {'chan'}, use_global_device_ids=true, to_apply=%region_28.29 | all-reduce | flops 131072 | bytes 786432 | tf_op jit(solution)/shard_map/psum | solution.py:28
  843.8 3.9 all-to-all-start.1
  848.3 9.9 %all-to-all-done.1 = bf16[32,4,256]{2,1,0:T(4,128)(2,1)S(1)} async-done(((bf16[32,4,256]{2,1,0:T(4,128)(2,1)}), bf16[32,4,256]{2,1,0:T(4,128)(2,1)S(1)}, u32[]{:S(2)}, u32[]{:S(2)}) %all-to-all-start.1) | async-done | bytes 65568 | tf_op jit(solution)/shard_map/all_to_all | solution.py:29
  858.2 3.9 all-to-all-start.3
  862.7 9.9 %all-to-all-done.3 = bf16[32,4,256]{2,1,0:T(4,128)(2,1)S(1)} async-done(((bf16[32,4,256]{2,1,0:T(4,128)(2,1)}), bf16[32,4,256]{2,1,0:T(4,128)(2,1)S(1)}, u32[]{:S(2)}, u32[]{:S(2)}) %all-to-all-start.3) | async-done | bytes 65568 | tf_op jit(solution)/shard_map/all_to_all | solution.py:29
  877.2 9.9 %all-to-all-done.5 = bf16[32,4,256]{2,1,0:T(4,128)(2,1)S(1)} async-done(((bf16[32,4,256]{2,1,0:T(4,128)(2,1)}), bf16[32,4,256]{2,1,0:T(4,128)(2,1)S(1)}, u32[]{:S(2)}, u32[]{:S(2)}) %all-to-all-start.5) | async-done | bytes 65568 | tf_op jit(solution)/shard_map/all_to_all | solution.py:29
  887.1 3.9 all-to-all-start.7
  891.7 9.8 %all-to-all-done.7 = bf16[32,4,256]{2,1,0:T(4,128)(2,1)S(1)} async-done(((bf16[32,4,256]{2,1,0:T(4,128)(2,1)}), bf16[32,4,256]{2,1,0:T(4,128)(2,1)S(1)}, u32[]{:S(2)}, u32[]{:S(2)}) %all-to-all-start.7) | async-done | bytes 65568 | tf_op jit(solution)/shard_map/all_to_all | solution.py:29
  (159 shorter events, 67.0 us)
Async XLA Ops:
  7.2 569.2 %copy-start = (bf16[2048,544]{0,1:T(8,128)(2,1)S(1)}, bf16[2048,544]{0,1:T(8,128)(2,1)}, u32[]{:S(2)}) copy-start(bf16[2048,544]{0,1:T(8,128)(2,1)} %param.21) | copy-start | bytes 6684676
  7.2 313.1 %all-reduce.12.cloned.1.call-start = ((), (), s32[]{:S(2)}) async-start(), calls=%async_computation.9 | async-start | bytes 2097152
  57.9 312.1 %copy-start.15 = (f32[16,2048]{1,0:T(8,128)S(1)}, f32[16,2048]{1,0:T(8,128)}, u32[]{:S(2)}) copy-start(f32[16,2048]{1,0:T(8,128)} %param.25) | copy-start | bytes 393220
  351.7 14.4 %all-to-all-start = ((bf16[4,32,256]{2,0,1:T(4,128)(2,1)}), bf16[4,32,256]{2,0,1:T(4,128)(2,1)S(1)}, u32[]{:S(2)}, u32[]{:S(2)}) async-start(bf16[4,32,256]{2,0,1:T(4,128)(2,1)} %get-tuple-element.41), calls=%async_computation | async-start | bytes 131072 | tf_op jit(solution)/shard_map/all_to_all | solution.py:13
  355.6 256.9 %all-gather.7.cloned.1.call-start = ((), (), s32[]{:S(2)}) async-start(), calls=%async_computation.8 | async-start | bytes 2162688 | tf_op jit(solution)/shard_map/all_gather | solution.py:87
  366.1 14.4 %all-to-all-start.2 = ((bf16[4,32,256]{2,0,1:T(4,128)(2,1)}), bf16[4,32,256]{2,0,1:T(4,128)(2,1)S(1)}, u32[]{:S(2)}, u32[]{:S(2)}) async-start(bf16[4,32,256]{2,0,1:T(4,128)(2,1)} %get-tuple-element.39), calls=%async_computation.2 | async-start | bytes 131072 | tf_op jit(solution)/shard_map/all_to_all | solution.py:13
  380.6 14.2 %all-to-all-start.4 = ((bf16[4,32,256]{2,0,1:T(4,128)(2,1)}), bf16[4,32,256]{2,0,1:T(4,128)(2,1)S(1)}, u32[]{:S(2)}, u32[]{:S(2)}) async-start(bf16[4,32,256]{2,0,1:T(4,128)(2,1)} %get-tuple-element.38), calls=%async_computation.4 | async-start | bytes 131072 | tf_op jit(solution)/shard_map/all_to_all | solution.py:13
  394.8 15.4 %all-to-all-start.6 = ((bf16[4,32,256]{2,0,1:T(4,128)(2,1)}), bf16[4,32,256]{2,0,1:T(4,128)(2,1)S(1)}, u32[]{:S(2)}, u32[]{:S(2)}) async-start(bf16[4,32,256]{2,0,1:T(4,128)(2,1)} %get-tuple-element.40), calls=%async_computation.6 | async-start | bytes 131072 | tf_op jit(solution)/shard_map/all_to_all | solution.py:13
  413.6 162.4 %copy-start.10 = (f32[4,3,2048]{2,0,1:T(4,128)S(1)}, f32[4,3,2048]{2,0,1:T(4,128)}, u32[]{:S(2)}) copy-start(f32[4,3,2048]{2,0,1:T(4,128)} %param.28) | copy-start | bytes 294916
  413.6 162.5 %copy-start.28 = (f32[4,2048]{1,0:T(4,128)S(1)}, f32[4,2048]{1,0:T(4,128)}, u32[]{:S(2)}) copy-start(f32[4,2048]{1,0:T(4,128)} %param.19) | copy-start | bytes 98308
  413.6 162.8 %copy-start.11 = (f32[2048]{0:T(1024)S(1)}, f32[2048]{0:T(1024)}, u32[]{:S(2)}) copy-start(f32[2048]{0:T(1024)} %param.20) | copy-start | bytes 24580
  576.3 39.3 %copy-start.7 = (f32[4,2048]{1,0:T(4,128)}, f32[4,2048]{1,0:T(4,128)S(1)}, u32[]{:S(2)}) copy-start(f32[4,2048]{1,0:T(4,128)S(1)} %get-tuple-element.11) | copy-start | bytes 98308
  576.3 39.3 %copy-start.8 = (f32[4,2048]{1,0:T(4,128)}, f32[4,2048]{1,0:T(4,128)S(1)}, u32[]{:S(2)}) copy-start(f32[4,2048]{1,0:T(4,128)S(1)} %get-tuple-element.12) | copy-start | bytes 98308
  576.3 39.3 %copy-start.9 = (f32[4,2048]{1,0:T(4,128)}, f32[4,2048]{1,0:T(4,128)S(1)}, u32[]{:S(2)}) copy-start(f32[4,2048]{1,0:T(4,128)S(1)} %get-tuple-element.13) | copy-start | bytes 98308
  616.1 46.2 %copy-start.3 = (bf16[2048,256]{1,0:T(8,128)(2,1)S(1)}, bf16[2048,256]{1,0:T(8,128)(2,1)}, u32[]{:S(2)}) copy-start(bf16[2048,256]{1,0:T(8,128)(2,1)} %param.27) | copy-start | bytes 3145732
  619.8 43.9 %copy-start.26 = (bf16[1,4,2048]{2,1,0:T(4,128)(2,1)S(1)}, bf16[1,4,2048]{2,1,0:T(4,128)(2,1)}, u32[]{:S(2)}) copy-start(bf16[1,4,2048]{2,1,0:T(4,128)(2,1)} %get-tuple-element.43) | copy-start | bytes 49156
  662.4 47.8 %copy-start.25 = (bf16[1,4,2048]{2,1,0:T(4,128)(2,1)S(1)}, bf16[1,4,2048]{2,1,0:T(4,128)(2,1)}, u32[]{:S(2)}) copy-start(bf16[1,4,2048]{2,1,0:T(4,128)(2,1)} %get-tuple-element.44) | copy-start | bytes 49156
  708.1 46.7 %copy-start.24 = (bf16[1,4,2048]{2,1,0:T(4,128)(2,1)S(1)}, bf16[1,4,2048]{2,1,0:T(4,128)(2,1)}, u32[]{:S(2)}) copy-start(bf16[1,4,2048]{2,1,0:T(4,128)(2,1)} %get-tuple-element.45) | copy-start | bytes 49156
  797.0 94.0 %copy-start.13 = (f32[4,1,2048]{2,0,1:T(4,128)S(1)}, f32[4,1,2048]{2,0,1:T(4,128)}, u32[]{:S(2)}) copy-start(f32[4,1,2048]{2,0,1:T(4,128)} %copy-done.12) | copy-start | bytes 98308
  801.0 100.6 %copy-start.5 = (f32[4,4,8192]{2,1,0:T(4,128)S(1)}, f32[4,4,8192]{2,1,0:T(4,128)}, u32[]{:S(2)}) copy-start(f32[4,4,8192]{2,1,0:T(4,128)} %copy-done.4) | copy-start | bytes 1572868
  843.8 14.4 %all-to-all-start.1 = ((bf16[32,4,256]{2,1,0:T(4,128)(2,1)}), bf16[32,4,256]{2,1,0:T(4,128)(2,1)S(1)}, u32[]{:S(2)}, u32[]{:S(2)}) async-start(bf16[32,4,256]{2,1,0:T(4,128)(2,1)} %all_to_all.91), calls=%async_computation.1 | async-start | bytes 131072 | tf_op jit(solution)/shard_map/all_to_all | solution.py:29
  858.2 14.4 %all-to-all-start.3 = ((bf16[32,4,256]{2,1,0:T(4,128)(2,1)}), bf16[32,4,256]{2,1,0:T(4,128)(2,1)S(1)}, u32[]{:S(2)}, u32[]{:S(2)}) async-start(bf16[32,4,256]{2,1,0:T(4,128)(2,1)} %all_to_all.96), calls=%async_computation.3 | async-start | bytes 131072 | tf_op jit(solution)/shard_map/all_to_all | solution.py:29
  872.6 14.4 %all-to-all-start.5 = ((bf16[32,4,256]{2,1,0:T(4,128)(2,1)}), bf16[32,4,256]{2,1,0:T(4,128)(2,1)S(1)}, u32[]{:S(2)}, u32[]{:S(2)}) async-start(bf16[32,4,256]{2,1,0:T(4,128)(2,1)} %all_to_all.101), calls=%async_computation.5 | async-start | bytes 131072 | tf_op jit(solution)/shard_map/all_to_all | solution.py:29
  887.1 14.4 %all-to-all-start.7 = ((bf16[32,4,256]{2,1,0:T(4,128)(2,1)}), bf16[32,4,256]{2,1,0:T(4,128)(2,1)S(1)}, u32[]{:S(2)}, u32[]{:S(2)}) async-start(bf16[32,4,256]{2,1,0:T(4,128)(2,1)} %all_to_all.106), calls=%async_computation.7 | async-start | bytes 131072 | tf_op jit(solution)/shard_map/all_to_all | solution.py:29
  (24 other events, 114.9 us)
Sparse Core Ops, SparseCore 0:
  58.0 262.1 all-reduce.11
  359.6 81.4 all-gather.6
where the time goes:
time: 912 us; the launch traced here: 909 us
  blocking collectives  472 us (52%)
  waiting for transfers between devices  330 us (36%)
  starting transfers between devices  31.9 us (3%)
  matrix products  31.3 us (3%)
  local copies, waits for them, and re-layouts  21.7 us (2%)
  between operations  15.5 us (2%)
    unnamed x3, waiting for transfers between devices  262 us
    all_gather x4, blocking collectives, output_rows(): lax.all_gather(gated_rows, 'batch', axis=0, tiled=True)  166 us
    unnamed x1, blocking collectives  160 us
    all_gather x1, blocking collectives, local(): every_ids = lax.all_gather(token_ids, 'batch', axis=1, tiled=True)  44.1 us
    psum x1, blocking collectives, output_rows(): mixed_cols = lax.psum(partial_out, 'chan').astype(jnp.bfloat16)  42.1 us
    all_to_all x4, waiting for transfers between devices, output_rows(): lax.all_to_all(mixed_cols, 'batch', split_axis=0, concat_axis=1, tiled=True)  39.6 us
    psum x1, blocking collectives, local(): lax.psum(jnp.dot(convolved_low, select_weight, preferred_element_type=jnp...  30.7 us
    all_to_all x4, waiting for transfers between devices, input_sums(): lax.all_to_all(normed_rows, 'batch', split_axis=1, concat_axis=0, tiled=T...  28.6 us
  transfers between devices with their start and end apart: 10, of which 9 were waited for; matrix products, arithmetic and copies ran while one was open for 3% of the time, Pallas kernels for 0%

commit v1 on v0

v1 whole, which is shorter than its diff:
```python
import jax
import jax.numpy as jnp
from jax import lax
from jax.sharding import Mesh, PartitionSpec as P

BATCH = ("h", "z", "k")
CHAN = ("x", "l")
SIZES = {"h": 2, "z": 8, "k": 2, "x": 4, "l": 2}
AXES = BATCH + CHAN
F32 = jnp.float32
BF16 = jnp.bfloat16


def count(axes):
    total = 1
    for axis in axes:
        total *= SIZES[axis]
    return total


def gather_copies(block, axes):
    copies = jnp.broadcast_to(block[None], (count(axes),) + block.shape)
    return lax.all_to_all(copies, axes, 0, 0, tiled=True)


def swap(block, axis):
    return lax.ppermute(block, axis, [(0, 1), (1, 0)])


def feature_route():
    pairs = []
    for b in range(32):
        for c in range(8):
            pairs.append((b * 8 + c, (4 * c + b // 8) * 8 + b % 8))
    return pairs


def ring_gather(block, axis):
    n = SIZES[axis]
    up = [(i, (i + 1) % n) for i in range(n)]
    down = [(i, (i - 1) % n) for i in range(n)]
    found = {0: block}
    a = b = block
    for step in range(1, n // 2 + 1):
        a = lax.ppermute(a, axis, up)
        found[-step % n] = a
        if step < n // 2:
            b = lax.ppermute(b, axis, down)
            found[step] = b
    return [found[i] for i in range(n)]


def local(
    token_ids,
    embed_table,
    norm_gain,
    in_weight,
    filter_weight,
    filter_bias,
    select_weight,
    step_gain,
    step_weight,
    step_bias,
    decay_log,
    skip_gain,
    out_weight,
    filter_state,
    scan_state,
):
    steps, reqs = token_ids.shape
    vocab_rows, width = embed_table.shape
    feats, _, channels = in_weight.shape
    half = channels // 2
    rank_size = step_gain.shape[0]
    state_size = decay_log.shape[0]
    rows = steps * reqs
    nb, nc = count(BATCH), count(CHAN)
    tokens = nb * rows
    core = lax.axis_index("k")
    me = lax.axis_index(BATCH)
    features = norm_gain.shape[0]

    step_full = lax.all_gather(step_weight, BATCH, axis=0, tiled=True)
    halves = in_weight.reshape(feats, 2, 2, half)
    w_mine = lax.dynamic_index_in_dim(halves, core, axis=2, keepdims=False)
    w_other = swap(lax.dynamic_index_in_dim(halves, 1 - core, axis=2, keepdims=False), "k")

    ids = gather_copies(token_ids.reshape(rows), BATCH).reshape(tokens)
    vocab_index = me * vocab_rows + lax.broadcasted_iota(jnp.int32, (vocab_rows, tokens), 0)
    hot = (vocab_index == ids[None, :]).astype(BF16)
    picked = lax.dot_general(
        embed_table, hot, (((0,), (0,)), ((), ())), preferred_element_type=F32
    ).astype(BF16)
    pieces = lax.all_to_all(picked.reshape(nb, width // nb, tokens), BATCH, 0, 0, tiled=True)
    piece = jnp.sum(pieces.astype(F32), axis=0).astype(BF16)
    piece = lax.ppermute(piece, AXES, feature_route())
    chip_feats = gather_copies(piece, ("k",) + CHAN).reshape(2, feats, tokens)

    wide = chip_feats.astype(F32)
    square = jnp.sum(wide * wide, axis=(0, 1))
    gains = lax.dynamic_slice_in_dim(norm_gain, (me - core) * feats, 2 * feats).reshape(2, feats)
    scaled = (wide * gains[:, :, None]).astype(BF16)
    x_mine = lax.dynamic_index_in_dim(scaled, core, keepdims=False)
    x_other = lax.dynamic_index_in_dim(scaled, 1 - core, keepdims=False)
    own_feats = lax.dynamic_index_in_dim(chip_feats, core, keepdims=False)

    def project(which):
        dims = (((0,), (0,)), ((), ()))
        return lax.dot_general(
            x_mine, w_mine[:, which], dims, preferred_element_type=F32
        ) + lax.dot_general(x_other, w_other[:, which], dims, preferred_element_type=F32)

    def exchange(part):
        sent = part.astype(BF16).reshape(nb, rows, part.shape[1])
        got = lax.all_to_all(sent, BATCH, 0, 0, tiled=True)
        return got.reshape(nb // 2, 2, rows, part.shape[1]).astype(F32)

    square = square[:, None]
    high = square.astype(BF16)
    low = (square - high.astype(F32)).astype(BF16)
    lane = lax.broadcasted_iota(jnp.int32, (1, 128), 1)
    tail = jnp.where(lane == 0, high, jnp.where(lane == 1, low, 0.0)).astype(F32)
    got = exchange(jnp.concatenate([project(0), tail], axis=1))
    summed = jnp.sum(got, axis=0)
    total = jnp.sum(summed[0, :, half : half + 2], axis=1, keepdims=True)
    scale = lax.rsqrt(total / features + 1e-06)

    def finish(two):
        return (jnp.concatenate([two[0], two[1]], axis=1) * scale).astype(BF16).astype(F32)

    stream = finish(summed[:, :, :half])
    gate_part = project(1)
    gate = finish(jnp.sum(exchange(gate_part), axis=0))

    stream = stream.reshape(steps, reqs, channels)
    window = jnp.concatenate([filter_state.transpose(1, 0, 2), stream], axis=0)
    taps = filter_weight.shape[0]
    mixed_in = sum(window[i : i + steps] * filter_weight[i] for i in range(taps))
    convolved = jax.nn.silu(mixed_in + filter_bias)
    filter_out = window[steps:].transpose(1, 0, 2)
    conv_rows = convolved.reshape(rows, channels)
    part = jnp.dot(conv_rows.astype(BF16), select_weight, preferred_element_type=F32)
    selected = jnp.sum(gather_copies(part, CHAN), axis=0)
    rank = selected[:, :rank_size]
    bvec = selected[:, rank_size : rank_size + state_size].reshape(steps, reqs, state_size)
    cvec = selected[:, rank_size + state_size :].reshape(steps, reqs, state_size)
    mean_square = jnp.mean(rank * rank, axis=-1, keepdims=True)
    rank_normed = (rank * lax.rsqrt(mean_square + 1e-06) * step_gain).astype(BF16)
    delta = jax.nn.softplus(
        jnp.dot(rank_normed, step_full, preferred_element_type=F32) + step_bias
    ).reshape(steps, reqs, channels)

    decay_rate = -jnp.exp(decay_log)
    scan_now = scan_state
    readouts = []
    for t in range(steps):
        factor = jnp.exp(delta[t][:, None, :] * decay_rate[None])
        scan_now = factor * scan_now + (delta[t] * convolved[t])[:, None, :] * bvec[t][:, :, None]
        readouts.append(jnp.sum(scan_now * cvec[t][:, :, None], axis=1) + skip_gain * convolved[t])
    readout = jnp.stack(readouts).reshape(rows, channels)
    gated = (readout * jax.nn.silu(gate)).astype(BF16)

    both = jnp.stack([gated, swap(gated, "h")])
    ring = jnp.stack(ring_gather(both, "z"))
    every = jnp.stack([ring, swap(ring, "k")])
    part_out = jnp.dot(
        every.reshape(tokens, channels), out_weight, preferred_element_type=F32
    ).astype(BF16)
    per = rows // nc
    sent = part_out.reshape(nb, nc, per, feats).transpose(1, 0, 2, 3)
    got = lax.all_to_all(sent, CHAN, 0, 0, tiled=True)
    mixed = jnp.sum(got.astype(F32), axis=0).astype(BF16)

    z, h = lax.axis_index("z"), lax.axis_index("h")
    dest = lax.broadcasted_iota(jnp.int32, (nb, 1), 0)
    source = lax.broadcasted_iota(jnp.int32, (1, nb), 1)
    s_k, s_z, s_h = source // 16, (source // 2) % 8, source % 2
    place = ((s_h + h) % 2) * 16 + ((s_z + z) % 8) * 2 + (s_k + core) % 2
    order = (dest == place).astype(BF16)
    mixed = jnp.dot(order, mixed.reshape(nb, per * feats), preferred_element_type=F32)
    mixed = mixed.reshape(nb * per, feats)
    column = lax.axis_index(CHAN)
    row = lax.broadcasted_iota(jnp.int32, (nb * per, 1), 0)
    token = lax.broadcasted_iota(jnp.int32, (1, tokens), 1)
    pick = (token == (row // per) * rows + column * per + row % per).astype(BF16)
    embedded = lax.dot_general(
        pick, own_feats, (((1,), (1,)), ((), ())), preferred_element_type=F32
    )
    hidden = (embedded + mixed).astype(BF16).reshape(nb, per, feats)
    home = lax.all_to_all(hidden, BATCH, 0, 0, tiled=True)
    home = home.transpose(1, 0, 2).reshape(per, nb * feats)
    hidden = gather_copies(home, CHAN).reshape(steps, reqs, features)
    return (hidden, filter_out, scan_now)


def solution(mesh):
    fine = Mesh(mesh.devices.reshape([SIZES[axis] for axis in AXES]), AXES)
    return jax.shard_map(
        local,
        mesh=fine,
        in_specs=(
            P(None, BATCH),
            P(BATCH, CHAN),
            P(),
            P(BATCH, None, CHAN),
            P(None, CHAN),
            P(CHAN),
            P(CHAN, None),
            P(),
            P(BATCH, CHAN),
            P(CHAN),
            P(None, CHAN),
            P(CHAN),
            P(CHAN, BATCH),
            P(BATCH, None, CHAN),
            P(BATCH, None, CHAN),
        ),
        out_specs=(P(None, BATCH, None), P(BATCH, None, CHAN), P(BATCH, None, CHAN)),
        check_vma=False,
    )
```

time: 912 us -> 300 us (0.33)
  blocking collectives: 472 us -> 33.5 us
  waiting for transfers between devices: 330 us -> 127 us
  starting transfers between devices: 31.9 us -> 67.8 us
  matrix products: 31.3 us -> 16.5 us
    unnamed x3 -> x1, waiting for transfers between devices: 262 us -> 0.68 us
    all_gather x6 -> x0, blocking collectives: 239 us -> none  [the longest x4 166 us: output_rows(): lax.all_gather(gated_rows, 'batch', axis=0, tiled=True)]
    unnamed x1 -> x0, blocking collectives: 160 us -> none
    psum x2 -> x0, blocking collectives: 72.8 us -> none  [the longest x1 42.1 us: output_rows(): mixed_cols = lax.psum(partial_out, 'chan').astype(jnp.bfloat16)]
    all_to_all x0 -> x1, blocking collectives: none -> 33.5 us  [local(): lax.all_to_all(picked.reshape(nb, width // nb, tokens), BATCH, 0, 0, tile...]
    ppermute x0 -> x11, waiting for transfers between devices: none -> 27.2 us  [the longest x4 13.2 us: ring_gather(): a = lax.ppermute(a, axis, up)]
    all_to_all x8, waiting for transfers between devices: 68.2 us -> 92.3 us  [the longest x2 56.3 us: exchange(): got = lax.all_to_all(sent, BATCH, 0, 0, tiled=True)]
    all_to_all x8, starting transfers between devices: 31.8 us -> 53.9 us  [the longest x4 31.2 us: gather_copies(): return lax.all_to_all(copies, axes, 0, 0, tiled=True)]
  transfers between devices with their start and end apart: 10 -> 20, of which waited for: 9 -> 15; matrix products, arithmetic and copies ran while one was open for 3% -> 10% of each run, Pallas kernels for 0% -> 0%
where the time goes in v1:
time: 300 us; the launch traced here: 298 us
  waiting for transfers between devices  127 us (42%)
  starting transfers between devices  67.8 us (23%)
  blocking collectives  33.5 us (11%)
  local copies, waits for them, and re-layouts  27.2 us (9%)
  matrix products  16.5 us (6%)
  between operations  14.6 us (5%)
  other arithmetic  11.5 us (4%)
    all_to_all x2, waiting for transfers between devices, exchange(): got = lax.all_to_all(sent, BATCH, 0, 0, tiled=True)  56.3 us
    all_to_all x1, blocking collectives, local(): lax.all_to_all(picked.reshape(nb, width // nb, tokens), BATCH, 0, 0, tile...  33.5 us
    all_to_all x4, starting transfers between devices, gather_copies(): return lax.all_to_all(copies, axes, 0, 0, tiled=True)  31.2 us
    all_to_all x4, waiting for transfers between devices, gather_copies(): return lax.all_to_all(copies, axes, 0, 0, tiled=True)  19.6 us
    ppermute x4, waiting for transfers between devices, ring_gather(): a = lax.ppermute(a, axis, up)  13.2 us
    all_to_all x2, starting transfers between devices, exchange(): got = lax.all_to_all(sent, BATCH, 0, 0, tiled=True)  11.9 us
    all_to_all x1, waiting for transfers between devices, local(): home = lax.all_to_all(hidden, BATCH, 0, 0, tiled=True)  10 us
    ppermute x3, starting transfers between devices, ring_gather(): b = lax.ppermute(b, axis, down)  9.12 us
  transfers between devices with their start and end apart: 20, of which 15 were waited for; matrix products, arithmetic and copies ran while one was open for 10% of the time, Pallas kernels for 0%

profile of v1, /device:TPU:8, one launch (start us, length us, event | category | flops | bytes accessed | tf_op | source)
XLA Modules:
  0.0 298.0 jit_solution(15853864697035029160)
XLA Ops:
  8.7 10.6 %all-to-all-start = ((s32[32,1,16]{2,1,0:T(1,128)}), s32[32,1,16]{2,1,0:T(1,128)S(1)}, u32[]{:S(2)}, u32[]{:S(2)}) async-start(s32[32,1,16]{2,1,0:T(1,128)} %broadcast_in_dim.49), calls=%async_computation | async-start | bytes 32768 | tf_op jit(solution)/shard_map/all_to_all | solution.py:23
  19.3 9.8 %all-to-all-done = s32[32,1,16]{2,1,0:T(1,128)S(1)} async-done(((s32[32,1,16]{2,1,0:T(1,128)}), s32[32,1,16]{2,1,0:T(1,128)S(1)}, u32[]{:S(2)}, u32[]{:S(2)}) %all-to-all-start) | async-done | bytes 2080 | tf_op jit(solution)/shard_map/all_to_all | solution.py:23
  30.4 5.6 %fusion.7 = bf16[1024,512]{0,1:T(8,128)(2,1)} fusion(bf16[2048,1024]{1,0:T(8,128)(2,1)} %param.16, s32[512]{0:T(512)S(1)} %eq.69, s32[2048]{0:T(1024)S(1)} %iota_add_fusion), kind=kOutput, calls=%fused_computation.11 | convolution fusion | flops 2149056512 | bytes 5253120 | tf_op jit(solution)/shard_map/dot_general | solution.py:91
  37.5 33.5 %all_to_all.46 = bf16[32,32,512]{2,1,0:T(8,128)(2,1)} all-to-all(bf16[32,32,512]{2,1,0:T(8,128)(2,1)S(1)} %bitcast.108), channel_id=1, replica_groups=mesh['h'=2,'z'=8,'k'=2,'x'=4,'l'=2] {'h','z','k'}, dimensions={0} | all-to-all | bytes 2097152 | tf_op jit(solution)/shard_map/all_to_all | solution.py:94
  72.5 3.8 %collective-permute-start = (bf16[32,512]{1,0:T(8,128)(2,1)S(1)}, bf16[32,512]{1,0:T(8,128)(2,1)S(1)}, u32[]{:S(2)}, u32[]{:S(2)}) collective-permute-start(bf16[32,512]{1,0:T(8,128)(2,1)S(1)} %reduce_sum.124), channel_id=1, source_target_pairs={{0,0},{1,32},{2,64},{3,96},{4,128},{5,160},{6,192},{7,224},{8,1},{... | collective-permute-start | bytes 98312 | tf_op jit(solution)/shard_map/ppermute | solution.py:96
  78.7 10.2 %all-to-all-start.2 = ((bf16[16,32,512]{2,1,0:T(8,128)(2,1)}), bf16[16,32,512]{2,1,0:T(8,128)(2,1)S(1)}, u32[]{:S(2)}, u32[]{:S(2)}) async-start(bf16[16,32,512]{2,1,0:T(8,128)(2,1)} %broadcast_in_dim.50), calls=%async_computation.2 | async-start | bytes 1048576 | tf_op jit(solution)/shard_map/all_to_all | solution.py:23
  89.0 6.1 %copy.29 = bf16[256,2,2048]{0,2,1:T(8,128)(2,1)} copy(bf16[256,2,2048]{2,1,0:T(2,128)(2,1)} %param.18) | data formatting | bytes 4194304 | tf_op args[3]
  108.4 7.1 %all-to-all-start.3 = ((bf16[32,16,1152]{2,1,0:T(8,128)(2,1)}), bf16[32,16,1152]{2,1,0:T(8,128)(2,1)}, u32[]{:S(2)}, u32[]{:S(2)}) async-start(bf16[32,16,1152]{2,1,0:T(8,128)(2,1)} %pad_maximum_fusion.1), calls=%async_computation.3 | async-start | bytes 2359296 | tf_op jit(solution)/shard_map/all_to_all | solution.py:115
  120.3 28.9 %all-to-all-done.3 = bf16[32,16,1152]{2,1,0:T(8,128)(2,1)} async-done(((bf16[32,16,1152]{2,1,0:T(8,128)(2,1)}), bf16[32,16,1152]{2,1,0:T(8,128)(2,1)}, u32[]{:S(2)}, u32[]{:S(2)}) %all-to-all-start.3) | async-done | bytes 1179680 | tf_op jit(solution)/shard_map/all_to_all | solution.py:115
  149.2 4.8 %all-to-all-start.5 = ((bf16[32,16,1024]{2,1,0:T(8,128)(2,1)}), bf16[32,16,1024]{2,1,0:T(8,128)(2,1)}, u32[]{:S(2)}, u32[]{:S(2)}) async-start(bf16[32,16,1024]{2,1,0:T(8,128)(2,1)} %bitcast.109), calls=%async_computation.5 | async-start | bytes 2097152 | tf_op jit(solution)/shard_map/all_to_all | solution.py:115
  157.4 27.4 %all-to-all-done.5 = bf16[32,16,1024]{2,1,0:T(8,128)(2,1)} async-done(((bf16[32,16,1024]{2,1,0:T(8,128)(2,1)}), bf16[32,16,1024]{2,1,0:T(8,128)(2,1)}, u32[]{:S(2)}, u32[]{:S(2)}) %all-to-all-start.5) | async-done | bytes 1048608 | tf_op jit(solution)/shard_map/all_to_all | solution.py:115
  185.6 5.6 %all-to-all-start.4 = ((f32[8,16,544]{2,1,0:T(8,128)}), f32[8,16,544]{2,1,0:T(8,128)S(1)}, u32[]{:S(2)}, u32[]{:S(2)}) async-start(f32[8,16,544]{2,1,0:T(8,128)} %broadcast_in_dim.56), calls=%async_computation.4 | async-start | bytes 655360 | tf_op jit(solution)/shard_map/all_to_all | solution.py:23
  193.3 4.4 %all-to-all-done.4 = f32[8,16,544]{2,1,0:T(8,128)S(1)} async-done(((f32[8,16,544]{2,1,0:T(8,128)}), f32[8,16,544]{2,1,0:T(8,128)S(1)}, u32[]{:S(2)}, u32[]{:S(2)}) %all-to-all-start.4) | async-done | bytes 278560 | tf_op jit(solution)/shard_map/all_to_all | solution.py:23
  198.5 6.8 %all-gather.2.cloned.1.call-done = bf16[512,2048]{1,0:T(8,128)(2,1)} async-done(((bf16[16,2048]{1,0:T(8,128)(2,1)}), bf16[512,2048]{1,0:T(8,128)(2,1)}) %all-gather.2.cloned.1.call-update) | async-done | bytes 2097168 | tf_op jit(solution)/shard_map/all_gather | solution.py:83
  212.1 4.4 %collective-permute-done.2 = bf16[16,2048]{1,0:T(8,128)(2,1)S(1)} collective-permute-done((bf16[16,2048]{1,0:T(8,128)(2,1)S(1)}, bf16[16,2048]{1,0:T(8,128)(2,1)S(1)}, u32[]{:S(2)}, u32[]{:S(2)}) %collective-permute-start.2) | collective-permute-done | bytes 65568 | tf_op jit(solution)/shard_map/ppermute | solution.py:27
  227.4 3.7 %collective-permute-start.5 = (bf16[2,16,2048]{2,1,0:T(8,128)(2,1)S(1)}, bf16[2,16,2048]{2,1,0:T(8,128)(2,1)S(1)}, u32[]{:S(2)}, u32[]{:S(2)}) collective-permute-start(bf16[2,16,2048]{2,1,0:T(8,128)(2,1)S(1)} %collective-permute-done.4), channel_id=1, source_target_pairs={{0,112},{16,0},{32,16},{48,32},{64,48},{80,64},{96,80},{112,96},{1... | collective-permute-start | bytes 393224 | tf_op jit(solution)/shard_map/ppermute | solution.py:48
  231.1 7.0 %collective-permute-done.8 = bf16[2,16,2048]{2,1,0:T(8,128)(2,1)S(1)} collective-permute-done((bf16[2,16,2048]{2,1,0:T(8,128)(2,1)S(1)}, bf16[2,16,2048]{2,1,0:T(8,128)(2,1)S(1)}, u32[]{:S(2)}, u32[]{:S(2)}) %collective-permute-start.8) | collective-permute-done | bytes 131104 | tf_op jit(solution)/shard_map/ppermute | solution.py:45
  238.1 6.2 %collective-permute-done.9 = bf16[2,16,2048]{2,1,0:T(8,128)(2,1)S(1)} collective-permute-done((bf16[2,16,2048]{2,1,0:T(8,128)(2,1)S(1)}, bf16[2,16,2048]{2,1,0:T(8,128)(2,1)S(1)}, u32[]{:S(2)}, u32[]{:S(2)}) %collective-permute-start.9) | collective-permute-done | bytes 131104 | tf_op jit(solution)/shard_map/ppermute | solution.py:45
  250.1 5.7 %all-to-all-start.6 = ((bf16[8,32,2,256]{3,2,1,0:T(2,128)(2,1)}), bf16[8,32,2,256]{3,2,1,0:T(2,128)(2,1)S(1)}, u32[]{:S(2)}, u32[]{:S(2)}) async-start(bf16[8,32,2,256]{3,2,1,0:T(2,128)(2,1)} %bitcast.103), calls=%async_computation.6 | async-start | bytes 524288 | tf_op jit(solution)/shard_map/all_to_all | solution.py:171
  255.8 6.4 %all-to-all-done.6 = bf16[8,32,2,256]{3,2,1,0:T(2,128)(2,1)S(1)} async-done(((bf16[8,32,2,256]{3,2,1,0:T(2,128)(2,1)}), bf16[8,32,2,256]{3,2,1,0:T(2,128)(2,1)S(1)}, u32[]{:S(2)}, u32[]{:S(2)}) %all-to-all-start.6) | async-done | bytes 262176 | tf_op jit(solution)/shard_map/all_to_all | solution.py:171
  263.5 5.0 %all-to-all-start.7 = ((bf16[32,2,256]{2,1,0:T(2,128)(2,1)}), bf16[32,2,256]{2,1,0:T(2,128)(2,1)S(1)}, u32[]{:S(2)}, u32[]{:S(2)}) async-start(bf16[32,2,256]{2,1,0:T(2,128)(2,1)} %reshape.547), calls=%async_computation.7 | async-start | bytes 65536 | tf_op jit(solution)/shard_map/all_to_all | solution.py:190
  268.6 10.0 %all-to-all-done.7 = bf16[32,2,256]{2,1,0:T(2,128)(2,1)S(1)} async-done(((bf16[32,2,256]{2,1,0:T(2,128)(2,1)}), bf16[32,2,256]{2,1,0:T(2,128)(2,1)S(1)}, u32[]{:S(2)}, u32[]{:S(2)}) %all-to-all-start.7) | async-done | bytes 32800 | tf_op jit(solution)/shard_map/all_to_all | solution.py:190
  279.4 4.8 %all-to-all-start.8 = ((bf16[8,2,8192]{2,1,0:T(2,128)(2,1)}), bf16[8,2,8192]{2,1,0:T(2,128)(2,1)S(1)}, u32[]{:S(2)}, u32[]{:S(2)}) async-start(bf16[8,2,8192]{2,1,0:T(2,128)(2,1)} %broadcast_in_dim.90), calls=%async_computation.8 | async-start | bytes 524288 | tf_op jit(solution)/shard_map/all_to_all | solution.py:23
  285.0 5.4 %all-to-all-done.8 = bf16[8,2,8192]{2,1,0:T(2,128)(2,1)S(1)} async-done(((bf16[8,2,8192]{2,1,0:T(2,128)(2,1)}), bf16[8,2,8192]{2,1,0:T(2,128)(2,1)S(1)}, u32[]{:S(2)}, u32[]{:S(2)}) %all-to-all-start.8) | async-done | bytes 262176 | tf_op jit(solution)/shard_map/all_to_all | solution.py:23
  (138 shorter events, 60.2 us)
Async XLA Ops:
  7.2 149.5 %copy-start = (bf16[2048,544]{0,1:T(8,128)(2,1)S(1)}, bf16[2048,544]{0,1:T(8,128)(2,1)}, u32[]{:S(2)}) copy-start(bf16[2048,544]{0,1:T(8,128)(2,1)} %param.21) | copy-start | bytes 6684676
  8.7 20.4 %all-to-all-start = ((s32[32,1,16]{2,1,0:T(1,128)}), s32[32,1,16]{2,1,0:T(1,128)S(1)}, u32[]{:S(2)}, u32[]{:S(2)}) async-start(s32[32,1,16]{2,1,0:T(1,128)} %broadcast_in_dim.49), calls=%async_computation | async-start | bytes 32768 | tf_op jit(solution)/shard_map/all_to_all | solution.py:23
  72.5 5.4 %collective-permute-start = (bf16[32,512]{1,0:T(8,128)(2,1)S(1)}, bf16[32,512]{1,0:T(8,128)(2,1)S(1)}, u32[]{:S(2)}, u32[]{:S(2)}) collective-permute-start(bf16[32,512]{1,0:T(8,128)(2,1)S(1)} %reduce_sum.124), channel_id=1, source_target_pairs={{0,0},{1,32},{2,64},{3,96},{4,128},{5,160},{6,192},{7,224},{8,1},{... | collective-permute-start | bytes 98312 | tf_op jit(solution)/shard_map/ppermute | solution.py:96
  78.7 24.8 %all-to-all-start.2 = ((bf16[16,32,512]{2,1,0:T(8,128)(2,1)}), bf16[16,32,512]{2,1,0:T(8,128)(2,1)S(1)}, u32[]{:S(2)}, u32[]{:S(2)}) async-start(bf16[16,32,512]{2,1,0:T(8,128)(2,1)} %broadcast_in_dim.50), calls=%async_computation.2 | async-start | bytes 1048576 | tf_op jit(solution)/shard_map/all_to_all | solution.py:23
  100.3 5.4 %collective-permute-start.1 = (bf16[256,2,1024]{2,0,1:T(8,128)(2,1)}, bf16[256,2,1024]{2,0,1:T(8,128)(2,1)}, u32[]{:S(2)}, u32[]{:S(2)}) collective-permute-start(bf16[256,2,1024]{2,0,1:T(8,128)(2,1)} %bitcast.115), channel_id=1, source_target_pairs={{0,8},{8,0},{1,9},{9,1},{2,10},{10,2},{3,11},{11,3},{4,12},{12,4},... | collective-permute-start | bytes 3145736 | tf_op jit(solution)/shard_map/ppermute | solution.py:27
  108.4 40.8 %all-to-all-start.3 = ((bf16[32,16,1152]{2,1,0:T(8,128)(2,1)}), bf16[32,16,1152]{2,1,0:T(8,128)(2,1)}, u32[]{:S(2)}, u32[]{:S(2)}) async-start(bf16[32,16,1152]{2,1,0:T(8,128)(2,1)} %pad_maximum_fusion.1), calls=%async_computation.3 | async-start | bytes 2359296 | tf_op jit(solution)/shard_map/all_to_all | solution.py:115
  115.5 89.8 %all-gather.2.cloned.1.call-start = ((), (), s32[]{:S(2)}) async-start(), calls=%async_computation.9 | async-start | bytes 2162688 | tf_op jit(solution)/shard_map/all_gather | solution.py:83
  149.2 35.6 %all-to-all-start.5 = ((bf16[32,16,1024]{2,1,0:T(8,128)(2,1)}), bf16[32,16,1024]{2,1,0:T(8,128)(2,1)}, u32[]{:S(2)}, u32[]{:S(2)}) async-start(bf16[32,16,1024]{2,1,0:T(8,128)(2,1)} %bitcast.109), calls=%async_computation.5 | async-start | bytes 2097152 | tf_op jit(solution)/shard_map/all_to_all | solution.py:115
  157.4 47.9 %copy-start.9 = (f32[2048]{0:T(1024)S(1)}, f32[2048]{0:T(1024)}, u32[]{:S(2)}) copy-start(f32[2048]{0:T(1024)} %param.24) | copy-start | bytes 24580
  157.4 47.9 %copy-start.17 = (f32[512]{0:T(512)S(1)}, f32[512]{0:T(512)}, u32[]{:S(2)}) copy-start(f32[512]{0:T(512)} %param.22) | copy-start | bytes 6148
  185.6 12.1 %all-to-all-start.4 = ((f32[8,16,544]{2,1,0:T(8,128)}), f32[8,16,544]{2,1,0:T(8,128)S(1)}, u32[]{:S(2)}, u32[]{:S(2)}) async-start(f32[8,16,544]{2,1,0:T(8,128)} %broadcast_in_dim.56), calls=%async_computation.4 | async-start | bytes 655360 | tf_op jit(solution)/shard_map/all_to_all | solution.py:23
  210.7 5.9 %collective-permute-start.2 = (bf16[16,2048]{1,0:T(8,128)(2,1)S(1)}, bf16[16,2048]{1,0:T(8,128)(2,1)S(1)}, u32[]{:S(2)}, u32[]{:S(2)}) collective-permute-start(bf16[16,2048]{1,0:T(8,128)(2,1)S(1)} %fusion.45), channel_id=1, source_target_pairs={{0,128},{128,0},{1,129},{129,1},{2,130},{130,2},{3,131},{131,3},{4... | collective-permute-start | bytes 196616 | tf_op jit(solution)/shard_map/ppermute | solution.py:27
  216.5 5.0 %collective-permute-start.3 = (bf16[2,16,2048]{2,1,0:T(8,128)(2,1)S(1)}, bf16[2,16,2048]{2,1,0:T(8,128)(2,1)S(1)}, u32[]{:S(2)}, u32[]{:S(2)}) collective-permute-start(bf16[2,16,2048]{2,1,0:T(8,128)(2,1)S(1)} %pad_maximum_fusion.5), channel_id=1, source_target_pairs={{0,112},{16,0},{32,16},{48,32},{64,48},{80,64},{96,80},{112,96},{1... | collective-permute-start | bytes 393224 | tf_op jit(solution)/shard_map/ppermute | solution.py:48
  218.7 6.2 %collective-permute-start.6 = (bf16[2,16,2048]{2,1,0:T(8,128)(2,1)S(1)}, bf16[2,16,2048]{2,1,0:T(8,128)(2,1)S(1)}, u32[]{:S(2)}, u32[]{:S(2)}) collective-permute-start(bf16[2,16,2048]{2,1,0:T(8,128)(2,1)S(1)} %pad_maximum_fusion.5), channel_id=1, source_target_pairs={{0,16},{16,32},{32,48},{48,64},{64,80},{80,96},{96,112},{112,0},{1... | collective-permute-start | bytes 393224 | tf_op jit(solution)/shard_map/ppermute | solution.py:45
  221.6 5.8 %collective-permute-start.4 = (bf16[2,16,2048]{2,1,0:T(8,128)(2,1)S(1)}, bf16[2,16,2048]{2,1,0:T(8,128)(2,1)S(1)}, u32[]{:S(2)}, u32[]{:S(2)}) collective-permute-start(bf16[2,16,2048]{2,1,0:T(8,128)(2,1)S(1)} %collective-permute-done.3), channel_id=1, source_target_pairs={{0,112},{16,0},{32,16},{48,32},{64,48},{80,64},{96,80},{112,96},{1... | collective-permute-start | bytes 393224 | tf_op jit(solution)/shard_map/ppermute | solution.py:48
  224.9 6.2 %collective-permute-start.7 = (bf16[2,16,2048]{2,1,0:T(8,128)(2,1)S(1)}, bf16[2,16,2048]{2,1,0:T(8,128)(2,1)S(1)}, u32[]{:S(2)}, u32[]{:S(2)}) collective-permute-start(bf16[2,16,2048]{2,1,0:T(8,128)(2,1)S(1)} %collective-permute-done.6), channel_id=1, source_target_pairs={{0,16},{16,32},{32,48},{48,64},{64,80},{80,96},{96,112},{112,0},{1... | collective-permute-start | bytes 393224 | tf_op jit(solution)/shard_map/ppermute | solution.py:45
  227.4 10.7 %collective-permute-start.5 = (bf16[2,16,2048]{2,1,0:T(8,128)(2,1)S(1)}, bf16[2,16,2048]{2,1,0:T(8,128)(2,1)S(1)}, u32[]{:S(2)}, u32[]{:S(2)}) collective-permute-start(bf16[2,16,2048]{2,1,0:T(8,128)(2,1)S(1)} %collective-permute-done.4), channel_id=1, source_target_pairs={{0,112},{16,0},{32,16},{48,32},{64,48},{80,64},{96,80},{112,96},{1... | collective-permute-start | bytes 393224 | tf_op jit(solution)/shard_map/ppermute | solution.py:48
  231.1 7.1 %collective-permute-start.8 = (bf16[2,16,2048]{2,1,0:T(8,128)(2,1)S(1)}, bf16[2,16,2048]{2,1,0:T(8,128)(2,1)S(1)}, u32[]{:S(2)}, u32[]{:S(2)}) collective-permute-start(bf16[2,16,2048]{2,1,0:T(8,128)(2,1)S(1)} %collective-permute-done.7), channel_id=1, source_target_pairs={{0,16},{16,32},{32,48},{48,64},{64,80},{80,96},{96,112},{112,0},{1... | collective-permute-start | bytes 393224 | tf_op jit(solution)/shard_map/ppermute | solution.py:45
  238.1 6.2 %collective-permute-start.9 = (bf16[2,16,2048]{2,1,0:T(8,128)(2,1)S(1)}, bf16[2,16,2048]{2,1,0:T(8,128)(2,1)S(1)}, u32[]{:S(2)}, u32[]{:S(2)}) collective-permute-start(bf16[2,16,2048]{2,1,0:T(8,128)(2,1)S(1)} %collective-permute-done.8), channel_id=1, source_target_pairs={{0,16},{16,32},{32,48},{48,64},{64,80},{80,96},{96,112},{112,0},{1... | collective-permute-start | bytes 393224 | tf_op jit(solution)/shard_map/ppermute | solution.py:45
  244.4 2.7 collective-permute-start.10
  249.1 35.2 %copy-start.3 = (f32[16,1024]{1,0:T(8,128)S(1)}, f32[16,1024]{1,0:T(8,128)}, u32[]{:S(2)}) copy-start(f32[16,1024]{1,0:T(8,128)} %get-tuple-element.20) | copy-start | bytes 196612
  250.1 12.1 %all-to-all-start.6 = ((bf16[8,32,2,256]{3,2,1,0:T(2,128)(2,1)}), bf16[8,32,2,256]{3,2,1,0:T(2,128)(2,1)S(1)}, u32[]{:S(2)}, u32[]{:S(2)}) async-start(bf16[8,32,2,256]{3,2,1,0:T(2,128)(2,1)} %bitcast.103), calls=%async_computation.6 | async-start | bytes 524288 | tf_op jit(solution)/shard_map/all_to_all | solution.py:171
  263.5 15.1 %all-to-all-start.7 = ((bf16[32,2,256]{2,1,0:T(2,128)(2,1)}), bf16[32,2,256]{2,1,0:T(2,128)(2,1)S(1)}, u32[]{:S(2)}, u32[]{:S(2)}) async-start(bf16[32,2,256]{2,1,0:T(2,128)(2,1)} %reshape.547), calls=%async_computation.7 | async-start | bytes 65536 | tf_op jit(solution)/shard_map/all_to_all | solution.py:190
  279.4 11.0 %all-to-all-start.8 = ((bf16[8,2,8192]{2,1,0:T(2,128)(2,1)}), bf16[8,2,8192]{2,1,0:T(2,128)(2,1)S(1)}, u32[]{:S(2)}, u32[]{:S(2)}) async-start(bf16[8,2,8192]{2,1,0:T(2,128)(2,1)} %broadcast_in_dim.90), calls=%async_computation.8 | async-start | bytes 524288 | tf_op jit(solution)/shard_map/all_to_all | solution.py:23
  (15 other events, 160.0 us)
Sparse Core Ops, SparseCore 0:
  119.1 86.1 all-gather.1

commit v2 on v1

v2 whole, which is shorter than its diff:
```python
import jax
import jax.numpy as jnp
from jax import lax
from jax.sharding import Mesh, PartitionSpec as P

BATCH = ("h", "z", "k")
CHAN = ("x", "l")
SIZES = {"h": 2, "z": 8, "k": 2, "x": 4, "l": 2}
AXES = BATCH + CHAN
F32 = jnp.float32
BF16 = jnp.bfloat16


def count(axes):
    total = 1
    for axis in axes:
        total *= SIZES[axis]
    return total


def gather_copies(block, axes):
    copies = jnp.broadcast_to(block[None], (count(axes),) + block.shape)
    return lax.all_to_all(copies, axes, 0, 0, tiled=True)


def swap(block, axis):
    return lax.ppermute(block, axis, [(0, 1), (1, 0)])


def shift(block, axis, distance):
    n = SIZES[axis]
    return lax.ppermute(block, axis, [(i, (i + distance) % n) for i in range(n)])


def take(block, index):
    return lax.dynamic_index_in_dim(block, index, keepdims=False)


def add(a, b):
    return (a.astype(F32) + b.astype(F32)).astype(BF16)


def ring_sums(parts, axis):
    n = SIZES[axis]
    here = lax.axis_index(axis)
    up = [None] * len(parts)
    down = [None] * len(parts)
    for away in range(n // 2, 0, -1):
        for i, part in enumerate(parts):
            term = take(part, (here + away) % n)
            up[i] = shift(term if up[i] is None else add(term, up[i]), axis, 1)
            if away < n // 2:
                term = take(part, (here - away) % n)
                down[i] = shift(term if down[i] is None else add(term, down[i]), axis, -1)
    return [
        (take(part, here).astype(F32) + u.astype(F32) + d.astype(F32)).astype(BF16)
        for part, u, d in zip(parts, up, down)
    ]


def local(
    token_ids,
    embed_table,
    norm_gain,
    in_weight,
    filter_weight,
    filter_bias,
    select_weight,
    step_gain,
    step_weight,
    step_bias,
    decay_log,
    skip_gain,
    out_weight,
    filter_state,
    scan_state,
):
    steps, reqs = token_ids.shape
    vocab_rows, width = embed_table.shape
    feats, _, channels = in_weight.shape
    half = channels // 2
    rank_size = step_gain.shape[0]
    state_size = decay_log.shape[0]
    rows = steps * reqs
    nb, nc = count(BATCH), count(CHAN)
    tokens = nb * rows
    core = lax.axis_index("k")
    me = lax.axis_index(BATCH)
    features = norm_gain.shape[0]

    step_full = lax.all_gather(step_weight, BATCH, axis=0, tiled=True)
    in_flat = in_weight.reshape(feats, 2 * channels)

    ids = gather_copies(token_ids.reshape(rows), BATCH).reshape(nb // 2, 2, rows)
    ids = ids.transpose(1, 0, 2).reshape(tokens)
    ids, in_flat = lax.optimization_barrier((ids, in_flat))
    vocab_index = me * vocab_rows + lax.broadcasted_iota(jnp.int32, (tokens, vocab_rows), 1)
    hot = (vocab_index == ids[:, None]).astype(BF16)
    picked = jnp.dot(hot, embed_table, preferred_element_type=F32).astype(BF16)
    picked = picked.reshape(2, nb // 2, rows, width)
    picked = add(take(picked, core), swap(take(picked, 1 - core), "k"))
    picked = lax.all_to_all(picked, ("h", "z"), 0, 0, tiled=True)
    own = jnp.sum(picked.astype(F32), axis=0).astype(BF16)
    embedded = gather_copies(own, CHAN).transpose(1, 0, 2).reshape(rows, features)
    embed_wide = embedded.astype(F32)
    mean_square = jnp.mean(embed_wide * embed_wide, axis=-1, keepdims=True)
    normed = (embed_wide * lax.rsqrt(mean_square + 1e-06) * norm_gain).astype(BF16)
    spread = normed.reshape(rows, nb, feats).transpose(1, 0, 2)
    x = lax.all_to_all(spread, BATCH, 0, 0, tiled=True).reshape(tokens, feats)
    x, step_full = lax.optimization_barrier((x, step_full))

    side = lax.axis_index("h")

    def project(which, part_of):
        w = lax.dynamic_slice_in_dim(in_flat, which * channels + part_of * half, half, axis=1)
        part = jnp.dot(x, w, preferred_element_type=F32).astype(BF16)
        return part.reshape(2, 8, 2 * rows, half)

    theirs = [swap(project(which, 1 - core), "k") for which in range(2)]
    parts = [add(project(which, core), theirs[which]) for which in range(2)]
    sums = ring_sums([part.transpose(1, 0, 2, 3) for part in parts], "z")
    sums = [add(take(one, side), swap(take(one, 1 - side), "h")) for one in sums]
    both = jnp.stack(sums).reshape(2, 2, rows, half)
    mine = lax.dynamic_index_in_dim(both, core, axis=1, keepdims=False)
    other = swap(lax.dynamic_index_in_dim(both, 1 - core, axis=1, keepdims=False), "k")
    first = jnp.where(core == 0, mine, other)
    last = jnp.where(core == 0, other, mine)
    stream = jnp.concatenate([first[0], last[0]], axis=1).astype(F32)
    gate = jnp.concatenate([first[1], last[1]], axis=1).astype(F32)

    stream = stream.reshape(steps, reqs, channels)
    window = jnp.concatenate([filter_state.transpose(1, 0, 2), stream], axis=0)
    taps = filter_weight.shape[0]
    mixed_in = sum(window[i : i + steps] * filter_weight[i] for i in range(taps))
    convolved = jax.nn.silu(mixed_in + filter_bias)
    filter_out = window[steps:].transpose(1, 0, 2)
    conv_rows = convolved.reshape(rows, channels)
    part = jnp.dot(conv_rows.astype(BF16), select_weight, preferred_element_type=F32)
    selected = jnp.sum(gather_copies(part, CHAN), axis=0)
    rank = selected[:, :rank_size]
    bvec = selected[:, rank_size : rank_size + state_size].reshape(steps, reqs, state_size)
    cvec = selected[:, rank_size + state_size :].reshape(steps, reqs, state_size)
    mean_square = jnp.mean(rank * rank, axis=-1, keepdims=True)
    rank_normed = (rank * lax.rsqrt(mean_square + 1e-06) * step_gain).astype(BF16)
    delta = jax.nn.softplus(
        jnp.dot(rank_normed, step_full, preferred_element_type=F32) + step_bias
    ).reshape(steps, reqs, channels)

    decay_rate = -jnp.exp(decay_log)
    scan_now = scan_state
    readouts = []
    for t in range(steps):
        factor = jnp.exp(delta[t][:, None, :] * decay_rate[None])
        scan_now = factor * scan_now + (delta[t] * convolved[t])[:, None, :] * bvec[t][:, :, None]
        readouts.append(jnp.sum(scan_now * cvec[t][:, :, None], axis=1) + skip_gain * convolved[t])
    readout = jnp.stack(readouts).reshape(rows, channels)
    gated = (readout * jax.nn.silu(gate)).astype(BF16)

    every = lax.all_gather(gated, "z")
    every = jnp.stack([every, swap(every, "h")])
    every = jnp.stack([every, swap(every, "k")])
    part_out = jnp.dot(
        every.reshape(tokens, channels), out_weight, preferred_element_type=F32
    ).astype(BF16)
    per = rows // nc
    sent = part_out.reshape(nb, nc, per, feats).transpose(1, 0, 2, 3)
    got = lax.all_to_all(sent, CHAN, 0, 0, tiled=True)
    mixed = jnp.sum(got.astype(F32), axis=0).astype(BF16)

    dest = lax.broadcasted_iota(jnp.int32, (nb, 1), 0)
    source = lax.broadcasted_iota(jnp.int32, (1, nb), 1)
    s_k, s_h, s_z = source // 16, (source // 8) % 2, source % 8
    place = ((s_h + side) % 2) * 16 + s_z * 2 + (s_k + core) % 2
    order = (dest == place).astype(BF16)
    mixed = jnp.dot(order, mixed.reshape(nb, per * feats), preferred_element_type=F32)
    mixed = mixed.astype(BF16).reshape(nb, 1, per, feats)
    copies = jnp.broadcast_to(mixed, (nb, nc, per, feats)).reshape(nb * nc, per, feats)
    home = lax.all_to_all(copies, AXES, 0, 0, tiled=True).reshape(nb, nc * per, feats)
    home = home.transpose(1, 0, 2).reshape(rows, features)
    hidden = (embed_wide + home.astype(F32)).astype(BF16).reshape(steps, reqs, features)
    return (hidden, filter_out, scan_now)


def solution(mesh):
    fine = Mesh(mesh.devices.reshape([SIZES[axis] for axis in AXES]), AXES)
    return jax.shard_map(
        local,
        mesh=fine,
        in_specs=(
            P(None, BATCH),
            P(BATCH, CHAN),
            P(),
            P(BATCH, None, CHAN),
            P(None, CHAN),
            P(CHAN),
            P(CHAN, None),
            P(),
            P(BATCH, CHAN),
            P(CHAN),
            P(None, CHAN),
            P(CHAN),
            P(CHAN, BATCH),
            P(BATCH, None, CHAN),
            P(BATCH, None, CHAN),
        ),
        out_specs=(P(None, BATCH, None), P(BATCH, None, CHAN), P(BATCH, None, CHAN)),
        check_vma=False,
    )
```

time: 300 us -> 273 us (0.910)
  waiting for transfers between devices: 127 us -> 104 us
  blocking collectives: 33.5 us -> 48.7 us
  local copies, waits for them, and re-layouts: 27.2 us -> 17.3 us
  starting transfers between devices: 67.8 us -> 59.5 us
    all_to_all x3 -> x2, waiting for transfers between devices: 66.3 us -> 29.1 us  [the longest x1 16.1 us: local(): x = lax.all_to_all(spread, BATCH, 0, 0, tiled=True).reshape(tokens, feats)]
    all_gather x0 -> x1, blocking collectives: none -> 25.6 us  [local(): every = lax.all_gather(gated, 'z')]
    ppermute x3 -> x8, waiting for transfers between devices: 7.02 us -> 18.2 us  [swap(): return lax.ppermute(block, axis, [(0, 1), (1, 0)])]
    all_to_all x1, blocking collectives: 33.5 us -> 23.1 us  [local(): picked = lax.all_to_all(picked, ('h', 'z'), 0, 0, tiled=True)]
    all_to_all x4 -> x3, starting transfers between devices: 31.2 us -> 22.7 us  [gather_copies(): return lax.all_to_all(copies, axes, 0, 0, tiled=True)]
    dynamic_slice x4 -> x0, local copies, waits for them, and re-layouts: 8.3 us -> none  [the longest x2 5.25 us: local(): lax.dynamic_index_in_dim(halves, 1 - core, axis=2, keepdims=False)]
    ppermute x3 -> x8, starting transfers between devices: 0.94 us -> 6.75 us  [swap(): return lax.ppermute(block, axis, [(0, 1), (1, 0)])]
    convert_element_type x3 -> x18, other arithmetic: 0.26 us -> 5.89 us  [the longest x13 4.87 us: add(): return (a.astype(F32) + b.astype(F32)).astype(BF16)]
  transfers between devices with their start and end apart: 20 -> 29, of which waited for: 15 -> 22; matrix products, arithmetic and copies ran while one was open for 10% -> 9% of each run, Pallas kernels for 0% -> 0%
where the time goes in v2:
time: 273 us; the launch traced here: 271 us
  waiting for transfers between devices  104 us (38%)
  starting transfers between devices  59.5 us (22%)
  blocking collectives  48.7 us (18%)
  local copies, waits for them, and re-layouts  17.3 us (6%)
  matrix products  16 us (6%)
  between operations  14.7 us (5%)
  other arithmetic  10.9 us (4%)
    all_gather x1, blocking collectives, local(): every = lax.all_gather(gated, 'z')  25.6 us
    all_to_all x1, blocking collectives, local(): picked = lax.all_to_all(picked, ('h', 'z'), 0, 0, tiled=True)  23.1 us
    all_to_all x3, starting transfers between devices, gather_copies(): return lax.all_to_all(copies, axes, 0, 0, tiled=True)  22.7 us
    ppermute x14, waiting for transfers between devices, shift(): lax.ppermute(block, axis, [(i, (i + distance) % n) for i in range(n)])  21.2 us
    ppermute x8, waiting for transfers between devices, swap(): return lax.ppermute(block, axis, [(0, 1), (1, 0)])  18.2 us
    all_to_all x3, waiting for transfers between devices, gather_copies(): return lax.all_to_all(copies, axes, 0, 0, tiled=True)  17.8 us
    all_to_all x1, waiting for transfers between devices, local(): x = lax.all_to_all(spread, BATCH, 0, 0, tiled=True).reshape(tokens, feats)  16.1 us
    all_to_all x1, waiting for transfers between devices, local(): lax.all_to_all(copies, AXES, 0, 0, tiled=True).reshape(nb, nc * per, feats)  13 us
  transfers between devices with their start and end apart: 29, of which 22 were waited for; matrix products, arithmetic and copies ran while one was open for 9% of the time, Pallas kernels for 0%

profile of v2, /device:TPU:8, one launch (start us, length us, event | category | flops | bytes accessed | tf_op | source)
XLA Modules:
  0.0 270.9 jit_solution(17820237136588137286)
XLA Ops:
  8.7 10.6 %all-to-all-start = ((s32[32,1,16]{2,1,0:T(1,128)}), s32[32,1,16]{2,1,0:T(1,128)S(1)}, u32[]{:S(2)}, u32[]{:S(2)}) async-start(s32[32,1,16]{2,1,0:T(1,128)} %broadcast_in_dim.13), calls=%async_computation | async-start | bytes 32768 | tf_op jit(solution)/shard_map/all_to_all | solution.py:23
  20.1 3.8 %copy.97 = bf16[32,8,2,2048]{3,1,2,0:T(8,128)(2,1)} copy(bf16[32,8,2,2048]{3,2,1,0:T(2,128)(2,1)} %bitcast.170) | data formatting | bytes 4194304
  23.9 5.2 %all-to-all-done = s32[32,1,16]{2,1,0:T(1,128)S(1)} async-done(((s32[32,1,16]{2,1,0:T(1,128)}), s32[32,1,16]{2,1,0:T(1,128)S(1)}, u32[]{:S(2)}, u32[]{:S(2)}) %all-to-all-start) | async-done | bytes 2080 | tf_op jit(solution)/shard_map/all_to_all | solution.py:23
  29.2 4.6 %fusion.6 = bf16[512,1024]{1,0:T(8,128)(2,1)S(1)} fusion(bf16[2048,1024]{1,0:T(8,128)(2,1)} %param.16, s32[2048]{0:T(1024)S(1)} %iota_add_fusion, s32[512]{0:T(512)S(1)} %reshape.477), kind=kOutput, calls=%fused_computation.10 | convolution fusion | flops 2149056512 | bytes 5253120 | tf_op jit(solution)/shard_map/dot_general | solution.py:99
  38.1 23.1 %all_to_all.36 = bf16[16,16,1024]{2,1,0:T(8,128)(2,1)S(1)} all-to-all(bf16[16,16,1024]{2,1,0:T(8,128)(2,1)S(1)} %fusion.9), channel_id=1, replica_groups=mesh['h'=2,'z'=8,'k'=2,'x'=4,'l'=2] {'h','z'}, dimensions={0} | all-to-all | bytes 1048576 | tf_op jit(solution)/shard_map/all_to_all | solution.py:102
  62.1 5.6 %all-to-all-start.2 = ((bf16[8,16,1024]{2,1,0:T(8,128)(2,1)}), bf16[8,16,1024]{2,1,0:T(8,128)(2,1)S(1)}, u32[]{:S(2)}, u32[]{:S(2)}) async-start(bf16[8,16,1024]{2,1,0:T(8,128)(2,1)} %broadcast_in_dim.14), calls=%async_computation.2 | async-start | bytes 524288 | tf_op jit(solution)/shard_map/all_to_all | solution.py:23
  68.3 5.5 %all-to-all-done.2 = bf16[8,16,1024]{2,1,0:T(8,128)(2,1)S(1)} async-done(((bf16[8,16,1024]{2,1,0:T(8,128)(2,1)}), bf16[8,16,1024]{2,1,0:T(8,128)(2,1)S(1)}, u32[]{:S(2)}, u32[]{:S(2)}) %all-to-all-start.2) | async-done | bytes 262176 | tf_op jit(solution)/shard_map/all_to_all | solution.py:23
  76.3 4.9 %all-to-all-start.3 = ((bf16[32,16,256]{2,1,0:T(8,128)(2,1)}), bf16[32,16,256]{2,1,0:T(8,128)(2,1)S(1)}, u32[]{:S(2)}, u32[]{:S(2)}) async-start(bf16[32,16,256]{2,1,0:T(8,128)(2,1)} %copy.72), calls=%async_computation.3 | async-start | bytes 524288 | tf_op jit(solution)/shard_map/all_to_all | solution.py:109
  81.2 16.1 %all-to-all-done.3 = bf16[32,16,256]{2,1,0:T(8,128)(2,1)S(1)} async-done(((bf16[32,16,256]{2,1,0:T(8,128)(2,1)}), bf16[32,16,256]{2,1,0:T(8,128)(2,1)S(1)}, u32[]{:S(2)}, u32[]{:S(2)}) %all-to-all-start.3) | async-done | bytes 262176 | tf_op jit(solution)/shard_map/all_to_all | solution.py:109
  97.3 9.9 %all-gather.2.cloned.1.call-done = bf16[512,2048]{1,0:T(8,128)(2,1)} async-done(((bf16[16,2048]{1,0:T(8,128)(2,1)}), bf16[512,2048]{1,0:T(8,128)(2,1)}) %all-gather.2.cloned.1.call-update) | async-done | bytes 2097168 | tf_op jit(solution)/shard_map/all_gather | solution.py:91
  122.6 3.2 %collective-permute-start.6 = (bf16[2,32,1024]{2,1,0:T(8,128)(2,1)S(1)}, bf16[2,32,1024]{2,1,0:T(8,128)(2,1)S(1)}, u32[]{:S(2)}, u32[]{:S(2)}) collective-permute-start(bf16[2,32,1024]{2,1,0:T(8,128)(2,1)S(1)} %get-tuple-element.27), channel_id=1, source_target_pairs={{0,112},{16,0},{32,16},{48,32},{64,48},{80,64},{96,80},{112,96},{1... | collective-permute-start | bytes 393224 | tf_op jit(solution)/shard_map/ppermute | solution.py:32
  126.0 2.9 %collective-permute-done.2 = bf16[2,32,1024]{2,1,0:T(8,128)(2,1)S(1)} collective-permute-done((bf16[2,32,1024]{2,1,0:T(8,128)(2,1)S(1)}, bf16[2,32,1024]{2,1,0:T(8,128)(2,1)S(1)}, u32[]{:S(2)}, u32[]{:S(2)}) %collective-permute-start.2) | collective-permute-done | bytes 131104 | tf_op jit(solution)/shard_map/ppermute | solution.py:32
  129.1 3.6 %collective-permute-done.12 = bf16[2,32,1024]{2,1,0:T(8,128)(2,1)S(1)} collective-permute-done((bf16[2,32,1024]{2,1,0:T(8,128)(2,1)S(1)}, bf16[2,32,1024]{2,1,0:T(8,128)(2,1)S(1)}, u32[]{:S(2)}, u32[]{:S(2)}) %collective-permute-start.12) | collective-permute-done | bytes 131104 | tf_op jit(solution)/shard_map/ppermute | solution.py:32
  132.8 3.6 %collective-permute-done.3 = bf16[2,32,1024]{2,1,0:T(8,128)(2,1)S(1)} collective-permute-done((bf16[2,32,1024]{2,1,0:T(8,128)(2,1)S(1)}, bf16[2,32,1024]{2,1,0:T(8,128)(2,1)S(1)}, u32[]{:S(2)}, u32[]{:S(2)}) %collective-permute-start.3) | collective-permute-done | bytes 131104 | tf_op jit(solution)/shard_map/ppermute | solution.py:32
  136.5 3.6 %collective-permute-done.13 = bf16[2,32,1024]{2,1,0:T(8,128)(2,1)S(1)} collective-permute-done((bf16[2,32,1024]{2,1,0:T(8,128)(2,1)S(1)}, bf16[2,32,1024]{2,1,0:T(8,128)(2,1)S(1)}, u32[]{:S(2)}, u32[]{:S(2)}) %collective-permute-start.13) | collective-permute-done | bytes 131104 | tf_op jit(solution)/shard_map/ppermute | solution.py:32
  157.7 3.1 %collective-permute-done.9 = bf16[32,1024]{1,0:T(8,128)(2,1)S(1)} collective-permute-done((bf16[32,1024]{1,0:T(8,128)(2,1)S(1)}, bf16[32,1024]{1,0:T(8,128)(2,1)S(1)}, u32[]{:S(2)}, u32[]{:S(2)}) %collective-permute-start.9) | collective-permute-done | bytes 65568 | tf_op jit(solution)/shard_map/ppermute | solution.py:27
  164.6 6.5 %all-to-all-start.4 = ((f32[8,16,544]{2,1,0:T(8,128)}), f32[8,16,544]{2,1,0:T(8,128)S(1)}, u32[]{:S(2)}, u32[]{:S(2)}) async-start(f32[8,16,544]{2,1,0:T(8,128)} %broadcast_in_dim.15), calls=%async_computation.4 | async-start | bytes 655360 | tf_op jit(solution)/shard_map/all_to_all | solution.py:23
  171.1 7.1 %all-to-all-done.4 = f32[8,16,544]{2,1,0:T(8,128)S(1)} async-done(((f32[8,16,544]{2,1,0:T(8,128)}), f32[8,16,544]{2,1,0:T(8,128)S(1)}, u32[]{:S(2)}, u32[]{:S(2)}) %all-to-all-start.4) | async-done | bytes 278560 | tf_op jit(solution)/shard_map/all_to_all | solution.py:23
  182.8 25.6 %all_gather.8 = bf16[8,16,2048]{2,1,0:T(8,128)(2,1)S(1)} all-gather(bf16[1,16,2048]{2,1,0:T(8,128)(2,1)S(1)} %fusion.45), channel_id=1, replica_groups=mesh['h'=2,'z'=8,'k'=2,'x'=4,'l'=2] {'z'}, dimensions={0}, use_global_device_ids=true | all-gather | bytes 589824 | tf_op jit(solution)/shard_map/all_gather | solution.py:159
  210.5 8.5 %collective-permute-done.20 = bf16[8,16,2048]{2,1,0:T(8,128)(2,1)S(1)} collective-permute-done((bf16[8,16,2048]{2,1,0:T(8,128)(2,1)S(1)}, bf16[8,16,2048]{2,1,0:T(8,128)(2,1)S(1)}, u32[]{:S(2)}, u32[]{:S(2)}) %collective-permute-start.20) | collective-permute-done | bytes 524320 | tf_op jit(solution)/shard_map/ppermute | solution.py:27
  224.9 4.0 %all-to-all-start.5 = ((bf16[8,32,2,256]{3,2,1,0:T(2,128)(2,1)}), bf16[8,32,2,256]{3,2,1,0:T(2,128)(2,1)S(1)}, u32[]{:S(2)}, u32[]{:S(2)}) async-start(bf16[8,32,2,256]{3,2,1,0:T(2,128)(2,1)} %bitcast.159), calls=%async_computation.5 | async-start | bytes 524288 | tf_op jit(solution)/shard_map/all_to_all | solution.py:167
  229.0 6.7 %all-to-all-done.5 = bf16[8,32,2,256]{3,2,1,0:T(2,128)(2,1)S(1)} async-done(((bf16[8,32,2,256]{3,2,1,0:T(2,128)(2,1)}), bf16[8,32,2,256]{3,2,1,0:T(2,128)(2,1)S(1)}, u32[]{:S(2)}, u32[]{:S(2)}) %all-to-all-start.5) | async-done | bytes 262176 | tf_op jit(solution)/shard_map/all_to_all | solution.py:167
  236.9 8.9 %all-to-all-start.6 = ((bf16[256,2,256]{2,1,0:T(2,128)(2,1)}), bf16[256,2,256]{2,1,0:T(2,128)(2,1)S(1)}, u32[]{:S(2)}, u32[]{:S(2)}) async-start(bf16[256,2,256]{2,1,0:T(2,128)(2,1)} %bitcast.57), calls=%async_computation.6 | async-start | bytes 524288 | tf_op jit(solution)/shard_map/all_to_all | solution.py:178
  247.7 13.0 %all-to-all-done.6 = bf16[256,2,256]{2,1,0:T(2,128)(2,1)S(1)} async-done(((bf16[256,2,256]{2,1,0:T(2,128)(2,1)}), bf16[256,2,256]{2,1,0:T(2,128)(2,1)S(1)}, u32[]{:S(2)}, u32[]{:S(2)}) %all-to-all-start.6) | async-done | bytes 262176 | tf_op jit(solution)/shard_map/all_to_all | solution.py:178
  (143 shorter events, 66.4 us)
Async XLA Ops:
  8.7 20.4 %all-to-all-start = ((s32[32,1,16]{2,1,0:T(1,128)}), s32[32,1,16]{2,1,0:T(1,128)S(1)}, u32[]{:S(2)}, u32[]{:S(2)}) async-start(s32[32,1,16]{2,1,0:T(1,128)} %broadcast_in_dim.13), calls=%async_computation | async-start | bytes 32768 | tf_op jit(solution)/shard_map/all_to_all | solution.py:23
  19.3 88.0 %all-gather.2.cloned.1.call-start = ((), (), s32[]{:S(2)}) async-start(), calls=%async_computation.7 | async-start | bytes 2162688 | tf_op jit(solution)/shard_map/all_gather | solution.py:91
  62.1 11.8 %all-to-all-start.2 = ((bf16[8,16,1024]{2,1,0:T(8,128)(2,1)}), bf16[8,16,1024]{2,1,0:T(8,128)(2,1)S(1)}, u32[]{:S(2)}, u32[]{:S(2)}) async-start(bf16[8,16,1024]{2,1,0:T(8,128)(2,1)} %broadcast_in_dim.14), calls=%async_computation.2 | async-start | bytes 524288 | tf_op jit(solution)/shard_map/all_to_all | solution.py:23
  76.3 21.0 %all-to-all-start.3 = ((bf16[32,16,256]{2,1,0:T(8,128)(2,1)}), bf16[32,16,256]{2,1,0:T(8,128)(2,1)S(1)}, u32[]{:S(2)}, u32[]{:S(2)}) async-start(bf16[32,16,256]{2,1,0:T(8,128)(2,1)} %copy.72), calls=%async_computation.3 | async-start | bytes 524288 | tf_op jit(solution)/shard_map/all_to_all | solution.py:109
  109.7 6.0 %collective-permute-start.10 = (bf16[2,8,32,1024]{3,2,1,0:T(8,128)(2,1)}, bf16[2,8,32,1024]{3,2,1,0:T(8,128)(2,1)}, u32[]{:S(2)}, u32[]{:S(2)}) collective-permute-start(bf16[2,8,32,1024]{3,2,1,0:T(8,128)(2,1)} %bitcast.24), channel_id=1, source_target_pairs={{0,8},{8,0},{1,9},{9,1},{2,10},{10,2},{3,11},{11,3},{4,12},{12,4},... | collective-permute-start | bytes 3145736 | tf_op jit(solution)/shard_map/ppermute | solution.py:27
  112.5 8.2 %collective-permute-start.1 = (bf16[2,8,32,1024]{3,2,1,0:T(8,128)(2,1)}, bf16[2,8,32,1024]{3,2,1,0:T(8,128)(2,1)}, u32[]{:S(2)}, u32[]{:S(2)}) collective-permute-start(bf16[2,8,32,1024]{3,2,1,0:T(8,128)(2,1)} %bitcast.10), channel_id=1, source_target_pairs={{0,8},{8,0},{1,9},{9,1},{2,10},{10,2},{3,11},{11,3},{4,12},{12,4},... | collective-permute-start | bytes 3145736 | tf_op jit(solution)/shard_map/ppermute | solution.py:27
  117.4 8.5 %collective-permute-start.11 = (bf16[2,32,1024]{2,1,0:T(8,128)(2,1)S(1)}, bf16[2,32,1024]{2,1,0:T(8,128)(2,1)S(1)}, u32[]{:S(2)}, u32[]{:S(2)}) collective-permute-start(bf16[2,32,1024]{2,1,0:T(8,128)(2,1)S(1)} %get-tuple-element.22), channel_id=1, source_target_pairs={{0,16},{16,32},{32,48},{48,64},{64,80},{80,96},{96,112},{112,0},{1... | collective-permute-start | bytes 393224 | tf_op jit(solution)/shard_map/ppermute | solution.py:32
  118.5 18.1 %collective-permute-start.15 = (bf16[2,32,1024]{2,1,0:T(8,128)(2,1)S(1)}, bf16[2,32,1024]{2,1,0:T(8,128)(2,1)S(1)}, u32[]{:S(2)}, u32[]{:S(2)}) collective-permute-start(bf16[2,32,1024]{2,1,0:T(8,128)(2,1)S(1)} %get-tuple-element.23), channel_id=1, source_target_pairs={{0,112},{16,0},{32,16},{48,32},{64,48},{80,64},{96,80},{112,96},{1... | collective-permute-start | bytes 393224 | tf_op jit(solution)/shard_map/ppermute | solution.py:32
  122.4 6.6 %collective-permute-start.2 = (bf16[2,32,1024]{2,1,0:T(8,128)(2,1)S(1)}, bf16[2,32,1024]{2,1,0:T(8,128)(2,1)S(1)}, u32[]{:S(2)}, u32[]{:S(2)}) collective-permute-start(bf16[2,32,1024]{2,1,0:T(8,128)(2,1)S(1)} %get-tuple-element.26), channel_id=1, source_target_pairs={{0,16},{16,32},{32,48},{48,64},{64,80},{80,96},{96,112},{112,0},{1... | collective-permute-start | bytes 393224 | tf_op jit(solution)/shard_map/ppermute | solution.py:32
  122.6 19.7 %collective-permute-start.6 = (bf16[2,32,1024]{2,1,0:T(8,128)(2,1)S(1)}, bf16[2,32,1024]{2,1,0:T(8,128)(2,1)S(1)}, u32[]{:S(2)}, u32[]{:S(2)}) collective-permute-start(bf16[2,32,1024]{2,1,0:T(8,128)(2,1)S(1)} %get-tuple-element.27), channel_id=1, source_target_pairs={{0,112},{16,0},{32,16},{48,32},{64,48},{80,64},{96,80},{112,96},{1... | collective-permute-start | bytes 393224 | tf_op jit(solution)/shard_map/ppermute | solution.py:32
  125.9 6.8 %collective-permute-start.12 = (bf16[2,32,1024]{2,1,0:T(8,128)(2,1)S(1)}, bf16[2,32,1024]{2,1,0:T(8,128)(2,1)S(1)}, u32[]{:S(2)}, u32[]{:S(2)}) collective-permute-start(bf16[2,32,1024]{2,1,0:T(8,128)(2,1)S(1)} %fusion.18), channel_id=1, source_target_pairs={{0,16},{16,32},{32,48},{48,64},{64,80},{80,96},{96,112},{112,0},{1... | collective-permute-start | bytes 393224 | tf_op jit(solution)/shard_map/ppermute | solution.py:32
  129.0 7.4 %collective-permute-start.3 = (bf16[2,32,1024]{2,1,0:T(8,128)(2,1)S(1)}, bf16[2,32,1024]{2,1,0:T(8,128)(2,1)S(1)}, u32[]{:S(2)}, u32[]{:S(2)}) collective-permute-start(bf16[2,32,1024]{2,1,0:T(8,128)(2,1)S(1)} %fusion.25), channel_id=1, source_target_pairs={{0,16},{16,32},{32,48},{48,64},{64,80},{80,96},{96,112},{112,0},{1... | collective-permute-start | bytes 393224 | tf_op jit(solution)/shard_map/ppermute | solution.py:32
  132.7 7.4 %collective-permute-start.13 = (bf16[2,32,1024]{2,1,0:T(8,128)(2,1)S(1)}, bf16[2,32,1024]{2,1,0:T(8,128)(2,1)S(1)}, u32[]{:S(2)}, u32[]{:S(2)}) collective-permute-start(bf16[2,32,1024]{2,1,0:T(8,128)(2,1)S(1)} %fusion.19), channel_id=1, source_target_pairs={{0,16},{16,32},{32,48},{48,64},{64,80},{80,96},{96,112},{112,0},{1... | collective-permute-start | bytes 393224 | tf_op jit(solution)/shard_map/ppermute | solution.py:32
  136.4 6.9 %collective-permute-start.4 = (bf16[2,32,1024]{2,1,0:T(8,128)(2,1)S(1)}, bf16[2,32,1024]{2,1,0:T(8,128)(2,1)S(1)}, u32[]{:S(2)}, u32[]{:S(2)}) collective-permute-start(bf16[2,32,1024]{2,1,0:T(8,128)(2,1)S(1)} %fusion.26), channel_id=1, source_target_pairs={{0,16},{16,32},{32,48},{48,64},{64,80},{80,96},{96,112},{112,0},{1... | collective-permute-start | bytes 393224 | tf_op jit(solution)/shard_map/ppermute | solution.py:32
  140.2 6.5 %collective-permute-start.16 = (bf16[2,32,1024]{2,1,0:T(8,128)(2,1)S(1)}, bf16[2,32,1024]{2,1,0:T(8,128)(2,1)S(1)}, u32[]{:S(2)}, u32[]{:S(2)}) collective-permute-start(bf16[2,32,1024]{2,1,0:T(8,128)(2,1)S(1)} %get-tuple-element.21), channel_id=1, source_target_pairs={{0,112},{16,0},{32,16},{48,32},{64,48},{80,64},{96,80},{112,96},{1... | collective-permute-start | bytes 393224 | tf_op jit(solution)/shard_map/ppermute | solution.py:32
  140.3 9.8 %collective-permute-start.14 = (bf16[2,32,1024]{2,1,0:T(8,128)(2,1)S(1)}, bf16[2,32,1024]{2,1,0:T(8,128)(2,1)S(1)}, u32[]{:S(2)}, u32[]{:S(2)}) collective-permute-start(bf16[2,32,1024]{2,1,0:T(8,128)(2,1)S(1)} %get-tuple-element.20), channel_id=1, source_target_pairs={{0,16},{16,32},{32,48},{48,64},{64,80},{80,96},{96,112},{112,0},{1... | collective-permute-start | bytes 393224 | tf_op jit(solution)/shard_map/ppermute | solution.py:32
  143.5 6.3 %collective-permute-start.7 = (bf16[2,32,1024]{2,1,0:T(8,128)(2,1)S(1)}, bf16[2,32,1024]{2,1,0:T(8,128)(2,1)S(1)}, u32[]{:S(2)}, u32[]{:S(2)}) collective-permute-start(bf16[2,32,1024]{2,1,0:T(8,128)(2,1)S(1)} %get-tuple-element.25), channel_id=1, source_target_pairs={{0,112},{16,0},{32,16},{48,32},{64,48},{80,64},{96,80},{112,96},{1... | collective-permute-start | bytes 393224 | tf_op jit(solution)/shard_map/ppermute | solution.py:32
  143.8 9.9 %collective-permute-start.5 = (bf16[2,32,1024]{2,1,0:T(8,128)(2,1)S(1)}, bf16[2,32,1024]{2,1,0:T(8,128)(2,1)S(1)}, u32[]{:S(2)}, u32[]{:S(2)}) collective-permute-start(bf16[2,32,1024]{2,1,0:T(8,128)(2,1)S(1)} %get-tuple-element.24), channel_id=1, source_target_pairs={{0,16},{16,32},{32,48},{48,64},{64,80},{80,96},{96,112},{112,0},{1... | collective-permute-start | bytes 393224 | tf_op jit(solution)/shard_map/ppermute | solution.py:32
  151.8 5.9 %collective-permute-start.18 = (bf16[32,1024]{1,0:T(8,128)(2,1)S(1)}, bf16[32,1024]{1,0:T(8,128)(2,1)S(1)}, u32[]{:S(2)}, u32[]{:S(2)}) collective-permute-start(bf16[32,1024]{1,0:T(8,128)(2,1)S(1)} %dynamic-slice_bitcast_fusion.5), channel_id=1, source_target_pairs={{0,128},{128,0},{1,129},{129,1},{2,130},{130,2},{3,131},{131,3},{4... | collective-permute-start | bytes 196616 | tf_op jit(solution)/shard_map/ppermute | solution.py:27
  154.9 5.9 %collective-permute-start.9 = (bf16[32,1024]{1,0:T(8,128)(2,1)S(1)}, bf16[32,1024]{1,0:T(8,128)(2,1)S(1)}, u32[]{:S(2)}, u32[]{:S(2)}) collective-permute-start(bf16[32,1024]{1,0:T(8,128)(2,1)S(1)} %dynamic-slice_bitcast_fusion.6), channel_id=1, source_target_pairs={{0,128},{128,0},{1,129},{129,1},{2,130},{130,2},{3,131},{131,3},{4... | collective-permute-start | bytes 196616 | tf_op jit(solution)/shard_map/ppermute | solution.py:27
  164.6 13.6 %all-to-all-start.4 = ((f32[8,16,544]{2,1,0:T(8,128)}), f32[8,16,544]{2,1,0:T(8,128)S(1)}, u32[]{:S(2)}, u32[]{:S(2)}) async-start(f32[8,16,544]{2,1,0:T(8,128)} %broadcast_in_dim.15), calls=%async_computation.4 | async-start | bytes 655360 | tf_op jit(solution)/shard_map/all_to_all | solution.py:23
  208.4 10.7 %collective-permute-start.20 = (bf16[8,16,2048]{2,1,0:T(8,128)(2,1)S(1)}, bf16[8,16,2048]{2,1,0:T(8,128)(2,1)S(1)}, u32[]{:S(2)}, u32[]{:S(2)}) collective-permute-start(bf16[8,16,2048]{2,1,0:T(8,128)(2,1)S(1)} %all_gather.8), channel_id=1, source_target_pairs={{0,128},{128,0},{1,129},{129,1},{2,130},{130,2},{3,131},{131,3},{4... | collective-permute-start | bytes 1572872 | tf_op jit(solution)/shard_map/ppermute | solution.py:27
  224.9 10.8 %all-to-all-start.5 = ((bf16[8,32,2,256]{3,2,1,0:T(2,128)(2,1)}), bf16[8,32,2,256]{3,2,1,0:T(2,128)(2,1)S(1)}, u32[]{:S(2)}, u32[]{:S(2)}) async-start(bf16[8,32,2,256]{3,2,1,0:T(2,128)(2,1)} %bitcast.159), calls=%async_computation.5 | async-start | bytes 524288 | tf_op jit(solution)/shard_map/all_to_all | solution.py:167
  236.9 23.8 %all-to-all-start.6 = ((bf16[256,2,256]{2,1,0:T(2,128)(2,1)}), bf16[256,2,256]{2,1,0:T(2,128)(2,1)S(1)}, u32[]{:S(2)}, u32[]{:S(2)}) async-start(bf16[256,2,256]{2,1,0:T(2,128)(2,1)} %bitcast.57), calls=%async_computation.6 | async-start | bytes 524288 | tf_op jit(solution)/shard_map/all_to_all | solution.py:178
  (17 other events, 322.4 us)
Sparse Core Ops, SparseCore 0:
  22.9 84.2 all-gather.1

commit v3 on v2

--- a/solution.py
+++ b/solution.py
@@ -30,6 +30,11 @@
 def shift(block, axis, distance):
     n = SIZES[axis]
     return lax.ppermute(block, axis, [(i, (i + distance) % n) for i in range(n)])
+
+
+def in_order(mine, other, index):
+    first = jnp.where(index == 0, mine, other)
+    return jnp.concatenate([first, jnp.where(index == 0, other, mine)])
 
 
 def take(block, index):
@@ -78,7 +83,6 @@
     steps, reqs = token_ids.shape
     vocab_rows, width = embed_table.shape
     feats, _, channels = in_weight.shape
-    half = channels // 2
     rank_size = step_gain.shape[0]
     state_size = decay_log.shape[0]
     rows = steps * reqs
@@ -88,12 +92,18 @@
     me = lax.axis_index(BATCH)
     features = norm_gain.shape[0]
 
-    step_full = lax.all_gather(step_weight, BATCH, axis=0, tiled=True)
+    side = lax.axis_index("h")
+    step_rows = in_order(step_weight, swap(step_weight, "k"), core)
+    step_rows = in_order(step_rows, swap(step_rows, "h"), side)
+    step_full = lax.all_gather(step_rows, "z", axis=0, tiled=True)
     in_flat = in_weight.reshape(feats, 2 * channels)
 
     ids = gather_copies(token_ids.reshape(rows), BATCH).reshape(nb // 2, 2, rows)
     ids = ids.transpose(1, 0, 2).reshape(tokens)
     ids, in_flat = lax.optimization_barrier((ids, in_flat))
+    in_other = swap(in_flat, "k")
+    out_pair = jnp.stack([out_weight, swap(out_weight, "k")])
+    out_far = swap(out_pair, "h")
     vocab_index = me * vocab_rows + lax.broadcasted_iota(jnp.int32, (tokens, vocab_rows), 1)
     hot = (vocab_index == ids[:, None]).astype(BF16)
     picked = jnp.dot(hot, embed_table, preferred_element_type=F32).astype(BF16)
@@ -105,28 +115,23 @@
     embed_wide = embedded.astype(F32)
     mean_square = jnp.mean(embed_wide * embed_wide, axis=-1, keepdims=True)
     normed = (embed_wide * lax.rsqrt(mean_square + 1e-06) * norm_gain).astype(BF16)
-    spread = normed.reshape(rows, nb, feats).transpose(1, 0, 2)
-    x = lax.all_to_all(spread, BATCH, 0, 0, tiled=True).reshape(tokens, feats)
-    x, step_full = lax.optimization_barrier((x, step_full))
-
-    side = lax.axis_index("h")
-
-    def project(which, part_of):
-        w = lax.dynamic_slice_in_dim(in_flat, which * channels + part_of * half, half, axis=1)
-        part = jnp.dot(x, w, preferred_element_type=F32).astype(BF16)
-        return part.reshape(2, 8, 2 * rows, half)
-
-    theirs = [swap(project(which, 1 - core), "k") for which in range(2)]
-    parts = [add(project(which, core), theirs[which]) for which in range(2)]
-    sums = ring_sums([part.transpose(1, 0, 2, 3) for part in parts], "z")
-    sums = [add(take(one, side), swap(take(one, 1 - side), "h")) for one in sums]
-    both = jnp.stack(sums).reshape(2, 2, rows, half)
-    mine = lax.dynamic_index_in_dim(both, core, axis=1, keepdims=False)
-    other = swap(lax.dynamic_index_in_dim(both, 1 - core, axis=1, keepdims=False), "k")
-    first = jnp.where(core == 0, mine, other)
-    last = jnp.where(core == 0, other, mine)
-    stream = jnp.concatenate([first[0], last[0]], axis=1).astype(F32)
-    gate = jnp.concatenate([first[1], last[1]], axis=1).astype(F32)
+    spread = normed.reshape(rows, nb // 2, 2 * feats).transpose(1, 0, 2)
+    x = lax.all_to_all(spread, ("h", "z"), 0, 0, tiled=True).reshape(tokens // 2, 2 * feats)
+    x_mine = lax.dynamic_slice_in_dim(x, core * feats, feats, axis=1)
+    x_other = lax.dynamic_slice_in_dim(x, (1 - core) * feats, feats, axis=1)
+
+
+    def project(which):
+        cols = slice(which * channels, (which + 1) * channels)
+        part = jnp.dot(x_mine, in_flat[:, cols], preferred_element_type=F32)
+        part += jnp.dot(x_other, in_other[:, cols], preferred_element_type=F32)
+        return part.astype(BF16).reshape(2, 8, rows, channels).transpose(1, 0, 2, 3)
+
+    first, step_full = lax.optimization_barrier((project(0), step_full))
+    sums = ring_sums([first, project(1)], "z")
+    stream, gate = [
+        add(take(one, side), swap(take(one, 1 - side), "h")).astype(F32) for one in sums
+    ]
 
     stream = stream.reshape(steps, reqs, channels)
     window = jnp.concatenate([filter_state.transpose(1, 0, 2), stream], axis=0)
@@ -142,6 +147,8 @@
     cvec = selected[:, rank_size + state_size :].reshape(steps, reqs, state_size)
     mean_square = jnp.mean(rank * rank, axis=-1, keepdims=True)
     rank_normed = (rank * lax.rsqrt(mean_square + 1e-06) * step_gain).astype(BF16)
+    rank_normed = rank_normed.reshape(rows, 2, 8, rank_size // 16)
+    rank_normed = rank_normed.transpose(0, 2, 1, 3).reshape(rows, rank_size)
     delta = jax.nn.softplus(
         jnp.dot(rank_normed, step_full, preferred_element_type=F32) + step_bias
     ).reshape(steps, reqs, channels)
@@ -156,27 +163,19 @@
     readout = jnp.stack(readouts).reshape(rows, channels)
     gated = (readout * jax.nn.silu(gate)).astype(BF16)
 
-    every = lax.all_gather(gated, "z")
-    every = jnp.stack([every, swap(every, "h")])
-    every = jnp.stack([every, swap(every, "k")])
-    part_out = jnp.dot(
-        every.reshape(tokens, channels), out_weight, preferred_element_type=F32
-    ).astype(BF16)
+    every = lax.all_gather(gated, "z").reshape(8 * rows, channels)
+    blocks = [out_pair[0], out_pair[1], out_far[0], out_far[1]]
+    part_out = [jnp.dot(every, w, preferred_element_type=F32).astype(BF16) for w in blocks]
     per = rows // nc
-    sent = part_out.reshape(nb, nc, per, feats).transpose(1, 0, 2, 3)
+    sent = jnp.concatenate(part_out, axis=1).reshape(8, nc, per, 4 * feats).transpose(1, 0, 2, 3)
     got = lax.all_to_all(sent, CHAN, 0, 0, tiled=True)
-    mixed = jnp.sum(got.astype(F32), axis=0).astype(BF16)
-
-    dest = lax.broadcasted_iota(jnp.int32, (nb, 1), 0)
-    source = lax.broadcasted_iota(jnp.int32, (1, nb), 1)
-    s_k, s_h, s_z = source // 16, (source // 8) % 2, source % 8
-    place = ((s_h + side) % 2) * 16 + s_z * 2 + (s_k + core) % 2
-    order = (dest == place).astype(BF16)
-    mixed = jnp.dot(order, mixed.reshape(nb, per * feats), preferred_element_type=F32)
-    mixed = mixed.astype(BF16).reshape(nb, 1, per, feats)
-    copies = jnp.broadcast_to(mixed, (nb, nc, per, feats)).reshape(nb * nc, per, feats)
-    home = lax.all_to_all(copies, AXES, 0, 0, tiled=True).reshape(nb, nc * per, feats)
-    home = home.transpose(1, 0, 2).reshape(rows, features)
+    mixed = jnp.sum(got.astype(F32), axis=0).astype(BF16).reshape(8, per, 2, 2, feats)
+    mixed = jnp.where(core == 0, mixed, mixed[:, :, :, ::-1])
+    mixed = jnp.where(side == 0, mixed, mixed[:, :, ::-1]).reshape(8, 1, per, 4 * feats)
+
+    copies = jnp.broadcast_to(mixed, (8, nc, per, 4 * feats)).reshape(8 * nc, per, 4 * feats)
+    home = lax.all_to_all(copies, ("z",) + CHAN, 0, 0, tiled=True)
+    home = home.reshape(8, rows, 2, 2 * feats).transpose(1, 2, 0, 3).reshape(rows, features)
     hidden = (embed_wide + home.astype(F32)).astype(BF16).reshape(steps, reqs, features)
     return (hidden, filter_out, scan_now)
 

time: 273 us -> 230 us (0.84)
  waiting for transfers between devices: 104 us -> 55.9 us
  blocking collectives: 48.7 us -> 35.1 us
  other arithmetic: 10.9 us -> 18.1 us
  matrix products: 16 us -> 21.1 us
  starting transfers between devices: 59.5 us -> 63.8 us
    ppermute x8, waiting for transfers between devices: 18.2 us -> 2.15 us  [swap(): return lax.ppermute(block, axis, [(0, 1), (1, 0)])]
    all_to_all x1, blocking collectives: 23.1 us -> 9.83 us  [local(): got = lax.all_to_all(sent, CHAN, 0, 0, tiled=True)]
    ppermute x14, waiting for transfers between devices: 21.2 us -> 9.43 us  [shift(): lax.ppermute(block, axis, [(i, (i + distance) % n) for i in range(n)])]
    all_gather x1, waiting for transfers between devices: 9.94 us -> 0.01 us  [local(): step_full = lax.all_gather(step_rows, 'z', axis=0, tiled=True)]
    ppermute x14, starting transfers between devices: 12.1 us -> 17.7 us  [shift(): lax.ppermute(block, axis, [(i, (i + distance) % n) for i in range(n)])]
    all_to_all x3, waiting for transfers between devices: 35.8 us -> 30.4 us  [the longest x1 15.2 us: local(): picked = lax.all_to_all(picked, ('h', 'z'), 0, 0, tiled=True)]
    dot_general x6 -> x8, matrix products: 8.76 us -> 13.8 us  [the longest x4 6.15 us: local(): jnp.dot(every, w, preferred_element_type=F32).astype(BF16)]
    all_to_all x3, waiting for transfers between devices: 17.8 us -> 13.9 us  [gather_copies(): return lax.all_to_all(copies, axes, 0, 0, tiled=True)]
  transfers between devices with their start and end apart: 29 -> 29, of which waited for: 22 -> 13; matrix products, arithmetic and copies ran while one was open for 9% -> 20% of each run, Pallas kernels for 0% -> 0%
where the time goes in v3:
time: 230 us; the launch traced here: 229 us
  starting transfers between devices  63.8 us (28%)
  waiting for transfers between devices  55.9 us (24%)
  blocking collectives  35.1 us (15%)
  matrix products  21.1 us (9%)
  local copies, waits for them, and re-layouts  20 us (9%)
  other arithmetic  18.1 us (8%)
  between operations  14.7 us (6%)
    all_gather x1, blocking collectives, local(): every = lax.all_gather(gated, 'z').reshape(8 * rows, channels)  25.3 us
    all_to_all x3, starting transfers between devices, gather_copies(): return lax.all_to_all(copies, axes, 0, 0, tiled=True)  23.4 us
    ppermute x14, starting transfers between devices, shift(): lax.ppermute(block, axis, [(i, (i + distance) % n) for i in range(n)])  17.7 us
    all_to_all x1, waiting for transfers between devices, local(): picked = lax.all_to_all(picked, ('h', 'z'), 0, 0, tiled=True)  15.2 us
    all_to_all x3, waiting for transfers between devices, gather_copies(): return lax.all_to_all(copies, axes, 0, 0, tiled=True)  13.9 us
    all_to_all x1, waiting for transfers between devices, local(): home = lax.all_to_all(copies, ('z',) + CHAN, 0, 0, tiled=True)  10.1 us
    all_to_all x1, blocking collectives, local(): got = lax.all_to_all(sent, CHAN, 0, 0, tiled=True)  9.83 us
    ppermute x14, waiting for transfers between devices, shift(): lax.ppermute(block, axis, [(i, (i + distance) % n) for i in range(n)])  9.43 us
  transfers between devices with their start and end apart: 29, of which 13 were waited for; matrix products, arithmetic and copies ran while one was open for 20% of the time, Pallas kernels for 0%

profile of v3, /device:TPU:8, one launch (start us, length us, event | category | flops | bytes accessed | tf_op | source)
XLA Modules:
  0.0 228.8 jit_solution(13735831783357892909)
XLA Ops:
  8.7 10.6 %all-to-all-start = ((s32[32,1,16]{2,1,0:T(1,128)}), s32[32,1,16]{2,1,0:T(1,128)S(1)}, u32[]{:S(2)}, u32[]{:S(2)}) async-start(s32[32,1,16]{2,1,0:T(1,128)} %broadcast_in_dim.13), calls=%async_computation | async-start | bytes 32768 | tf_op jit(solution)/shard_map/all_to_all | solution.py:23
  19.7 3.9 %copy.97 = bf16[32,8,2,2048]{3,1,2,0:T(8,128)(2,1)} copy(bf16[32,8,2,2048]{3,2,1,0:T(2,128)(2,1)} %bitcast.154) | data formatting | bytes 4194304
  23.6 5.6 %all-to-all-done = s32[32,1,16]{2,1,0:T(1,128)S(1)} async-done(((s32[32,1,16]{2,1,0:T(1,128)}), s32[32,1,16]{2,1,0:T(1,128)S(1)}, u32[]{:S(2)}, u32[]{:S(2)}) %all-to-all-start) | async-done | bytes 2080 | tf_op jit(solution)/shard_map/all_to_all | solution.py:23
  29.2 4.6 %fusion.6 = bf16[512,1024]{1,0:T(8,128)(2,1)S(1)} fusion(bf16[2048,1024]{1,0:T(8,128)(2,1)} %param.16, s32[2048]{0:T(1024)S(1)} %iota_add_fusion, s32[512]{0:T(512)S(1)} %reshape.255), kind=kOutput, calls=%fused_computation.10 | convolution fusion | flops 2149056512 | bytes 5253120 | tf_op jit(solution)/shard_map/dot_general | solution.py:109
  36.9 4.0 %all-to-all-start.1 = ((bf16[16,16,1024]{2,1,0:T(8,128)(2,1)}), bf16[16,16,1024]{2,1,0:T(8,128)(2,1)S(1)}, u32[]{:S(2)}, u32[]{:S(2)}) async-start(bf16[16,16,1024]{2,1,0:T(8,128)(2,1)} %fusion.11), calls=%async_computation.1 | async-start | bytes 1048576 | tf_op jit(solution)/shard_map/all_to_all | solution.py:112
  43.0 15.2 %all-to-all-done.1 = bf16[16,16,1024]{2,1,0:T(8,128)(2,1)S(1)} async-done(((bf16[16,16,1024]{2,1,0:T(8,128)(2,1)}), bf16[16,16,1024]{2,1,0:T(8,128)(2,1)S(1)}, u32[]{:S(2)}, u32[]{:S(2)}) %all-to-all-start.1) | async-done | bytes 524320 | tf_op jit(solution)/shard_map/all_to_all | solution.py:112
  59.1 5.8 %all-to-all-start.2 = ((bf16[8,16,1024]{2,1,0:T(8,128)(2,1)}), bf16[8,16,1024]{2,1,0:T(8,128)(2,1)S(1)}, u32[]{:S(2)}, u32[]{:S(2)}) async-start(bf16[8,16,1024]{2,1,0:T(8,128)(2,1)} %broadcast_in_dim.14), calls=%async_computation.2 | async-start | bytes 524288 | tf_op jit(solution)/shard_map/all_to_all | solution.py:23
  65.5 5.4 %all-to-all-done.2 = bf16[8,16,1024]{2,1,0:T(8,128)(2,1)S(1)} async-done(((bf16[8,16,1024]{2,1,0:T(8,128)(2,1)}), bf16[8,16,1024]{2,1,0:T(8,128)(2,1)S(1)}, u32[]{:S(2)}, u32[]{:S(2)}) %all-to-all-start.2) | async-done | bytes 262176 | tf_op jit(solution)/shard_map/all_to_all | solution.py:23
  73.4 5.0 %all-to-all-start.3 = ((bf16[16,16,512]{2,1,0:T(8,128)(2,1)}), bf16[16,16,512]{2,1,0:T(8,128)(2,1)S(1)}, u32[]{:S(2)}, u32[]{:S(2)}) async-start(bf16[16,16,512]{2,1,0:T(8,128)(2,1)} %copy.76), calls=%async_computation.3 | async-start | bytes 524288 | tf_op jit(solution)/shard_map/all_to_all | solution.py:119
  79.4 3.1 %pad_maximum_fusion = bf16[2,2048,256]{2,1,0:T(8,128)(2,1)} fusion(bf16[1,2048,256]{2,1,0:T(8,128)(2,1)} %bitcast.46, bf16[1,2048,256]{2,1,0:T(8,128)(2,1)} %bitcast.149), kind=kLoop, calls=%fused_computation.7 | loop fusion | flops 1048576 | bytes 4194304 | tf_op jit(solution)/shard_map/stack | solution.py:105
  82.5 3.4 %collective-permute-start.21 = (bf16[2,2048,256]{2,1,0:T(8,128)(2,1)}, bf16[2,2048,256]{2,1,0:T(8,128)(2,1)}, u32[]{:S(2)}, u32[]{:S(2)}) collective-permute-start(bf16[2,2048,256]{2,1,0:T(8,128)(2,1)} %pad_maximum_fusion), channel_id=1, source_target_pairs={{0,128},{128,0},{1,129},{129,1},{2,130},{130,2},{3,131},{131,3},{4... | collective-permute-start | bytes 6291464 | tf_op jit(solution)/shard_map/ppermute | solution.py:27
  85.9 5.0 %all-to-all-done.3 = bf16[16,16,512]{2,1,0:T(8,128)(2,1)S(1)} async-done(((bf16[16,16,512]{2,1,0:T(8,128)(2,1)}), bf16[16,16,512]{2,1,0:T(8,128)(2,1)S(1)}, u32[]{:S(2)}, u32[]{:S(2)}) %all-to-all-start.3) | async-done | bytes 262176 | tf_op jit(solution)/shard_map/all_to_all | solution.py:119
  93.3 2.6 %fusion.3 = bf16[256,2048]{1,0:T(8,128)(2,1)} fusion(f32[256,2048]{1,0:T(8,128)S(1)} %fusion.12, bf16[256,4096]{1,0:T(8,128)(2,1)} %collective-permute-done.1, bf16[256,512]{1,0:T(8,128)(2,1)S(1)} %bitcast.152, s32[]{:T(128)S(6)} %select_n.147), kind=kOutput, calls=%fused_computation.5 | convolution fusion | flops 269484032 | bytes 4325380 | tf_op jit(solution)/shard_map/dot_general | solution.py:127
  95.9 2.8 %fusion.2 = bf16[256,2048]{1,0:T(8,128)(2,1)} fusion(f32[256,2048]{1,0:T(8,128)S(1)} %fusion.14, bf16[256,4096]{1,0:T(8,128)(2,1)} %collective-permute-done.1, bf16[256,512]{1,0:T(8,128)(2,1)S(1)} %bitcast.153, s32[]{:T(128)S(6)} %select_n.147), kind=kOutput, calls=%fused_computation.4 | convolution fusion | flops 269484032 | bytes 4325380 | tf_op jit(solution)/shard_map/dot_general | solution.py:127
  108.4 2.6 %collective-permute-done.8 = bf16[2,16,2048]{2,1,0:T(8,128)(2,1)S(1)} collective-permute-done((bf16[2,16,2048]{2,1,0:T(8,128)(2,1)S(1)}, bf16[2,16,2048]{2,1,0:T(8,128)(2,1)S(1)}, u32[]{:S(2)}, u32[]{:S(2)}) %collective-permute-start.8) | collective-permute-done | bytes 131104 | tf_op jit(solution)/shard_map/ppermute | solution.py:32
  117.0 4.3 %collective-permute-done.6 = bf16[2,16,2048]{2,1,0:T(8,128)(2,1)S(1)} collective-permute-done((bf16[2,16,2048]{2,1,0:T(8,128)(2,1)S(1)}, bf16[2,16,2048]{2,1,0:T(8,128)(2,1)S(1)}, u32[]{:S(2)}, u32[]{:S(2)}) %collective-permute-start.6) | collective-permute-done | bytes 131104 | tf_op jit(solution)/shard_map/ppermute | solution.py:32
  124.6 3.2 %collective-permute-start.17 = (bf16[2,16,2048]{2,1,0:T(8,128)(2,1)S(1)}, bf16[2,16,2048]{2,1,0:T(8,128)(2,1)S(1)}, u32[]{:S(2)}, u32[]{:S(2)}) collective-permute-start(bf16[2,16,2048]{2,1,0:T(8,128)(2,1)S(1)} %get-tuple-element.21), channel_id=1, source_target_pairs={{0,112},{16,0},{32,16},{48,32},{64,48},{80,64},{96,80},{112,96},{1... | collective-permute-start | bytes 393224 | tf_op jit(solution)/shard_map/ppermute | solution.py:32
  132.7 2.5 %collective-permute-start.18 = (bf16[2,16,2048]{2,1,0:T(8,128)(2,1)}, bf16[2,16,2048]{2,1,0:T(8,128)(2,1)}, u32[]{:S(2)}, u32[]{:S(2)}) collective-permute-start(bf16[2,16,2048]{2,1,0:T(8,128)(2,1)} %get-tuple-element.19), channel_id=1, source_target_pairs={{0,112},{16,0},{32,16},{48,32},{64,48},{80,64},{96,80},{112,96},{1... | collective-permute-start | bytes 393224 | tf_op jit(solution)/shard_map/ppermute | solution.py:32
  137.3 7.1 %all-to-all-start.4 = ((f32[8,16,544]{2,1,0:T(8,128)}), f32[8,16,544]{2,1,0:T(8,128)S(1)}, u32[]{:S(2)}, u32[]{:S(2)}) async-start(f32[8,16,544]{2,1,0:T(8,128)} %broadcast_in_dim.15), calls=%async_computation.4 | async-start | bytes 655360 | tf_op jit(solution)/shard_map/all_to_all | solution.py:23
  147.9 2.9 %all-to-all-done.4 = f32[8,16,544]{2,1,0:T(8,128)S(1)} async-done(((f32[8,16,544]{2,1,0:T(8,128)}), f32[8,16,544]{2,1,0:T(8,128)S(1)}, u32[]{:S(2)}, u32[]{:S(2)}) %all-to-all-start.4) | async-done | bytes 278560 | tf_op jit(solution)/shard_map/all_to_all | solution.py:23
  156.6 25.3 %all-gather = bf16[128,2048]{1,0:T(8,128)(2,1)S(1)} all-gather(bf16[16,2048]{1,0:T(8,128)(2,1)S(1)} %fusion.47), channel_id=2, replica_groups=mesh['h'=2,'z'=8,'k'=2,'x'=4,'l'=2] {'z'}, dimensions={0}, use_global_device_ids=true | all-gather | bytes 589824 | tf_op jit(solution)/shard_map/all_gather | solution.py:166
  188.4 9.8 %all_to_all.36 = bf16[8,8,2,1024]{3,2,1,0:T(2,128)(2,1)S(1)} all-to-all(bf16[8,8,2,1024]{3,2,1,0:T(2,128)(2,1)S(1)} %bitcast.156), channel_id=1, replica_groups=mesh['h'=2,'z'=8,'k'=2,'x'=4,'l'=2] {'x','l'}, dimensions={0} | all-to-all | bytes 524288 | tf_op jit(solution)/shard_map/all_to_all | solution.py:171
  199.7 6.4 %all-to-all-start.6 = ((bf16[64,2,1024]{2,1,0:T(2,128)(2,1)}), bf16[64,2,1024]{2,1,0:T(2,128)(2,1)}, u32[]{:S(2)}, u32[]{:S(2)}) async-start(bf16[64,2,1024]{2,1,0:T(2,128)(2,1)} %bitcast.50), calls=%async_computation.6 | async-start | bytes 524288 | tf_op jit(solution)/shard_map/all_to_all | solution.py:177
  207.2 10.1 %all-to-all-done.6 = bf16[64,2,1024]{2,1,0:T(2,128)(2,1)} async-done(((bf16[64,2,1024]{2,1,0:T(2,128)(2,1)}), bf16[64,2,1024]{2,1,0:T(2,128)(2,1)}, u32[]{:S(2)}, u32[]{:S(2)}) %all-to-all-start.6) | async-done | bytes 262176 | tf_op jit(solution)/shard_map/all_to_all | solution.py:177
  (150 shorter events, 62.9 us)
Async XLA Ops:
  8.7 20.4 %all-to-all-start = ((s32[32,1,16]{2,1,0:T(1,128)}), s32[32,1,16]{2,1,0:T(1,128)S(1)}, u32[]{:S(2)}, u32[]{:S(2)}) async-start(s32[32,1,16]{2,1,0:T(1,128)} %broadcast_in_dim.13), calls=%async_computation | async-start | bytes 32768 | tf_op jit(solution)/shard_map/all_to_all | solution.py:23
  19.3 14.7 %collective-permute-start.2 = (bf16[16,2048]{1,0:T(8,128)(2,1)}, bf16[16,2048]{1,0:T(8,128)(2,1)S(1)}, u32[]{:S(2)}, u32[]{:S(2)}) collective-permute-start(bf16[16,2048]{1,0:T(8,128)(2,1)} %param.23), channel_id=1, source_target_pairs={{0,8},{8,0},{1,9},{9,1},{2,10},{10,2},{3,11},{11,3},{4,12},{12,4},... | collective-permute-start | bytes 196616 | tf_op jit(solution)/shard_map/ppermute | solution.py:27
  34.1 7.5 %collective-permute-start.3 = (bf16[32,2048]{1,0:T(8,128)(2,1)S(1)}, bf16[32,2048]{1,0:T(8,128)(2,1)S(1)}, u32[]{:S(2)}, u32[]{:S(2)}) collective-permute-start(bf16[32,2048]{1,0:T(8,128)(2,1)S(1)} %pad_maximum_fusion.4), channel_id=1, source_target_pairs={{0,128},{128,0},{1,129},{129,1},{2,130},{130,2},{3,131},{131,3},{4... | collective-permute-start | bytes 393224 | tf_op jit(solution)/shard_map/ppermute | solution.py:27
  36.9 21.4 %all-to-all-start.1 = ((bf16[16,16,1024]{2,1,0:T(8,128)(2,1)}), bf16[16,16,1024]{2,1,0:T(8,128)(2,1)S(1)}, u32[]{:S(2)}, u32[]{:S(2)}) async-start(bf16[16,16,1024]{2,1,0:T(8,128)(2,1)} %fusion.11), calls=%async_computation.1 | async-start | bytes 1048576 | tf_op jit(solution)/shard_map/all_to_all | solution.py:112
  40.8 57.9 %all-gather.3.cloned.1.call-start = ((), (), s32[]{:S(2)}) async-start(), calls=%async_computation.7 | async-start | bytes 2359296 | tf_op jit(solution)/shard_map/all_gather | solution.py:98
  42.3 37.1 %collective-permute-start.20 = (bf16[2048,256]{1,0:T(8,128)(2,1)}, bf16[2048,256]{1,0:T(8,128)(2,1)}, u32[]{:S(2)}, u32[]{:S(2)}) collective-permute-start(bf16[2048,256]{1,0:T(8,128)(2,1)} %param.27), channel_id=1, source_target_pairs={{0,8},{8,0},{1,9},{9,1},{2,10},{10,2},{3,11},{11,3},{4,12},{12,4},... | collective-permute-start | bytes 3145736 | tf_op jit(solution)/shard_map/ppermute | solution.py:27
  59.1 11.9 %all-to-all-start.2 = ((bf16[8,16,1024]{2,1,0:T(8,128)(2,1)}), bf16[8,16,1024]{2,1,0:T(8,128)(2,1)S(1)}, u32[]{:S(2)}, u32[]{:S(2)}) async-start(bf16[8,16,1024]{2,1,0:T(8,128)(2,1)} %broadcast_in_dim.14), calls=%async_computation.2 | async-start | bytes 524288 | tf_op jit(solution)/shard_map/all_to_all | solution.py:23
  65.5 27.7 %collective-permute-start.1 = (bf16[256,4096]{1,0:T(8,128)(2,1)}, bf16[256,4096]{1,0:T(8,128)(2,1)}, u32[]{:S(2)}, u32[]{:S(2)}) collective-permute-start(bf16[256,4096]{1,0:T(8,128)(2,1)} %bitcast.135), channel_id=1, source_target_pairs={{0,8},{8,0},{1,9},{9,1},{2,10},{10,2},{3,11},{11,3},{4,12},{12,4},... | collective-permute-start | bytes 6291464 | tf_op jit(solution)/shard_map/ppermute | solution.py:27
  73.4 17.6 %all-to-all-start.3 = ((bf16[16,16,512]{2,1,0:T(8,128)(2,1)}), bf16[16,16,512]{2,1,0:T(8,128)(2,1)S(1)}, u32[]{:S(2)}, u32[]{:S(2)}) async-start(bf16[16,16,512]{2,1,0:T(8,128)(2,1)} %copy.76), calls=%async_computation.3 | async-start | bytes 524288 | tf_op jit(solution)/shard_map/all_to_all | solution.py:119
  82.5 100.9 %collective-permute-start.21 = (bf16[2,2048,256]{2,1,0:T(8,128)(2,1)}, bf16[2,2048,256]{2,1,0:T(8,128)(2,1)}, u32[]{:S(2)}, u32[]{:S(2)}) collective-permute-start(bf16[2,2048,256]{2,1,0:T(8,128)(2,1)} %pad_maximum_fusion), channel_id=1, source_target_pairs={{0,128},{128,0},{1,129},{129,1},{2,130},{130,2},{3,131},{131,3},{4... | collective-permute-start | bytes 6291464 | tf_op jit(solution)/shard_map/ppermute | solution.py:27
  99.8 6.6 %collective-permute-start.4 = (bf16[2,16,2048]{2,1,0:T(8,128)(2,1)S(1)}, bf16[2,16,2048]{2,1,0:T(8,128)(2,1)S(1)}, u32[]{:S(2)}, u32[]{:S(2)}) collective-permute-start(bf16[2,16,2048]{2,1,0:T(8,128)(2,1)S(1)} %get-tuple-element.26), channel_id=1, source_target_pairs={{0,16},{16,32},{32,48},{48,64},{64,80},{80,96},{96,112},{112,0},{1... | collective-permute-start | bytes 393224 | tf_op jit(solution)/shard_map/ppermute | solution.py:32
  101.9 13.2 %collective-permute-start.12 = (bf16[2,16,2048]{2,1,0:T(8,128)(2,1)S(1)}, bf16[2,16,2048]{2,1,0:T(8,128)(2,1)S(1)}, u32[]{:S(2)}, u32[]{:S(2)}) collective-permute-start(bf16[2,16,2048]{2,1,0:T(8,128)(2,1)S(1)} %get-tuple-element.22), channel_id=1, source_target_pairs={{0,16},{16,32},{32,48},{48,64},{64,80},{80,96},{96,112},{112,0},{1... | collective-permute-start | bytes 393224 | tf_op jit(solution)/shard_map/ppermute | solution.py:32
  103.5 20.9 %collective-permute-start.16 = (bf16[2,16,2048]{2,1,0:T(8,128)(2,1)S(1)}, bf16[2,16,2048]{2,1,0:T(8,128)(2,1)S(1)}, u32[]{:S(2)}, u32[]{:S(2)}) collective-permute-start(bf16[2,16,2048]{2,1,0:T(8,128)(2,1)S(1)} %get-tuple-element.23), channel_id=1, source_target_pairs={{0,112},{16,0},{32,16},{48,32},{64,48},{80,64},{96,80},{112,96},{1... | collective-permute-start | bytes 393224 | tf_op jit(solution)/shard_map/ppermute | solution.py:32
  107.3 6.7 %collective-permute-start.5 = (bf16[2,16,2048]{2,1,0:T(8,128)(2,1)S(1)}, bf16[2,16,2048]{2,1,0:T(8,128)(2,1)S(1)}, u32[]{:S(2)}, u32[]{:S(2)}) collective-permute-start(bf16[2,16,2048]{2,1,0:T(8,128)(2,1)S(1)} %fusion.27), channel_id=1, source_target_pairs={{0,16},{16,32},{32,48},{48,64},{64,80},{80,96},{96,112},{112,0},{1... | collective-permute-start | bytes 393224 | tf_op jit(solution)/shard_map/ppermute | solution.py:32
  115.0 6.3 %collective-permute-start.6 = (bf16[2,16,2048]{2,1,0:T(8,128)(2,1)S(1)}, bf16[2,16,2048]{2,1,0:T(8,128)(2,1)S(1)}, u32[]{:S(2)}, u32[]{:S(2)}) collective-permute-start(bf16[2,16,2048]{2,1,0:T(8,128)(2,1)S(1)} %fusion.28), channel_id=1, source_target_pairs={{0,16},{16,32},{32,48},{48,64},{64,80},{80,96},{96,112},{112,0},{1... | collective-permute-start | bytes 393224 | tf_op jit(solution)/shard_map/ppermute | solution.py:32
  115.2 9.3 %collective-permute-start.13 = (bf16[2,16,2048]{2,1,0:T(8,128)(2,1)S(1)}, bf16[2,16,2048]{2,1,0:T(8,128)(2,1)S(1)}, u32[]{:S(2)}, u32[]{:S(2)}) collective-permute-start(bf16[2,16,2048]{2,1,0:T(8,128)(2,1)S(1)} %fusion.20), channel_id=1, source_target_pairs={{0,16},{16,32},{32,48},{48,64},{64,80},{80,96},{96,112},{112,0},{1... | collective-permute-start | bytes 393224 | tf_op jit(solution)/shard_map/ppermute | solution.py:32
  122.4 6.3 %collective-permute-start.7 = (bf16[2,16,2048]{2,1,0:T(8,128)(2,1)S(1)}, bf16[2,16,2048]{2,1,0:T(8,128)(2,1)S(1)}, u32[]{:S(2)}, u32[]{:S(2)}) collective-permute-start(bf16[2,16,2048]{2,1,0:T(8,128)(2,1)S(1)} %get-tuple-element.24), channel_id=1, source_target_pairs={{0,16},{16,32},{32,48},{48,64},{64,80},{80,96},{96,112},{112,0},{1... | collective-permute-start | bytes 393224 | tf_op jit(solution)/shard_map/ppermute | solution.py:32
  124.5 6.7 %collective-permute-start.14 = (bf16[2,16,2048]{2,1,0:T(8,128)(2,1)S(1)}, bf16[2,16,2048]{2,1,0:T(8,128)(2,1)S(1)}, u32[]{:S(2)}, u32[]{:S(2)}) collective-permute-start(bf16[2,16,2048]{2,1,0:T(8,128)(2,1)S(1)} %get-tuple-element.20), channel_id=1, source_target_pairs={{0,16},{16,32},{32,48},{48,64},{64,80},{80,96},{96,112},{112,0},{1... | collective-permute-start | bytes 393224 | tf_op jit(solution)/shard_map/ppermute | solution.py:32
  124.6 6.6 %collective-permute-start.17 = (bf16[2,16,2048]{2,1,0:T(8,128)(2,1)S(1)}, bf16[2,16,2048]{2,1,0:T(8,128)(2,1)S(1)}, u32[]{:S(2)}, u32[]{:S(2)}) collective-permute-start(bf16[2,16,2048]{2,1,0:T(8,128)(2,1)S(1)} %get-tuple-element.21), channel_id=1, source_target_pairs={{0,112},{16,0},{32,16},{48,32},{64,48},{80,64},{96,80},{112,96},{1... | collective-permute-start | bytes 393224 | tf_op jit(solution)/shard_map/ppermute | solution.py:32
  132.0 12.4 %collective-permute-start.15 = (bf16[2,16,2048]{2,1,0:T(8,128)(2,1)}, bf16[2,16,2048]{2,1,0:T(8,128)(2,1)S(1)}, u32[]{:S(2)}, u32[]{:S(2)}) collective-permute-start(bf16[2,16,2048]{2,1,0:T(8,128)(2,1)} %get-tuple-element.18), channel_id=1, source_target_pairs={{0,16},{16,32},{32,48},{48,64},{64,80},{80,96},{96,112},{112,0},{1... | collective-permute-start | bytes 393224 | tf_op jit(solution)/shard_map/ppermute | solution.py:32
  132.7 12.3 %collective-permute-start.18 = (bf16[2,16,2048]{2,1,0:T(8,128)(2,1)}, bf16[2,16,2048]{2,1,0:T(8,128)(2,1)}, u32[]{:S(2)}, u32[]{:S(2)}) collective-permute-start(bf16[2,16,2048]{2,1,0:T(8,128)(2,1)} %get-tuple-element.19), channel_id=1, source_target_pairs={{0,112},{16,0},{32,16},{48,32},{64,48},{80,64},{96,80},{112,96},{1... | collective-permute-start | bytes 393224 | tf_op jit(solution)/shard_map/ppermute | solution.py:32
  137.3 13.6 %all-to-all-start.4 = ((f32[8,16,544]{2,1,0:T(8,128)}), f32[8,16,544]{2,1,0:T(8,128)S(1)}, u32[]{:S(2)}, u32[]{:S(2)}) async-start(f32[8,16,544]{2,1,0:T(8,128)} %broadcast_in_dim.15), calls=%async_computation.4 | async-start | bytes 655360 | tf_op jit(solution)/shard_map/all_to_all | solution.py:23
  146.7 9.0 %collective-permute-start.19 = (bf16[16,2048]{1,0:T(8,128)(2,1)}, bf16[16,2048]{1,0:T(8,128)(2,1)}, u32[]{:S(2)}, u32[]{:S(2)}) collective-permute-start(bf16[16,2048]{1,0:T(8,128)(2,1)} %dynamic-slice_bitcast_fusion.5), channel_id=1, source_target_pairs={{0,128},{128,0},{1,129},{129,1},{2,130},{130,2},{3,131},{131,3},{4... | collective-permute-start | bytes 196616 | tf_op jit(solution)/shard_map/ppermute | solution.py:27
  199.7 17.6 %all-to-all-start.6 = ((bf16[64,2,1024]{2,1,0:T(2,128)(2,1)}), bf16[64,2,1024]{2,1,0:T(2,128)(2,1)}, u32[]{:S(2)}, u32[]{:S(2)}) async-start(bf16[64,2,1024]{2,1,0:T(2,128)(2,1)} %bitcast.50), calls=%async_computation.6 | async-start | bytes 524288 | tf_op jit(solution)/shard_map/all_to_all | solution.py:177
  (19 other events, 299.9 us)
Sparse Core Ops, SparseCore 0:
  43.5 46.8 all-gather.2

commit v4 on v3

--- a/solution.py
+++ b/solution.py
@@ -1,6 +1,8 @@
 import jax
 import jax.numpy as jnp
 from jax import lax
+from jax.experimental import pallas as pl
+from jax.experimental.pallas import tpu as pltpu
 from jax.sharding import Mesh, PartitionSpec as P
 
 BATCH = ("h", "z", "k")
@@ -32,9 +34,9 @@
     return lax.ppermute(block, axis, [(i, (i + distance) % n) for i in range(n)])
 
 
-def in_order(mine, other, index):
+def in_order(mine, other, index, axis):
     first = jnp.where(index == 0, mine, other)
-    return jnp.concatenate([first, jnp.where(index == 0, other, mine)])
+    return jnp.concatenate([first, jnp.where(index == 0, other, mine)], axis=axis)
 
 
 def take(block, index):
@@ -51,6 +53,8 @@
     up = [None] * len(parts)
     down = [None] * len(parts)
     for away in range(n // 2, 0, -1):
+        if up[0] is not None:
+            up[0], down[0] = lax.optimization_barrier((up[0], down[0]))
         for i, part in enumerate(parts):
             term = take(part, (here + away) % n)
             up[i] = shift(term if up[i] is None else add(term, up[i]), axis, 1)
@@ -61,6 +65,167 @@
         (take(part, here).astype(F32) + u.astype(F32) + d.astype(F32)).astype(BF16)
         for part, u, d in zip(parts, up, down)
     ]
+
+
+def convolve_kernel(mine_ref, got_ref, past_ref, taps_ref, bias_ref, select_ref, conv_ref, past_out_ref, part_ref):
+    kept, reqs, _ = past_ref.shape
+    rows = mine_ref.shape[0]
+    steps = rows // reqs
+    stream = (mine_ref[...].astype(F32) + got_ref[...].astype(F32)).astype(BF16).astype(F32)
+    window = [past_ref[i] for i in range(kept)]
+    window += [stream[i * reqs : (i + 1) * reqs] for i in range(steps)]
+    for i in range(kept):
+        past_out_ref[i] = window[steps + i]
+    found = []
+    for t in range(steps):
+        total = window[t] * taps_ref[0:1, :]
+        for i in range(1, kept + 1):
+            total += window[t + i] * taps_ref[i : i + 1, :]
+        total += bias_ref[...]
+        found.append(total * jax.nn.sigmoid(total))
+    convolved = jnp.concatenate(found, axis=0)
+    conv_ref[...] = convolved
+    low = convolved.astype(BF16)
+    rank_size = part_ref.shape[2] - 128
+    turned = (((1,), (1,)), ((), ()))
+    rank = lax.dot_general(low, select_ref[:rank_size, :], turned, preferred_element_type=F32)
+    rest = lax.dot_general(low, select_ref[rank_size:, :], turned, preferred_element_type=F32)
+    rest = jnp.concatenate([rest, jnp.zeros((rows, 128 - rest.shape[1]), F32)], axis=1)
+    for i in range(part_ref.shape[0]):
+        part_ref[i, :, :rank_size] = rank
+        part_ref[i, :, rank_size:] = rest
+
+
+def convolve(mine, got, past, taps, bias, select, rank_size, copies):
+    rows, channels = mine.shape
+    width = rank_size + 128
+    return pl.pallas_call(
+        convolve_kernel,
+        out_shape=(
+            jax.ShapeDtypeStruct((rows, channels), F32),
+            jax.ShapeDtypeStruct(past.shape, F32),
+            jax.ShapeDtypeStruct((copies, rows, width), F32),
+        ),
+        compiler_params=pltpu.CompilerParams(vmem_limit_bytes=24 * 1024 * 1024),
+        cost_estimate=pl.CostEstimate(
+            flops=2 * rows * channels * width,
+            bytes_accessed=2 * channels * width,
+            transcendentals=rows * channels,
+        ),
+        name="convolve",
+    )(mine, got, past, taps, bias[None], select)
+
+
+def scan_kernel(
+    got_ref, gain_ref, step_ref, bias_ref, decay_ref, skip_ref, conv_ref, gate_ref, gate_got_ref, state_ref,
+    gated_ref, state_out_ref, weight_ref,
+):
+    reqs, states, _ = state_ref.shape
+    rows = conv_ref.shape[0]
+    rank_size = gain_ref.shape[1]
+    turns, sides, tall, _ = step_ref.shape
+    for z in range(turns):
+        for h in range(sides):
+            first = (h * turns + z) * tall
+            weight_ref[first : first + tall, :] = step_ref[z, h]
+    selected = got_ref[0]
+    for i in range(1, got_ref.shape[0]):
+        selected += got_ref[i]
+    rank = selected[:, :rank_size]
+    mean_square = jnp.mean(rank * rank, axis=-1, keepdims=True)
+    normed = (rank * lax.rsqrt(mean_square + 1e-06) * gain_ref[...]).astype(BF16)
+    raw = jnp.dot(normed, weight_ref[...], preferred_element_type=F32) + bias_ref[...]
+    delta = jnp.maximum(raw, 0.0) + jnp.log1p(jnp.exp(-jnp.abs(raw)))
+    columns = jnp.transpose(selected[:, rank_size:])
+    rate = -jnp.exp(decay_ref[...])
+    convolved = conv_ref[...]
+    pushed = delta * convolved
+    gate = (gate_ref[...].astype(F32) + gate_got_ref[...].astype(F32)).astype(BF16).astype(F32)
+    gate = gate * jax.nn.sigmoid(gate)
+    skipped = skip_ref[...] * convolved
+    read = [None] * rows
+    for r in range(reqs):
+        state = state_ref[r]
+        for t in range(rows // reqs):
+            i = t * reqs + r
+            bvec = columns[:states, i : i + 1]
+            cvec = columns[states : 2 * states, i : i + 1]
+            state = jnp.exp(delta[i : i + 1] * rate) * state + pushed[i : i + 1] * bvec
+            read[i] = jnp.sum(state * cvec, axis=0, keepdims=True)
+        state_out_ref[r] = state
+    readout = jnp.concatenate(read, axis=0) + skipped
+    gated_ref[...] = (readout * gate).astype(BF16)
+
+
+def scan(got, gain, step, bias, decay, skip, conv, gate, gate_got, state):
+    rows, channels = conv.shape
+    return pl.pallas_call(
+        scan_kernel,
+        out_shape=(
+            jax.ShapeDtypeStruct((rows, channels), BF16),
+            jax.ShapeDtypeStruct(state.shape, F32),
+        ),
+        scratch_shapes=[pltpu.VMEM((gain.shape[0], channels), BF16)],
+        compiler_params=pltpu.CompilerParams(vmem_limit_bytes=32 * 1024 * 1024),
+        cost_estimate=pl.CostEstimate(
+            flops=2 * rows * gain.shape[0] * channels + 8 * state.size,
+            bytes_accessed=2 * gain.shape[0] * channels + 8 * state.size,
+            transcendentals=4 * state.size,
+        ),
+        name="scan",
+    )(got, gain[None], step, bias[None], decay, skip[None], conv, gate, gate_got, state)
+
+
+def mix_kernel(where_ref, *refs):
+    x_refs, w_refs, out_ref, total_ref = refs[:8], refs[8:12], refs[12], refs[13]
+    rows = x_refs[0].shape[0]
+    width = w_refs[0].shape[2]
+    step = pl.program_id(0)
+
+    @pl.when(step == 0)
+    def _():
+        total_ref[...] = jnp.zeros_like(total_ref)
+
+    x = jnp.concatenate([x_ref[...] for x_ref in x_refs], axis=0)
+    for i, w_ref in enumerate(w_refs):
+        cols = slice(i * width, (i + 1) * width)
+        total_ref[:, cols] += jnp.dot(x, w_ref[0], preferred_element_type=F32)
+
+    @pl.when(step == pl.num_programs(0) - 1)
+    def _():
+        for j in range(8):
+            row = pl.multiple_of(where_ref[4 + j] * rows, rows)
+            for i in range(4):
+                lane = pl.multiple_of(where_ref[i] * width, width)
+                tile = total_ref[j * rows : (j + 1) * rows, i * width : (i + 1) * width]
+                out_ref[pl.ds(row, rows), pl.ds(lane, width)] = tile.astype(BF16)
+
+
+def mix(where, xs, near, far):
+    rows, depth = xs[0].shape
+    width = near.shape[2]
+    tiles = 4
+    tall = depth // tiles
+    return pl.pallas_call(
+        mix_kernel,
+        grid=(tiles,),
+        out_shape=jax.ShapeDtypeStruct((8 * rows, 4 * width), BF16),
+        in_specs=[pl.BlockSpec(memory_space=pltpu.SMEM)]
+        + [pl.BlockSpec((rows, tall), lambda i: (0, i))] * 8
+        + [
+            pl.BlockSpec((1, tall, width), lambda i: (0, i, 0)),
+            pl.BlockSpec((1, tall, width), lambda i: (1, i, 0)),
+        ]
+        * 2,
+        out_specs=pl.BlockSpec((8 * rows, 4 * width), lambda i: (0, 0)),
+        scratch_shapes=[pltpu.VMEM((8 * rows, 4 * width), F32)],
+        cost_estimate=pl.CostEstimate(
+            flops=64 * rows * depth * width,
+            bytes_accessed=8 * depth * width + 64 * rows * width,
+            transcendentals=0,
+        ),
+        name="mix",
+    )(where, *xs, near, near, far, far)
 
 
 def local(
@@ -84,7 +249,6 @@
     vocab_rows, width = embed_table.shape
     feats, _, channels = in_weight.shape
     rank_size = step_gain.shape[0]
-    state_size = decay_log.shape[0]
     rows = steps * reqs
     nb, nc = count(BATCH), count(CHAN)
     tokens = nb * rows
@@ -93,8 +257,9 @@
     features = norm_gain.shape[0]
 
     side = lax.axis_index("h")
-    step_rows = in_order(step_weight, swap(step_weight, "k"), core)
-    step_rows = in_order(step_rows, swap(step_rows, "h"), side)
+    step_rows = in_order(step_weight, swap(step_weight, "h"), side, 0)
+    step_rows = step_rows.reshape(2, -1, channels)
+    step_rows = in_order(step_rows, swap(step_rows, "k"), core, 1).reshape(-1, channels)
     step_full = lax.all_gather(step_rows, "z", axis=0, tiled=True)
     in_flat = in_weight.reshape(feats, 2 * channels)
 
@@ -129,53 +294,36 @@
 
     first, step_full = lax.optimization_barrier((project(0), step_full))
     sums = ring_sums([first, project(1)], "z")
-    stream, gate = [
-        add(take(one, side), swap(take(one, 1 - side), "h")).astype(F32) for one in sums
+    stream, stream_got, gate, gate_got = [
+        piece
+        for one in sums
+        for piece in (take(one, side), swap(take(one, 1 - side), "h"))
     ]
-
-    stream = stream.reshape(steps, reqs, channels)
-    window = jnp.concatenate([filter_state.transpose(1, 0, 2), stream], axis=0)
-    taps = filter_weight.shape[0]
-    mixed_in = sum(window[i : i + steps] * filter_weight[i] for i in range(taps))
-    convolved = jax.nn.silu(mixed_in + filter_bias)
-    filter_out = window[steps:].transpose(1, 0, 2)
-    conv_rows = convolved.reshape(rows, channels)
-    part = jnp.dot(conv_rows.astype(BF16), select_weight, preferred_element_type=F32)
-    selected = jnp.sum(gather_copies(part, CHAN), axis=0)
-    rank = selected[:, :rank_size]
-    bvec = selected[:, rank_size : rank_size + state_size].reshape(steps, reqs, state_size)
-    cvec = selected[:, rank_size + state_size :].reshape(steps, reqs, state_size)
-    mean_square = jnp.mean(rank * rank, axis=-1, keepdims=True)
-    rank_normed = (rank * lax.rsqrt(mean_square + 1e-06) * step_gain).astype(BF16)
-    rank_normed = rank_normed.reshape(rows, 2, 8, rank_size // 16)
-    rank_normed = rank_normed.transpose(0, 2, 1, 3).reshape(rows, rank_size)
-    delta = jax.nn.softplus(
-        jnp.dot(rank_normed, step_full, preferred_element_type=F32) + step_bias
-    ).reshape(steps, reqs, channels)
-
-    decay_rate = -jnp.exp(decay_log)
-    scan_now = scan_state
-    readouts = []
-    for t in range(steps):
-        factor = jnp.exp(delta[t][:, None, :] * decay_rate[None])
-        scan_now = factor * scan_now + (delta[t] * convolved[t])[:, None, :] * bvec[t][:, :, None]
-        readouts.append(jnp.sum(scan_now * cvec[t][:, :, None], axis=1) + skip_gain * convolved[t])
-    readout = jnp.stack(readouts).reshape(rows, channels)
-    gated = (readout * jax.nn.silu(gate)).astype(BF16)
-
-    every = lax.all_gather(gated, "z").reshape(8 * rows, channels)
-    blocks = [out_pair[0], out_pair[1], out_far[0], out_far[1]]
-    part_out = [jnp.dot(every, w, preferred_element_type=F32).astype(BF16) for w in blocks]
+    past = filter_state.transpose(1, 0, 2)
+    convolved, past, part = convolve(
+        stream, stream_got, past, filter_weight, filter_bias, select_weight.T, rank_size, nc
+    )
+    filter_out = past.transpose(1, 0, 2)
+    got = lax.all_to_all(part, CHAN, 0, 0, tiled=True)
+    step_blocks = step_full.reshape(8, 2, rank_size // 16, channels)
+    gated, scan_now = scan(
+        got, step_gain, step_blocks, step_bias, decay_log, skip_gain, convolved, gate, gate_got, scan_state
+    )
+
+    every = [gated] + [shift(gated, "z", -j) for j in range(1, 8)]
+    place = jnp.arange(4, dtype=jnp.int32)
+    place = (place // 2 + side) % 2 * 2 + (place + core) % 2
+    turn = (jnp.arange(8, dtype=jnp.int32) + lax.axis_index("z")) % 8
+    part_out = mix(jnp.concatenate([place, turn]), every, out_pair, out_far)
     per = rows // nc
-    sent = jnp.concatenate(part_out, axis=1).reshape(8, nc, per, 4 * feats).transpose(1, 0, 2, 3)
+    sent = part_out.reshape(8, nc, per, 4 * feats).transpose(1, 0, 2, 3)
     got = lax.all_to_all(sent, CHAN, 0, 0, tiled=True)
-    mixed = jnp.sum(got.astype(F32), axis=0).astype(BF16).reshape(8, per, 2, 2, feats)
-    mixed = jnp.where(core == 0, mixed, mixed[:, :, :, ::-1])
-    mixed = jnp.where(side == 0, mixed, mixed[:, :, ::-1]).reshape(8, 1, per, 4 * feats)
+    mixed = jnp.sum(got.astype(F32), axis=0).astype(BF16).reshape(8, 1, per, 4 * feats)
 
     copies = jnp.broadcast_to(mixed, (8, nc, per, 4 * feats)).reshape(8 * nc, per, 4 * feats)
     home = lax.all_to_all(copies, ("z",) + CHAN, 0, 0, tiled=True)
     home = home.reshape(8, rows, 2, 2 * feats).transpose(1, 2, 0, 3).reshape(rows, features)
+    home = lax.optimization_barrier(home)
     hidden = (embed_wide + home.astype(F32)).astype(BF16).reshape(steps, reqs, features)
     return (hidden, filter_out, scan_now)
 

time: 230 us -> 220 us (0.957)
  blocking collectives: 35.1 us -> 10.7 us
  starting transfers between devices: 63.8 us -> 79.3 us
  waiting for transfers between devices: 55.9 us -> 69.7 us
  matrix products: 21.1 us -> 8.84 us
  Pallas kernels: 0 us -> 8.04 us
  local copies, waits for them, and re-layouts: 20 us -> 14.7 us
  other arithmetic: 18.1 us -> 13.4 us
    all_gather x1 -> x0, blocking collectives: 25.3 us -> none  [local(): every = lax.all_gather(gated, 'z').reshape(8 * rows, channels)]
    ppermute x14 -> x21, starting transfers between devices: 17.7 us -> 33 us  [shift(): lax.ppermute(block, axis, [(i, (i + distance) % n) for i in range(n)])]
    ppermute x8, waiting for transfers between devices: 2.15 us -> 11.7 us  [swap(): return lax.ppermute(block, axis, [(0, 1), (1, 0)])]
    dot_general x6 -> x0, matrix products: 8.89 us -> none  [the longest x4 6.15 us: local(): jnp.dot(every, w, preferred_element_type=F32).astype(BF16)]
    pallas_call x0 -> x3, Pallas kernels: none -> 8.04 us  [the longest x1 4.56 us: mix(): pl.pallas_call(mix_kernel, grid=(tiles,), out_shape=jax.ShapeDtypeStruct(...]
    all_to_all x3 -> x2, starting transfers between devices: 23.4 us -> 16.3 us  [gather_copies(): return lax.all_to_all(copies, axes, 0, 0, tiled=True)]
    ppermute x14 -> x21, waiting for transfers between devices: 9.43 us -> 14.5 us  [shift(): lax.ppermute(block, axis, [(i, (i + distance) % n) for i in range(n)])]
    all_to_all x0 -> x1, starting transfers between devices: none -> 4.64 us  [local(): got = lax.all_to_all(part, CHAN, 0, 0, tiled=True)]
  transfers between devices with their start and end apart: 29 -> 36, of which waited for: 13 -> 16; matrix products, arithmetic and copies ran while one was open for 20% -> 13% of each run, Pallas kernels for 0% -> 2%
where the time goes in v4:
time: 220 us; the launch traced here: 219 us
  starting transfers between devices  79.3 us (36%)
  waiting for transfers between devices  69.7 us (32%)
  local copies, waits for them, and re-layouts  14.7 us (7%)
  between operations  14.7 us (7%)
  other arithmetic  13.4 us (6%)
  blocking collectives  10.7 us (5%)
  matrix products  8.84 us (4%)
  Pallas kernels  8.04 us (4%)
    ppermute x21, starting transfers between devices, shift(): lax.ppermute(block, axis, [(i, (i + distance) % n) for i in range(n)])  33 us
    all_to_all x1, waiting for transfers between devices, local(): picked = lax.all_to_all(picked, ('h', 'z'), 0, 0, tiled=True)  16.4 us
    all_to_all x2, starting transfers between devices, gather_copies(): return lax.all_to_all(copies, axes, 0, 0, tiled=True)  16.3 us
    ppermute x21, waiting for transfers between devices, shift(): lax.ppermute(block, axis, [(i, (i + distance) % n) for i in range(n)])  14.5 us
    ppermute x8, waiting for transfers between devices, swap(): return lax.ppermute(block, axis, [(0, 1), (1, 0)])  11.7 us
    all_to_all x1, waiting for transfers between devices, local(): home = lax.all_to_all(copies, ('z',) + CHAN, 0, 0, tiled=True)  11.2 us
    all_to_all x1, blocking collectives, local(): got = lax.all_to_all(sent, CHAN, 0, 0, tiled=True)  10.7 us
    all_to_all x2, waiting for transfers between devices, gather_copies(): return lax.all_to_all(copies, axes, 0, 0, tiled=True)  10 us
  transfers between devices with their start and end apart: 36, of which 16 were waited for; matrix products, arithmetic and copies ran while one was open for 13% of the time, Pallas kernels for 2%

profile of v4, /device:TPU:8, one launch (start us, length us, event | category | flops | bytes accessed | tf_op | source)
XLA Modules:
  0.0 219.3 jit_solution(17543390620630493104)
XLA Ops:
  8.5 10.6 %all-to-all-start = ((s32[32,1,16]{2,1,0:T(1,128)}), s32[32,1,16]{2,1,0:T(1,128)S(1)}, u32[]{:S(2)}, u32[]{:S(2)}) async-start(s32[32,1,16]{2,1,0:T(1,128)} %broadcast_in_dim.34), calls=%async_computation | async-start | bytes 32768 | tf_op jit(solution)/shard_map/all_to_all | solution.py:25
  19.1 3.4 %collective-permute-start.2 = (bf16[16,2048]{1,0:T(8,128)(2,1)}, bf16[16,2048]{1,0:T(8,128)(2,1)S(1)}, u32[]{:S(2)}, u32[]{:S(2)}) collective-permute-start(bf16[16,2048]{1,0:T(8,128)(2,1)} %param.23), channel_id=1, source_target_pairs={{0,128},{128,0},{1,129},{129,1},{2,130},{130,2},{3,131},{131,3},{4... | collective-permute-start | bytes 196616 | tf_op jit(solution)/shard_map/ppermute | solution.py:29
  25.0 3.9 %all-to-all-done = s32[32,1,16]{2,1,0:T(1,128)S(1)} async-done(((s32[32,1,16]{2,1,0:T(1,128)}), s32[32,1,16]{2,1,0:T(1,128)S(1)}, u32[]{:S(2)}, u32[]{:S(2)}) %all-to-all-start) | async-done | bytes 2080 | tf_op jit(solution)/shard_map/all_to_all | solution.py:25
  29.1 4.6 %fusion.6 = bf16[512,1024]{1,0:T(8,128)(2,1)S(1)} fusion(bf16[2048,1024]{1,0:T(8,128)(2,1)} %param.16, s32[2048]{0:T(1024)S(1)} %iota_add_fusion, s32[512]{0:T(512)S(1)} %reshape.133), kind=kOutput, calls=%fused_computation.9 | convolution fusion | flops 2149056512 | bytes 5253120 | tf_op jit(solution)/shard_map/dot_general | solution.py:274
  36.7 3.7 %all-to-all-start.1 = ((bf16[16,16,1024]{2,1,0:T(8,128)(2,1)}), bf16[16,16,1024]{2,1,0:T(8,128)(2,1)S(1)}, u32[]{:S(2)}, u32[]{:S(2)}) async-start(bf16[16,16,1024]{2,1,0:T(8,128)(2,1)} %fusion.11), calls=%async_computation.1 | async-start | bytes 1048576 | tf_op jit(solution)/shard_map/all_to_all | solution.py:277
  41.5 16.4 %all-to-all-done.1 = bf16[16,16,1024]{2,1,0:T(8,128)(2,1)S(1)} async-done(((bf16[16,16,1024]{2,1,0:T(8,128)(2,1)}), bf16[16,16,1024]{2,1,0:T(8,128)(2,1)S(1)}, u32[]{:S(2)}, u32[]{:S(2)}) %all-to-all-start.1) | async-done | bytes 524320 | tf_op jit(solution)/shard_map/all_to_all | solution.py:277
  58.7 5.8 %all-to-all-start.2 = ((bf16[8,16,1024]{2,1,0:T(8,128)(2,1)}), bf16[8,16,1024]{2,1,0:T(8,128)(2,1)S(1)}, u32[]{:S(2)}, u32[]{:S(2)}) async-start(bf16[8,16,1024]{2,1,0:T(8,128)(2,1)} %broadcast_in_dim.35), calls=%async_computation.2 | async-start | bytes 524288 | tf_op jit(solution)/shard_map/all_to_all | solution.py:25
  64.5 6.1 %all-to-all-done.2 = bf16[8,16,1024]{2,1,0:T(8,128)(2,1)S(1)} async-done(((bf16[8,16,1024]{2,1,0:T(8,128)(2,1)}), bf16[8,16,1024]{2,1,0:T(8,128)(2,1)S(1)}, u32[]{:S(2)}, u32[]{:S(2)}) %all-to-all-start.2) | async-done | bytes 262176 | tf_op jit(solution)/shard_map/all_to_all | solution.py:25
  73.0 5.0 %all-to-all-start.3 = ((bf16[16,16,512]{2,1,0:T(8,128)(2,1)}), bf16[16,16,512]{2,1,0:T(8,128)(2,1)S(1)}, u32[]{:S(2)}, u32[]{:S(2)}) async-start(bf16[16,16,512]{2,1,0:T(8,128)(2,1)} %copy.45), calls=%async_computation.3 | async-start | bytes 524288 | tf_op jit(solution)/shard_map/all_to_all | solution.py:284
  78.2 3.1 %pad_maximum_fusion.refs_8_.refs_9_ = bf16[2,2048,256]{2,1,0:T(8,128)(2,1)} fusion(bf16[1,2048,256]{2,1,0:T(8,128)(2,1)} %bitcast.41, bf16[1,2048,256]{2,1,0:T(8,128)(2,1)} %bitcast.138), kind=kLoop, calls=%fused_computation.6 | loop fusion | flops 1048576 | bytes 4194304 | tf_op jit(solution)/shard_map/stack | solution.py:270
  81.2 3.3 %collective-permute-start.28 = (bf16[2,2048,256]{2,1,0:T(8,128)(2,1)}, bf16[2,2048,256]{2,1,0:T(8,128)(2,1)}, u32[]{:S(2)}, u32[]{:S(2)}) collective-permute-start(bf16[2,2048,256]{2,1,0:T(8,128)(2,1)} %pad_maximum_fusion.refs_8_.refs_9_), channel_id=1, source_target_pairs={{0,128},{128,0},{1,129},{129,1},{2,130},{130,2},{3,131},{131,3},{4... | collective-permute-start | bytes 6291464 | tf_op jit(solution)/shard_map/ppermute | solution.py:29
  84.5 5.8 %all-to-all-done.3 = bf16[16,16,512]{2,1,0:T(8,128)(2,1)S(1)} async-done(((bf16[16,16,512]{2,1,0:T(8,128)(2,1)}), bf16[16,16,512]{2,1,0:T(8,128)(2,1)S(1)}, u32[]{:S(2)}, u32[]{:S(2)}) %all-to-all-start.3) | async-done | bytes 262176 | tf_op jit(solution)/shard_map/all_to_all | solution.py:284
  110.6 3.2 %collective-permute-start.17 = (bf16[2,16,2048]{2,1,0:T(8,128)(2,1)S(1)}, bf16[2,16,2048]{2,1,0:T(8,128)(2,1)S(1)}, u32[]{:S(2)}, u32[]{:S(2)}) collective-permute-start(bf16[2,16,2048]{2,1,0:T(8,128)(2,1)S(1)} %get-tuple-element.32), channel_id=1, source_target_pairs={{0,112},{16,0},{32,16},{48,32},{64,48},{80,64},{96,80},{112,96},{1... | collective-permute-start | bytes 393224 | tf_op jit(solution)/shard_map/ppermute | solution.py:34
  115.4 3.2 %collective-permute-start.8 = (bf16[2,16,2048]{2,1,0:T(8,128)(2,1)S(1)}, bf16[2,16,2048]{2,1,0:T(8,128)(2,1)S(1)}, u32[]{:S(2)}, u32[]{:S(2)}) collective-permute-start(bf16[2,16,2048]{2,1,0:T(8,128)(2,1)S(1)} %get-tuple-element.37), channel_id=1, source_target_pairs={{0,112},{16,0},{32,16},{48,32},{64,48},{80,64},{96,80},{112,96},{1... | collective-permute-start | bytes 393224 | tf_op jit(solution)/shard_map/ppermute | solution.py:34
  123.5 3.3 %collective-permute-start.10 = (bf16[2,16,2048]{2,1,0:T(8,128)(2,1)S(1)}, bf16[2,16,2048]{2,1,0:T(8,128)(2,1)S(1)}, u32[]{:S(2)}, u32[]{:S(2)}) collective-permute-start(bf16[2,16,2048]{2,1,0:T(8,128)(2,1)S(1)} %get-tuple-element.36), channel_id=1, source_target_pairs={{0,112},{16,0},{32,16},{48,32},{64,48},{80,64},{96,80},{112,96},{1... | collective-permute-start | bytes 393224 | tf_op jit(solution)/shard_map/ppermute | solution.py:34
  129.3 3.8 %collective-permute-done.9 = bf16[2,16,2048]{2,1,0:T(8,128)(2,1)} collective-permute-done((bf16[2,16,2048]{2,1,0:T(8,128)(2,1)S(1)}, bf16[2,16,2048]{2,1,0:T(8,128)(2,1)}, u32[]{:S(2)}, u32[]{:S(2)}) %collective-permute-start.9) | collective-permute-done | bytes 131104 | tf_op jit(solution)/shard_map/ppermute | solution.py:34
  135.3 4.9 %collective-permute-done.11.got_ref = bf16[16,2048]{1,0:T(8,128)(2,1)S(1)} collective-permute-done((bf16[16,2048]{1,0:T(8,128)(2,1)S(1)}, bf16[16,2048]{1,0:T(8,128)(2,1)S(1)}, u32[]{:S(2)}, u32[]{:S(2)}) %collective-permute-start.11) | collective-permute-done | bytes 65568 | tf_op jit(solution)/shard_map/ppermute | solution.py:29
  141.7 4.6 %all-to-all-start.4 = ((f32[8,16,640]{2,1,0:T(8,128)}), f32[8,16,640]{2,1,0:T(8,128)S(1)}, u32[]{:S(2)}, u32[]{:S(2)}) async-start(f32[8,16,640]{2,1,0:T(8,128)} %get-tuple-element.23), calls=%async_computation.4 | async-start | bytes 655360 | tf_op jit(solution)/shard_map/all_to_all | solution.py:307
  147.5 5.5 %collective-permute-done.19.gate_got_ref = bf16[16,2048]{1,0:T(8,128)(2,1)S(1)} collective-permute-done((bf16[16,2048]{1,0:T(8,128)(2,1)S(1)}, bf16[16,2048]{1,0:T(8,128)(2,1)S(1)}, u32[]{:S(2)}, u32[]{:S(2)}) %collective-permute-start.19) | collective-permute-done | bytes 65568 | tf_op jit(solution)/shard_map/ppermute | solution.py:29
  164.8 3.5 %collective-permute-start.25 = (bf16[16,2048]{1,0:T(8,128)(2,1)S(1)}, bf16[16,2048]{1,0:T(8,128)(2,1)S(1)}, u32[]{:S(2)}, u32[]{:S(2)}) collective-permute-start(bf16[16,2048]{1,0:T(8,128)(2,1)S(1)} %get-tuple-element.26.refs_0_), channel_id=1, source_target_pairs={{0,32},{16,48},{32,64},{48,80},{64,96},{80,112},{96,0},{112,16},{1... | collective-permute-start | bytes 196616 | tf_op jit(solution)/shard_map/ppermute | solution.py:34
  175.4 4.6 %mix.1 = bf16[128,1024]{1,0:T(8,128)(2,1)} custom-call(s32[12]{0:T(128)} %pad_add_fusion.where_ref, bf16[16,2048]{1,0:T(8,128)(2,1)} %copy-done.5, bf16[16,2048]{1,0:T(8,128)(2,1)} %copy-done.14, bf16[16,2048]{1,0:T(8,128)(2,1)} %copy-done.15, bf16[16,2048]{1,0:T(8,128)(2,1)} %copy-done.16, bf16[16,2048]{1,0:T(8,128)(2,1)} %copy-done.17, ...), custom_call_target="tpu_custom_call" | custom-call | flops 536870912 | bytes 4456448 | tf_op jit(solution)/shard_map/mix/pallas_call | solution.py:209
  181.2 10.7 %all_to_all.36 = bf16[8,8,2,1024]{3,2,1,0:T(2,128)(2,1)S(1)} all-to-all(bf16[8,8,2,1024]{3,2,1,0:T(2,128)(2,1)S(1)} %bitcast.132), channel_id=1, replica_groups=mesh['h'=2,'z'=8,'k'=2,'x'=4,'l'=2] {'x','l'}, dimensions={0} | all-to-all | bytes 524288 | tf_op jit(solution)/shard_map/all_to_all | solution.py:320
  193.0 6.8 %all-to-all-start.6 = ((bf16[64,2,1024]{2,1,0:T(2,128)(2,1)}), bf16[64,2,1024]{2,1,0:T(2,128)(2,1)S(1)}, u32[]{:S(2)}, u32[]{:S(2)}) async-start(bf16[64,2,1024]{2,1,0:T(2,128)(2,1)} %bitcast.43), calls=%async_computation.6 | async-start | bytes 524288 | tf_op jit(solution)/shard_map/all_to_all | solution.py:324
  199.9 11.2 %all-to-all-done.6 = bf16[64,2,1024]{2,1,0:T(2,128)(2,1)S(1)} async-done(((bf16[64,2,1024]{2,1,0:T(2,128)(2,1)}), bf16[64,2,1024]{2,1,0:T(2,128)(2,1)S(1)}, u32[]{:S(2)}, u32[]{:S(2)}) %all-to-all-start.6) | async-done | bytes 262176 | tf_op jit(solution)/shard_map/all_to_all | solution.py:324
  (152 shorter events, 67.7 us)
Async XLA Ops:
  8.5 20.4 %all-to-all-start = ((s32[32,1,16]{2,1,0:T(1,128)}), s32[32,1,16]{2,1,0:T(1,128)S(1)}, u32[]{:S(2)}, u32[]{:S(2)}) async-start(s32[32,1,16]{2,1,0:T(1,128)} %broadcast_in_dim.34), calls=%async_computation | async-start | bytes 32768 | tf_op jit(solution)/shard_map/all_to_all | solution.py:25
  19.1 14.7 %collective-permute-start.2 = (bf16[16,2048]{1,0:T(8,128)(2,1)}, bf16[16,2048]{1,0:T(8,128)(2,1)S(1)}, u32[]{:S(2)}, u32[]{:S(2)}) collective-permute-start(bf16[16,2048]{1,0:T(8,128)(2,1)} %param.23), channel_id=1, source_target_pairs={{0,128},{128,0},{1,129},{129,1},{2,130},{130,2},{3,131},{131,3},{4... | collective-permute-start | bytes 196616 | tf_op jit(solution)/shard_map/ppermute | solution.py:29
  36.7 21.2 %all-to-all-start.1 = ((bf16[16,16,1024]{2,1,0:T(8,128)(2,1)}), bf16[16,16,1024]{2,1,0:T(8,128)(2,1)S(1)}, u32[]{:S(2)}, u32[]{:S(2)}) async-start(bf16[16,16,1024]{2,1,0:T(8,128)(2,1)} %fusion.11), calls=%async_computation.1 | async-start | bytes 1048576 | tf_op jit(solution)/shard_map/all_to_all | solution.py:277
  40.4 59.4 %all-gather.2.cloned.1.call-start = ((), (), s32[]{:S(2)}) async-start(), calls=%async_computation.7 | async-start | bytes 2359296 | tf_op jit(solution)/shard_map/all_gather | solution.py:263
  41.3 49.6 %collective-permute-start.1 = (bf16[256,4096]{1,0:T(8,128)(2,1)S(1)}, bf16[256,4096]{1,0:T(8,128)(2,1)}, u32[]{:S(2)}, u32[]{:S(2)}) collective-permute-start(bf16[256,4096]{1,0:T(8,128)(2,1)S(1)} %bitcast.116), channel_id=1, source_target_pairs={{0,8},{8,0},{1,9},{9,1},{2,10},{10,2},{3,11},{11,3},{4,12},{12,4},... | collective-permute-start | bytes 6291464 | tf_op jit(solution)/shard_map/ppermute | solution.py:29
  58.7 11.9 %all-to-all-start.2 = ((bf16[8,16,1024]{2,1,0:T(8,128)(2,1)}), bf16[8,16,1024]{2,1,0:T(8,128)(2,1)S(1)}, u32[]{:S(2)}, u32[]{:S(2)}) async-start(bf16[8,16,1024]{2,1,0:T(8,128)(2,1)} %broadcast_in_dim.35), calls=%async_computation.2 | async-start | bytes 524288 | tf_op jit(solution)/shard_map/all_to_all | solution.py:25
  64.4 13.7 %collective-permute-start.27 = (bf16[2048,256]{1,0:T(8,128)(2,1)}, bf16[2048,256]{1,0:T(8,128)(2,1)}, u32[]{:S(2)}, u32[]{:S(2)}) collective-permute-start(bf16[2048,256]{1,0:T(8,128)(2,1)} %param.27), channel_id=1, source_target_pairs={{0,8},{8,0},{1,9},{9,1},{2,10},{10,2},{3,11},{11,3},{4,12},{12,4},... | collective-permute-start | bytes 3145736 | tf_op jit(solution)/shard_map/ppermute | solution.py:29
  73.0 17.3 %all-to-all-start.3 = ((bf16[16,16,512]{2,1,0:T(8,128)(2,1)}), bf16[16,16,512]{2,1,0:T(8,128)(2,1)S(1)}, u32[]{:S(2)}, u32[]{:S(2)}) async-start(bf16[16,16,512]{2,1,0:T(8,128)(2,1)} %copy.45), calls=%async_computation.3 | async-start | bytes 524288 | tf_op jit(solution)/shard_map/all_to_all | solution.py:284
  81.2 82.1 %collective-permute-start.28 = (bf16[2,2048,256]{2,1,0:T(8,128)(2,1)}, bf16[2,2048,256]{2,1,0:T(8,128)(2,1)}, u32[]{:S(2)}, u32[]{:S(2)}) collective-permute-start(bf16[2,2048,256]{2,1,0:T(8,128)(2,1)} %pad_maximum_fusion.refs_8_.refs_9_), channel_id=1, source_target_pairs={{0,128},{128,0},{1,129},{129,1},{2,130},{130,2},{3,131},{131,3},{4... | collective-permute-start | bytes 6291464 | tf_op jit(solution)/shard_map/ppermute | solution.py:29
  93.3 7.6 %collective-permute-start.12 = (bf16[2,16,2048]{2,1,0:T(8,128)(2,1)}, bf16[2,16,2048]{2,1,0:T(8,128)(2,1)S(1)}, u32[]{:S(2)}, u32[]{:S(2)}) collective-permute-start(bf16[2,16,2048]{2,1,0:T(8,128)(2,1)} %get-tuple-element.33), channel_id=1, source_target_pairs={{0,16},{16,32},{32,48},{48,64},{64,80},{80,96},{96,112},{112,0},{1... | collective-permute-start | bytes 393224 | tf_op jit(solution)/shard_map/ppermute | solution.py:34
  94.6 13.6 %collective-permute-start.16 = (bf16[2,16,2048]{2,1,0:T(8,128)(2,1)}, bf16[2,16,2048]{2,1,0:T(8,128)(2,1)}, u32[]{:S(2)}, u32[]{:S(2)}) collective-permute-start(bf16[2,16,2048]{2,1,0:T(8,128)(2,1)} %get-tuple-element.34), channel_id=1, source_target_pairs={{0,112},{16,0},{32,16},{48,32},{64,48},{80,64},{96,80},{112,96},{1... | collective-permute-start | bytes 393224 | tf_op jit(solution)/shard_map/ppermute | solution.py:34
  101.0 8.4 %collective-permute-start.13 = (bf16[2,16,2048]{2,1,0:T(8,128)(2,1)S(1)}, bf16[2,16,2048]{2,1,0:T(8,128)(2,1)S(1)}, u32[]{:S(2)}, u32[]{:S(2)}) collective-permute-start(bf16[2,16,2048]{2,1,0:T(8,128)(2,1)S(1)} %fusion.20), channel_id=1, source_target_pairs={{0,16},{16,32},{32,48},{48,64},{64,80},{80,96},{96,112},{112,0},{1... | collective-permute-start | bytes 393224 | tf_op jit(solution)/shard_map/ppermute | solution.py:34
  102.5 11.3 %collective-permute-start.6 = (bf16[2,16,2048]{2,1,0:T(8,128)(2,1)S(1)}, bf16[2,16,2048]{2,1,0:T(8,128)(2,1)S(1)}, u32[]{:S(2)}, u32[]{:S(2)}) collective-permute-start(bf16[2,16,2048]{2,1,0:T(8,128)(2,1)S(1)} %get-tuple-element.39), channel_id=1, source_target_pairs={{0,112},{16,0},{32,16},{48,32},{64,48},{80,64},{96,80},{112,96},{1... | collective-permute-start | bytes 393224 | tf_op jit(solution)/shard_map/ppermute | solution.py:34
  110.5 8.2 %collective-permute-start.14 = (bf16[2,16,2048]{2,1,0:T(8,128)(2,1)S(1)}, bf16[2,16,2048]{2,1,0:T(8,128)(2,1)S(1)}, u32[]{:S(2)}, u32[]{:S(2)}) collective-permute-start(bf16[2,16,2048]{2,1,0:T(8,128)(2,1)S(1)} %get-tuple-element.31), channel_id=1, source_target_pairs={{0,16},{16,32},{32,48},{48,64},{64,80},{80,96},{96,112},{112,0},{1... | collective-permute-start | bytes 393224 | tf_op jit(solution)/shard_map/ppermute | solution.py:34
  110.6 8.1 %collective-permute-start.17 = (bf16[2,16,2048]{2,1,0:T(8,128)(2,1)S(1)}, bf16[2,16,2048]{2,1,0:T(8,128)(2,1)S(1)}, u32[]{:S(2)}, u32[]{:S(2)}) collective-permute-start(bf16[2,16,2048]{2,1,0:T(8,128)(2,1)S(1)} %get-tuple-element.32), channel_id=1, source_target_pairs={{0,112},{16,0},{32,16},{48,32},{64,48},{80,64},{96,80},{112,96},{1... | collective-permute-start | bytes 393224 | tf_op jit(solution)/shard_map/ppermute | solution.py:34
  115.3 7.1 %collective-permute-start.7 = (bf16[2,16,2048]{2,1,0:T(8,128)(2,1)S(1)}, bf16[2,16,2048]{2,1,0:T(8,128)(2,1)S(1)}, u32[]{:S(2)}, u32[]{:S(2)}) collective-permute-start(bf16[2,16,2048]{2,1,0:T(8,128)(2,1)S(1)} %get-tuple-element.38), channel_id=1, source_target_pairs={{0,16},{16,32},{32,48},{48,64},{64,80},{80,96},{96,112},{112,0},{1... | collective-permute-start | bytes 393224 | tf_op jit(solution)/shard_map/ppermute | solution.py:34
  141.7 11.4 %all-to-all-start.4 = ((f32[8,16,640]{2,1,0:T(8,128)}), f32[8,16,640]{2,1,0:T(8,128)S(1)}, u32[]{:S(2)}, u32[]{:S(2)}) async-start(f32[8,16,640]{2,1,0:T(8,128)} %get-tuple-element.23), calls=%async_computation.4 | async-start | bytes 655360 | tf_op jit(solution)/shard_map/all_to_all | solution.py:307
  156.7 8.1 %collective-permute-start.20 = (bf16[16,2048]{1,0:T(8,128)(2,1)S(1)}, bf16[16,2048]{1,0:T(8,128)(2,1)S(1)}, u32[]{:S(2)}, u32[]{:S(2)}) collective-permute-start(bf16[16,2048]{1,0:T(8,128)(2,1)S(1)} %get-tuple-element.26.refs_0_), channel_id=1, source_target_pairs={{0,112},{16,0},{32,16},{48,32},{64,48},{80,64},{96,80},{112,96},{1... | collective-permute-start | bytes 196616 | tf_op jit(solution)/shard_map/ppermute | solution.py:34
  156.7 11.5 %collective-permute-start.21 = (bf16[16,2048]{1,0:T(8,128)(2,1)S(1)}, bf16[16,2048]{1,0:T(8,128)(2,1)S(1)}, u32[]{:S(2)}, u32[]{:S(2)}) collective-permute-start(bf16[16,2048]{1,0:T(8,128)(2,1)S(1)} %get-tuple-element.26.refs_0_), channel_id=1, source_target_pairs={{0,96},{16,112},{32,0},{48,16},{64,32},{80,48},{96,64},{112,80},{1... | collective-permute-start | bytes 196616 | tf_op jit(solution)/shard_map/ppermute | solution.py:34
  158.1 12.8 %collective-permute-start.22 = (bf16[16,2048]{1,0:T(8,128)(2,1)S(1)}, bf16[16,2048]{1,0:T(8,128)(2,1)S(1)}, u32[]{:S(2)}, u32[]{:S(2)}) collective-permute-start(bf16[16,2048]{1,0:T(8,128)(2,1)S(1)} %get-tuple-element.26.refs_0_), channel_id=1, source_target_pairs={{0,80},{16,96},{32,112},{48,0},{64,16},{80,32},{96,48},{112,64},{1... | collective-permute-start | bytes 196616 | tf_op jit(solution)/shard_map/ppermute | solution.py:34
  160.9 10.0 %collective-permute-start.23 = (bf16[16,2048]{1,0:T(8,128)(2,1)S(1)}, bf16[16,2048]{1,0:T(8,128)(2,1)S(1)}, u32[]{:S(2)}, u32[]{:S(2)}) collective-permute-start(bf16[16,2048]{1,0:T(8,128)(2,1)S(1)} %get-tuple-element.26.refs_0_), channel_id=1, source_target_pairs={{0,64},{16,80},{32,96},{48,112},{64,0},{80,16},{96,32},{112,48},{1... | collective-permute-start | bytes 196616 | tf_op jit(solution)/shard_map/ppermute | solution.py:34
  163.3 7.6 %collective-permute-start.24 = (bf16[16,2048]{1,0:T(8,128)(2,1)S(1)}, bf16[16,2048]{1,0:T(8,128)(2,1)S(1)}, u32[]{:S(2)}, u32[]{:S(2)}) collective-permute-start(bf16[16,2048]{1,0:T(8,128)(2,1)S(1)} %get-tuple-element.26.refs_0_), channel_id=1, source_target_pairs={{0,48},{16,64},{32,80},{48,96},{64,112},{80,0},{96,16},{112,32},{1... | collective-permute-start | bytes 196616 | tf_op jit(solution)/shard_map/ppermute | solution.py:34
  164.8 7.9 %collective-permute-start.25 = (bf16[16,2048]{1,0:T(8,128)(2,1)S(1)}, bf16[16,2048]{1,0:T(8,128)(2,1)S(1)}, u32[]{:S(2)}, u32[]{:S(2)}) collective-permute-start(bf16[16,2048]{1,0:T(8,128)(2,1)S(1)} %get-tuple-element.26.refs_0_), channel_id=1, source_target_pairs={{0,32},{16,48},{32,64},{48,80},{64,96},{80,112},{96,0},{112,16},{1... | collective-permute-start | bytes 196616 | tf_op jit(solution)/shard_map/ppermute | solution.py:34
  193.0 18.1 %all-to-all-start.6 = ((bf16[64,2,1024]{2,1,0:T(2,128)(2,1)}), bf16[64,2,1024]{2,1,0:T(2,128)(2,1)S(1)}, u32[]{:S(2)}, u32[]{:S(2)}) async-start(bf16[64,2,1024]{2,1,0:T(2,128)(2,1)} %bitcast.43), calls=%async_computation.6 | async-start | bytes 524288 | tf_op jit(solution)/shard_map/all_to_all | solution.py:324
  (35 other events, 412.5 us)
Sparse Core Ops, SparseCore 0:
  43.0 46.6 all-gather.1

commit v5 on v4

--- a/solution.py
+++ b/solution.py
@@ -106,7 +106,7 @@
             jax.ShapeDtypeStruct(past.shape, F32),
             jax.ShapeDtypeStruct((copies, rows, width), F32),
         ),
-        compiler_params=pltpu.CompilerParams(vmem_limit_bytes=24 * 1024 * 1024),
+        compiler_params=pltpu.CompilerParams(vmem_limit_bytes=12 * 1024 * 1024),
         cost_estimate=pl.CostEstimate(
             flops=2 * rows * channels * width,
             bytes_accessed=2 * channels * width,
@@ -166,7 +166,7 @@
             jax.ShapeDtypeStruct(state.shape, F32),
         ),
         scratch_shapes=[pltpu.VMEM((gain.shape[0], channels), BF16)],
-        compiler_params=pltpu.CompilerParams(vmem_limit_bytes=32 * 1024 * 1024),
+        compiler_params=pltpu.CompilerParams(vmem_limit_bytes=14 * 1024 * 1024),
         cost_estimate=pl.CostEstimate(
             flops=2 * rows * gain.shape[0] * channels + 8 * state.size,
             bytes_accessed=2 * gain.shape[0] * channels + 8 * state.size,
@@ -177,55 +177,35 @@
 
 
 def mix_kernel(where_ref, *refs):
-    x_refs, w_refs, out_ref, total_ref = refs[:8], refs[8:12], refs[12], refs[13]
+    x_refs, near_ref, far_ref, out_ref = refs[:8], refs[8], refs[9], refs[10]
     rows = x_refs[0].shape[0]
-    width = w_refs[0].shape[2]
-    step = pl.program_id(0)
-
-    @pl.when(step == 0)
-    def _():
-        total_ref[...] = jnp.zeros_like(total_ref)
-
+    width = near_ref.shape[2]
     x = jnp.concatenate([x_ref[...] for x_ref in x_refs], axis=0)
-    for i, w_ref in enumerate(w_refs):
-        cols = slice(i * width, (i + 1) * width)
-        total_ref[:, cols] += jnp.dot(x, w_ref[0], preferred_element_type=F32)
-
-    @pl.when(step == pl.num_programs(0) - 1)
-    def _():
+    for i in range(4):
+        w = near_ref[i] if i < 2 else far_ref[i - 2]
+        total = jnp.dot(x, w, preferred_element_type=F32).astype(BF16)
+        lane = pl.multiple_of(where_ref[i] * width, width)
         for j in range(8):
             row = pl.multiple_of(where_ref[4 + j] * rows, rows)
-            for i in range(4):
-                lane = pl.multiple_of(where_ref[i] * width, width)
-                tile = total_ref[j * rows : (j + 1) * rows, i * width : (i + 1) * width]
-                out_ref[pl.ds(row, rows), pl.ds(lane, width)] = tile.astype(BF16)
+            out_ref[pl.ds(row, rows), pl.ds(lane, width)] = total[j * rows : (j + 1) * rows]
 
 
 def mix(where, xs, near, far):
     rows, depth = xs[0].shape
     width = near.shape[2]
-    tiles = 4
-    tall = depth // tiles
     return pl.pallas_call(
         mix_kernel,
-        grid=(tiles,),
         out_shape=jax.ShapeDtypeStruct((8 * rows, 4 * width), BF16),
         in_specs=[pl.BlockSpec(memory_space=pltpu.SMEM)]
-        + [pl.BlockSpec((rows, tall), lambda i: (0, i))] * 8
-        + [
-            pl.BlockSpec((1, tall, width), lambda i: (0, i, 0)),
-            pl.BlockSpec((1, tall, width), lambda i: (1, i, 0)),
-        ]
-        * 2,
-        out_specs=pl.BlockSpec((8 * rows, 4 * width), lambda i: (0, 0)),
-        scratch_shapes=[pltpu.VMEM((8 * rows, 4 * width), F32)],
+        + [pl.BlockSpec(memory_space=pltpu.VMEM)] * 10,
+        compiler_params=pltpu.CompilerParams(vmem_limit_bytes=12 * 1024 * 1024),
         cost_estimate=pl.CostEstimate(
             flops=64 * rows * depth * width,
             bytes_accessed=8 * depth * width + 64 * rows * width,
             transcendentals=0,
         ),
         name="mix",
-    )(where, *xs, near, near, far, far)
+    )(where, *xs, near, far)
 
 
 def local(

time: 220 us -> 220 us (level)
  other arithmetic: 13.4 us -> 8.3 us
  matrix products: 8.84 us -> 11.3 us
  Pallas kernels: 8.04 us -> 5.8 us
    convert_element_type x7, other arithmetic: 6.17 us -> 3.13 us  [add(): return (a.astype(F32) + b.astype(F32)).astype(BF16)]
    dot_general x2, matrix products: 0.87 us -> 3.32 us  [project(): part = jnp.dot(x_mine, in_flat[:, cols], preferred_element_type=F32)]
    ppermute x21, waiting for transfers between devices: 14.5 us -> 16.8 us  [shift(): lax.ppermute(block, axis, [(i, (i + distance) % n) for i in range(n)])]
    unnamed x48 -> x34, local copies, waits for them, and re-layouts: 4.95 us -> 7.28 us
    pallas_call x1, Pallas kernels: 4.56 us -> 2.32 us  [mix(): pl.pallas_call(mix_kernel, out_shape=jax.ShapeDtypeStruct((8 * rows, 4 *...]
  transfers between devices with their start and end apart: 36 -> 36, of which waited for: 16 -> 18; matrix products, arithmetic and copies ran while one was open for 13% -> 13% of each run, Pallas kernels for 2% -> 2%
where the time goes in v5:
time: 220 us; the launch traced here: 219 us
  starting transfers between devices  80.4 us (37%)
  waiting for transfers between devices  71.6 us (33%)
  local copies, waits for them, and re-layouts  16.1 us (7%)
  between operations  14.6 us (7%)
  matrix products  11.3 us (5%)
  blocking collectives  11.1 us (5%)
  other arithmetic  8.3 us (4%)
  Pallas kernels  5.8 us (3%)
    ppermute x21, starting transfers between devices, shift(): lax.ppermute(block, axis, [(i, (i + distance) % n) for i in range(n)])  32.3 us
    ppermute x21, waiting for transfers between devices, shift(): lax.ppermute(block, axis, [(i, (i + distance) % n) for i in range(n)])  16.8 us
    all_to_all x2, starting transfers between devices, gather_copies(): return lax.all_to_all(copies, axes, 0, 0, tiled=True)  16.3 us
    all_to_all x1, waiting for transfers between devices, local(): picked = lax.all_to_all(picked, ('h', 'z'), 0, 0, tiled=True)  16.3 us
    all_to_all x1, waiting for transfers between devices, local(): home = lax.all_to_all(copies, ('z',) + CHAN, 0, 0, tiled=True)  11.2 us
    ppermute x8, waiting for transfers between devices, swap(): return lax.ppermute(block, axis, [(0, 1), (1, 0)])  11.2 us
    all_to_all x1, blocking collectives, local(): got = lax.all_to_all(sent, CHAN, 0, 0, tiled=True)  11.1 us
    ppermute x8, starting transfers between devices, swap(): return lax.ppermute(block, axis, [(0, 1), (1, 0)])  10.4 us
  transfers between devices with their start and end apart: 36, of which 18 were waited for; matrix products, arithmetic and copies ran while one was open for 13% of the time, Pallas kernels for 2%

profile of v5, /device:TPU:8, one launch (start us, length us, event | category | flops | bytes accessed | tf_op | source)
XLA Modules:
  0.0 219.1 jit_solution(9929854446147692520)
XLA Ops:
  8.5 10.6 %all-to-all-start = ((s32[32,1,16]{2,1,0:T(1,128)}), s32[32,1,16]{2,1,0:T(1,128)S(1)}, u32[]{:S(2)}, u32[]{:S(2)}) async-start(s32[32,1,16]{2,1,0:T(1,128)} %broadcast_in_dim.34), calls=%async_computation | async-start | bytes 32768 | tf_op jit(solution)/shard_map/all_to_all | solution.py:25
  19.1 3.4 %collective-permute-start.2 = (bf16[16,2048]{1,0:T(8,128)(2,1)}, bf16[16,2048]{1,0:T(8,128)(2,1)S(1)}, u32[]{:S(2)}, u32[]{:S(2)}) collective-permute-start(bf16[16,2048]{1,0:T(8,128)(2,1)} %param.23), channel_id=1, source_target_pairs={{0,128},{128,0},{1,129},{129,1},{2,130},{130,2},{3,131},{131,3},{4... | collective-permute-start | bytes 196616 | tf_op jit(solution)/shard_map/ppermute | solution.py:29
  22.5 3.9 %copy.62 = bf16[32,8,2,2048]{3,1,2,0:T(8,128)(2,1)} copy(bf16[32,8,2,2048]{3,2,1,0:T(2,128)(2,1)} %bitcast.131) | data formatting | bytes 4194304
  26.4 2.6 %all-to-all-done = s32[32,1,16]{2,1,0:T(1,128)S(1)} async-done(((s32[32,1,16]{2,1,0:T(1,128)}), s32[32,1,16]{2,1,0:T(1,128)S(1)}, u32[]{:S(2)}, u32[]{:S(2)}) %all-to-all-start) | async-done | bytes 2080 | tf_op jit(solution)/shard_map/all_to_all | solution.py:25
  29.1 4.6 %fusion.6 = bf16[512,1024]{1,0:T(8,128)(2,1)S(1)} fusion(bf16[2048,1024]{1,0:T(8,128)(2,1)} %param.16, s32[2048]{0:T(1024)S(1)} %iota_add_fusion, s32[512]{0:T(512)S(1)} %reshape.133), kind=kOutput, calls=%fused_computation.9 | convolution fusion | flops 2149056512 | bytes 5253120 | tf_op jit(solution)/shard_map/dot_general | solution.py:254
  36.7 4.3 %all-to-all-start.1 = ((bf16[16,16,1024]{2,1,0:T(8,128)(2,1)}), bf16[16,16,1024]{2,1,0:T(8,128)(2,1)S(1)}, u32[]{:S(2)}, u32[]{:S(2)}) async-start(bf16[16,16,1024]{2,1,0:T(8,128)(2,1)} %fusion.11), calls=%async_computation.1 | async-start | bytes 1048576 | tf_op jit(solution)/shard_map/all_to_all | solution.py:257
  42.0 16.3 %all-to-all-done.1 = bf16[16,16,1024]{2,1,0:T(8,128)(2,1)S(1)} async-done(((bf16[16,16,1024]{2,1,0:T(8,128)(2,1)}), bf16[16,16,1024]{2,1,0:T(8,128)(2,1)S(1)}, u32[]{:S(2)}, u32[]{:S(2)}) %all-to-all-start.1) | async-done | bytes 524320 | tf_op jit(solution)/shard_map/all_to_all | solution.py:257
  59.1 5.8 %all-to-all-start.2 = ((bf16[8,16,1024]{2,1,0:T(8,128)(2,1)}), bf16[8,16,1024]{2,1,0:T(8,128)(2,1)S(1)}, u32[]{:S(2)}, u32[]{:S(2)}) async-start(bf16[8,16,1024]{2,1,0:T(8,128)(2,1)} %broadcast_in_dim.35), calls=%async_computation.2 | async-start | bytes 524288 | tf_op jit(solution)/shard_map/all_to_all | solution.py:25
  64.9 6.1 %all-to-all-done.2 = bf16[8,16,1024]{2,1,0:T(8,128)(2,1)S(1)} async-done(((bf16[8,16,1024]{2,1,0:T(8,128)(2,1)}), bf16[8,16,1024]{2,1,0:T(8,128)(2,1)S(1)}, u32[]{:S(2)}, u32[]{:S(2)}) %all-to-all-start.2) | async-done | bytes 262176 | tf_op jit(solution)/shard_map/all_to_all | solution.py:25
  73.5 4.8 %all-to-all-start.3 = ((bf16[16,16,512]{2,1,0:T(8,128)(2,1)}), bf16[16,16,512]{2,1,0:T(8,128)(2,1)S(1)}, u32[]{:S(2)}, u32[]{:S(2)}) async-start(bf16[16,16,512]{2,1,0:T(8,128)(2,1)} %copy.45), calls=%async_computation.3 | async-start | bytes 524288 | tf_op jit(solution)/shard_map/all_to_all | solution.py:264
  79.9 3.4 %collective-permute-start.28 = (bf16[2,2048,256]{2,1,0:T(8,128)(2,1)S(1)}, bf16[2,2048,256]{2,1,0:T(8,128)(2,1)}, u32[]{:S(2)}, u32[]{:S(2)}) collective-permute-start(bf16[2,2048,256]{2,1,0:T(8,128)(2,1)S(1)} %pad_maximum_fusion.refs_8_), channel_id=1, source_target_pairs={{0,128},{128,0},{1,129},{129,1},{2,130},{130,2},{3,131},{131,3},{4... | collective-permute-start | bytes 6291464 | tf_op jit(solution)/shard_map/ppermute | solution.py:29
  83.3 7.4 %all-to-all-done.3 = bf16[16,16,512]{2,1,0:T(8,128)(2,1)S(1)} async-done(((bf16[16,16,512]{2,1,0:T(8,128)(2,1)}), bf16[16,16,512]{2,1,0:T(8,128)(2,1)S(1)}, u32[]{:S(2)}, u32[]{:S(2)}) %all-to-all-start.3) | async-done | bytes 262176 | tf_op jit(solution)/shard_map/all_to_all | solution.py:264
  113.4 2.7 %collective-permute-start.17 = (bf16[2,16,2048]{2,1,0:T(8,128)(2,1)S(1)}, bf16[2,16,2048]{2,1,0:T(8,128)(2,1)S(1)}, u32[]{:S(2)}, u32[]{:S(2)}) collective-permute-start(bf16[2,16,2048]{2,1,0:T(8,128)(2,1)S(1)} %get-tuple-element.32), channel_id=1, source_target_pairs={{0,112},{16,0},{32,16},{48,32},{64,48},{80,64},{96,80},{112,96},{1... | collective-permute-start | bytes 393224 | tf_op jit(solution)/shard_map/ppermute | solution.py:34
  117.7 3.2 %collective-permute-start.8 = (bf16[2,16,2048]{2,1,0:T(8,128)(2,1)S(1)}, bf16[2,16,2048]{2,1,0:T(8,128)(2,1)S(1)}, u32[]{:S(2)}, u32[]{:S(2)}) collective-permute-start(bf16[2,16,2048]{2,1,0:T(8,128)(2,1)S(1)} %get-tuple-element.37), channel_id=1, source_target_pairs={{0,112},{16,0},{32,16},{48,32},{64,48},{80,64},{96,80},{112,96},{1... | collective-permute-start | bytes 393224 | tf_op jit(solution)/shard_map/ppermute | solution.py:34
  121.0 2.9 %collective-permute-start.18 = (bf16[2,16,2048]{2,1,0:T(8,128)(2,1)S(1)}, bf16[2,16,2048]{2,1,0:T(8,128)(2,1)S(1)}, u32[]{:S(2)}, u32[]{:S(2)}) collective-permute-start(bf16[2,16,2048]{2,1,0:T(8,128)(2,1)S(1)} %get-tuple-element.30), channel_id=1, source_target_pairs={{0,112},{16,0},{32,16},{48,32},{64,48},{80,64},{96,80},{112,96},{1... | collective-permute-start | bytes 393224 | tf_op jit(solution)/shard_map/ppermute | solution.py:34
  124.4 3.8 %collective-permute-start.10 = (bf16[2,16,2048]{2,1,0:T(8,128)(2,1)S(1)}, bf16[2,16,2048]{2,1,0:T(8,128)(2,1)}, u32[]{:S(2)}, u32[]{:S(2)}) collective-permute-start(bf16[2,16,2048]{2,1,0:T(8,128)(2,1)S(1)} %get-tuple-element.36), channel_id=1, source_target_pairs={{0,112},{16,0},{32,16},{48,32},{64,48},{80,64},{96,80},{112,96},{1... | collective-permute-start | bytes 393224 | tf_op jit(solution)/shard_map/ppermute | solution.py:34
  130.7 3.8 %collective-permute-done.9 = bf16[2,16,2048]{2,1,0:T(8,128)(2,1)} collective-permute-done((bf16[2,16,2048]{2,1,0:T(8,128)(2,1)S(1)}, bf16[2,16,2048]{2,1,0:T(8,128)(2,1)}, u32[]{:S(2)}, u32[]{:S(2)}) %collective-permute-start.9) | collective-permute-done | bytes 131104 | tf_op jit(solution)/shard_map/ppermute | solution.py:34
  137.3 4.4 %collective-permute-done.11.got_ref = bf16[16,2048]{1,0:T(8,128)(2,1)S(1)} collective-permute-done((bf16[16,2048]{1,0:T(8,128)(2,1)S(1)}, bf16[16,2048]{1,0:T(8,128)(2,1)S(1)}, u32[]{:S(2)}, u32[]{:S(2)}) %collective-permute-start.11) | collective-permute-done | bytes 65568 | tf_op jit(solution)/shard_map/ppermute | solution.py:29
  144.7 5.5 %all-to-all-start.4 = ((f32[8,16,640]{2,1,0:T(8,128)}), f32[8,16,640]{2,1,0:T(8,128)S(1)}, u32[]{:S(2)}, u32[]{:S(2)}) async-start(f32[8,16,640]{2,1,0:T(8,128)} %get-tuple-element.23), calls=%async_computation.4 | async-start | bytes 655360 | tf_op jit(solution)/shard_map/all_to_all | solution.py:287
  151.6 5.5 %collective-permute-done.19.gate_got_ref = bf16[16,2048]{1,0:T(8,128)(2,1)S(1)} collective-permute-done((bf16[16,2048]{1,0:T(8,128)(2,1)S(1)}, bf16[16,2048]{1,0:T(8,128)(2,1)S(1)}, u32[]{:S(2)}, u32[]{:S(2)}) %collective-permute-start.19) | collective-permute-done | bytes 65568 | tf_op jit(solution)/shard_map/ppermute | solution.py:29
  163.4 4.0 %collective-permute-start.23 = (bf16[16,2048]{1,0:T(8,128)(2,1)S(1)}, bf16[16,2048]{1,0:T(8,128)(2,1)S(1)}, u32[]{:S(2)}, u32[]{:S(2)}) collective-permute-start(bf16[16,2048]{1,0:T(8,128)(2,1)S(1)} %get-tuple-element.26.refs_0_), channel_id=1, source_target_pairs={{0,64},{16,80},{32,96},{48,112},{64,0},{80,16},{96,32},{112,48},{1... | collective-permute-start | bytes 196616 | tf_op jit(solution)/shard_map/ppermute | solution.py:34
  180.8 11.1 %all_to_all.36 = bf16[8,8,2,1024]{3,2,1,0:T(2,128)(2,1)S(1)} all-to-all(bf16[8,8,2,1024]{3,2,1,0:T(2,128)(2,1)S(1)} %bitcast.134), channel_id=1, replica_groups=mesh['h'=2,'z'=8,'k'=2,'x'=4,'l'=2] {'x','l'}, dimensions={0} | all-to-all | bytes 524288 | tf_op jit(solution)/shard_map/all_to_all | solution.py:300
  193.0 6.7 %all-to-all-start.6 = ((bf16[64,2,1024]{2,1,0:T(2,128)(2,1)}), bf16[64,2,1024]{2,1,0:T(2,128)(2,1)S(1)}, u32[]{:S(2)}, u32[]{:S(2)}) async-start(bf16[64,2,1024]{2,1,0:T(2,128)(2,1)} %bitcast.43), calls=%async_computation.6 | async-start | bytes 524288 | tf_op jit(solution)/shard_map/all_to_all | solution.py:304
  199.7 11.2 %all-to-all-done.6 = bf16[64,2,1024]{2,1,0:T(2,128)(2,1)S(1)} async-done(((bf16[64,2,1024]{2,1,0:T(2,128)(2,1)}), bf16[64,2,1024]{2,1,0:T(2,128)(2,1)S(1)}, u32[]{:S(2)}, u32[]{:S(2)}) %all-to-all-start.6) | async-done | bytes 262176 | tf_op jit(solution)/shard_map/all_to_all | solution.py:304
  (138 shorter events, 66.7 us)
Async XLA Ops:
  8.5 20.4 %all-to-all-start = ((s32[32,1,16]{2,1,0:T(1,128)}), s32[32,1,16]{2,1,0:T(1,128)S(1)}, u32[]{:S(2)}, u32[]{:S(2)}) async-start(s32[32,1,16]{2,1,0:T(1,128)} %broadcast_in_dim.34), calls=%async_computation | async-start | bytes 32768 | tf_op jit(solution)/shard_map/all_to_all | solution.py:25
  19.1 14.7 %collective-permute-start.2 = (bf16[16,2048]{1,0:T(8,128)(2,1)}, bf16[16,2048]{1,0:T(8,128)(2,1)S(1)}, u32[]{:S(2)}, u32[]{:S(2)}) collective-permute-start(bf16[16,2048]{1,0:T(8,128)(2,1)} %param.23), channel_id=1, source_target_pairs={{0,128},{128,0},{1,129},{129,1},{2,130},{130,2},{3,131},{131,3},{4... | collective-permute-start | bytes 196616 | tf_op jit(solution)/shard_map/ppermute | solution.py:29
  36.7 21.6 %all-to-all-start.1 = ((bf16[16,16,1024]{2,1,0:T(8,128)(2,1)}), bf16[16,16,1024]{2,1,0:T(8,128)(2,1)S(1)}, u32[]{:S(2)}, u32[]{:S(2)}) async-start(bf16[16,16,1024]{2,1,0:T(8,128)(2,1)} %fusion.11), calls=%async_computation.1 | async-start | bytes 1048576 | tf_op jit(solution)/shard_map/all_to_all | solution.py:257
  41.1 61.5 %all-gather.2.cloned.1.call-start = ((), (), s32[]{:S(2)}) async-start(), calls=%async_computation.7 | async-start | bytes 2359296 | tf_op jit(solution)/shard_map/all_gather | solution.py:243
  41.9 50.4 %collective-permute-start.1 = (bf16[256,4096]{1,0:T(8,128)(2,1)}, bf16[256,4096]{1,0:T(8,128)(2,1)}, u32[]{:S(2)}, u32[]{:S(2)}) collective-permute-start(bf16[256,4096]{1,0:T(8,128)(2,1)} %bitcast.75), channel_id=1, source_target_pairs={{0,8},{8,0},{1,9},{9,1},{2,10},{10,2},{3,11},{11,3},{4,12},{12,4},... | collective-permute-start | bytes 6291464 | tf_op jit(solution)/shard_map/ppermute | solution.py:29
  59.1 11.9 %all-to-all-start.2 = ((bf16[8,16,1024]{2,1,0:T(8,128)(2,1)}), bf16[8,16,1024]{2,1,0:T(8,128)(2,1)S(1)}, u32[]{:S(2)}, u32[]{:S(2)}) async-start(bf16[8,16,1024]{2,1,0:T(8,128)(2,1)} %broadcast_in_dim.35), calls=%async_computation.2 | async-start | bytes 524288 | tf_op jit(solution)/shard_map/all_to_all | solution.py:25
  64.9 13.6 %collective-permute-start.27 = (bf16[2048,256]{1,0:T(8,128)(2,1)S(1)}, bf16[2048,256]{1,0:T(8,128)(2,1)}, u32[]{:S(2)}, u32[]{:S(2)}) collective-permute-start(bf16[2048,256]{1,0:T(8,128)(2,1)S(1)} %copy-done.13), channel_id=1, source_target_pairs={{0,8},{8,0},{1,9},{9,1},{2,10},{10,2},{3,11},{11,3},{4,12},{12,4},... | collective-permute-start | bytes 3145736 | tf_op jit(solution)/shard_map/ppermute | solution.py:29
  73.5 17.2 %all-to-all-start.3 = ((bf16[16,16,512]{2,1,0:T(8,128)(2,1)}), bf16[16,16,512]{2,1,0:T(8,128)(2,1)S(1)}, u32[]{:S(2)}, u32[]{:S(2)}) async-start(bf16[16,16,512]{2,1,0:T(8,128)(2,1)} %copy.45), calls=%async_computation.3 | async-start | bytes 524288 | tf_op jit(solution)/shard_map/all_to_all | solution.py:264
  79.9 87.5 %collective-permute-start.28 = (bf16[2,2048,256]{2,1,0:T(8,128)(2,1)S(1)}, bf16[2,2048,256]{2,1,0:T(8,128)(2,1)}, u32[]{:S(2)}, u32[]{:S(2)}) collective-permute-start(bf16[2,2048,256]{2,1,0:T(8,128)(2,1)S(1)} %pad_maximum_fusion.refs_8_), channel_id=1, source_target_pairs={{0,128},{128,0},{1,129},{129,1},{2,130},{130,2},{3,131},{131,3},{4... | collective-permute-start | bytes 6291464 | tf_op jit(solution)/shard_map/ppermute | solution.py:29
  94.8 9.2 %collective-permute-start.12 = (bf16[2,16,2048]{2,1,0:T(8,128)(2,1)}, bf16[2,16,2048]{2,1,0:T(8,128)(2,1)S(1)}, u32[]{:S(2)}, u32[]{:S(2)}) collective-permute-start(bf16[2,16,2048]{2,1,0:T(8,128)(2,1)} %get-tuple-element.33), channel_id=1, source_target_pairs={{0,16},{16,32},{32,48},{48,64},{64,80},{80,96},{96,112},{112,0},{1... | collective-permute-start | bytes 393224 | tf_op jit(solution)/shard_map/ppermute | solution.py:34
  96.3 14.6 %collective-permute-start.16 = (bf16[2,16,2048]{2,1,0:T(8,128)(2,1)}, bf16[2,16,2048]{2,1,0:T(8,128)(2,1)}, u32[]{:S(2)}, u32[]{:S(2)}) collective-permute-start(bf16[2,16,2048]{2,1,0:T(8,128)(2,1)} %get-tuple-element.34), channel_id=1, source_target_pairs={{0,112},{16,0},{32,16},{48,32},{64,48},{80,64},{96,80},{112,96},{1... | collective-permute-start | bytes 393224 | tf_op jit(solution)/shard_map/ppermute | solution.py:34
  104.0 7.8 %collective-permute-start.13 = (bf16[2,16,2048]{2,1,0:T(8,128)(2,1)S(1)}, bf16[2,16,2048]{2,1,0:T(8,128)(2,1)S(1)}, u32[]{:S(2)}, u32[]{:S(2)}) collective-permute-start(bf16[2,16,2048]{2,1,0:T(8,128)(2,1)S(1)} %fusion.20), channel_id=1, source_target_pairs={{0,16},{16,32},{32,48},{48,64},{64,80},{80,96},{96,112},{112,0},{1... | collective-permute-start | bytes 393224 | tf_op jit(solution)/shard_map/ppermute | solution.py:34
  105.5 10.6 %collective-permute-start.6 = (bf16[2,16,2048]{2,1,0:T(8,128)(2,1)S(1)}, bf16[2,16,2048]{2,1,0:T(8,128)(2,1)S(1)}, u32[]{:S(2)}, u32[]{:S(2)}) collective-permute-start(bf16[2,16,2048]{2,1,0:T(8,128)(2,1)S(1)} %get-tuple-element.39), channel_id=1, source_target_pairs={{0,112},{16,0},{32,16},{48,32},{64,48},{80,64},{96,80},{112,96},{1... | collective-permute-start | bytes 393224 | tf_op jit(solution)/shard_map/ppermute | solution.py:34
  112.8 8.1 %collective-permute-start.14 = (bf16[2,16,2048]{2,1,0:T(8,128)(2,1)S(1)}, bf16[2,16,2048]{2,1,0:T(8,128)(2,1)S(1)}, u32[]{:S(2)}, u32[]{:S(2)}) collective-permute-start(bf16[2,16,2048]{2,1,0:T(8,128)(2,1)S(1)} %get-tuple-element.31), channel_id=1, source_target_pairs={{0,16},{16,32},{32,48},{48,64},{64,80},{80,96},{96,112},{112,0},{1... | collective-permute-start | bytes 393224 | tf_op jit(solution)/shard_map/ppermute | solution.py:34
  113.4 7.5 %collective-permute-start.17 = (bf16[2,16,2048]{2,1,0:T(8,128)(2,1)S(1)}, bf16[2,16,2048]{2,1,0:T(8,128)(2,1)S(1)}, u32[]{:S(2)}, u32[]{:S(2)}) collective-permute-start(bf16[2,16,2048]{2,1,0:T(8,128)(2,1)S(1)} %get-tuple-element.32), channel_id=1, source_target_pairs={{0,112},{16,0},{32,16},{48,32},{64,48},{80,64},{96,80},{112,96},{1... | collective-permute-start | bytes 393224 | tf_op jit(solution)/shard_map/ppermute | solution.py:34
  144.7 12.4 %all-to-all-start.4 = ((f32[8,16,640]{2,1,0:T(8,128)}), f32[8,16,640]{2,1,0:T(8,128)S(1)}, u32[]{:S(2)}, u32[]{:S(2)}) async-start(f32[8,16,640]{2,1,0:T(8,128)} %get-tuple-element.23), calls=%async_computation.4 | async-start | bytes 655360 | tf_op jit(solution)/shard_map/all_to_all | solution.py:287
  160.8 7.7 %collective-permute-start.20 = (bf16[16,2048]{1,0:T(8,128)(2,1)S(1)}, bf16[16,2048]{1,0:T(8,128)(2,1)S(1)}, u32[]{:S(2)}, u32[]{:S(2)}) collective-permute-start(bf16[16,2048]{1,0:T(8,128)(2,1)S(1)} %get-tuple-element.26.refs_0_), channel_id=1, source_target_pairs={{0,112},{16,0},{32,16},{48,32},{64,48},{80,64},{96,80},{112,96},{1... | collective-permute-start | bytes 196616 | tf_op jit(solution)/shard_map/ppermute | solution.py:34
  160.8 10.0 %collective-permute-start.21 = (bf16[16,2048]{1,0:T(8,128)(2,1)S(1)}, bf16[16,2048]{1,0:T(8,128)(2,1)S(1)}, u32[]{:S(2)}, u32[]{:S(2)}) collective-permute-start(bf16[16,2048]{1,0:T(8,128)(2,1)S(1)} %get-tuple-element.26.refs_0_), channel_id=1, source_target_pairs={{0,96},{16,112},{32,0},{48,16},{64,32},{80,48},{96,64},{112,80},{1... | collective-permute-start | bytes 196616 | tf_op jit(solution)/shard_map/ppermute | solution.py:34
  160.8 12.1 %collective-permute-start.22 = (bf16[16,2048]{1,0:T(8,128)(2,1)S(1)}, bf16[16,2048]{1,0:T(8,128)(2,1)S(1)}, u32[]{:S(2)}, u32[]{:S(2)}) collective-permute-start(bf16[16,2048]{1,0:T(8,128)(2,1)S(1)} %get-tuple-element.26.refs_0_), channel_id=1, source_target_pairs={{0,80},{16,96},{32,112},{48,0},{64,16},{80,32},{96,48},{112,64},{1... | collective-permute-start | bytes 196616 | tf_op jit(solution)/shard_map/ppermute | solution.py:34
  163.4 9.5 %collective-permute-start.23 = (bf16[16,2048]{1,0:T(8,128)(2,1)S(1)}, bf16[16,2048]{1,0:T(8,128)(2,1)S(1)}, u32[]{:S(2)}, u32[]{:S(2)}) collective-permute-start(bf16[16,2048]{1,0:T(8,128)(2,1)S(1)} %get-tuple-element.26.refs_0_), channel_id=1, source_target_pairs={{0,64},{16,80},{32,96},{48,112},{64,0},{80,16},{96,32},{112,48},{1... | collective-permute-start | bytes 196616 | tf_op jit(solution)/shard_map/ppermute | solution.py:34
  167.4 7.4 %collective-permute-start.24 = (bf16[16,2048]{1,0:T(8,128)(2,1)S(1)}, bf16[16,2048]{1,0:T(8,128)(2,1)S(1)}, u32[]{:S(2)}, u32[]{:S(2)}) collective-permute-start(bf16[16,2048]{1,0:T(8,128)(2,1)S(1)} %get-tuple-element.26.refs_0_), channel_id=1, source_target_pairs={{0,48},{16,64},{32,80},{48,96},{64,112},{80,0},{96,16},{112,32},{1... | collective-permute-start | bytes 196616 | tf_op jit(solution)/shard_map/ppermute | solution.py:34
  168.6 7.6 %collective-permute-start.25 = (bf16[16,2048]{1,0:T(8,128)(2,1)S(1)}, bf16[16,2048]{1,0:T(8,128)(2,1)S(1)}, u32[]{:S(2)}, u32[]{:S(2)}) collective-permute-start(bf16[16,2048]{1,0:T(8,128)(2,1)S(1)} %get-tuple-element.26.refs_0_), channel_id=1, source_target_pairs={{0,32},{16,48},{32,64},{48,80},{64,96},{80,112},{96,0},{112,16},{1... | collective-permute-start | bytes 196616 | tf_op jit(solution)/shard_map/ppermute | solution.py:34
  170.8 7.4 %collective-permute-start.26 = (bf16[16,2048]{1,0:T(8,128)(2,1)S(1)}, bf16[16,2048]{1,0:T(8,128)(2,1)S(1)}, u32[]{:S(2)}, u32[]{:S(2)}) collective-permute-start(bf16[16,2048]{1,0:T(8,128)(2,1)S(1)} %get-tuple-element.26.refs_0_), channel_id=1, source_target_pairs={{0,16},{16,32},{32,48},{48,64},{64,80},{80,96},{96,112},{112,0},{1... | collective-permute-start | bytes 196616 | tf_op jit(solution)/shard_map/ppermute | solution.py:34
  193.0 18.0 %all-to-all-start.6 = ((bf16[64,2,1024]{2,1,0:T(2,128)(2,1)}), bf16[64,2,1024]{2,1,0:T(2,128)(2,1)S(1)}, u32[]{:S(2)}, u32[]{:S(2)}) async-start(bf16[64,2,1024]{2,1,0:T(2,128)(2,1)} %bitcast.43), calls=%async_computation.6 | async-start | bytes 524288 | tf_op jit(solution)/shard_map/all_to_all | solution.py:304
  (28 other events, 400.0 us)
Sparse Core Ops, SparseCore 0:
  43.7 46.9 all-gather.1
